TPU v7x, 128 devices: a whole 4x4x4 slice. The times are simulated.
128 devices in a mesh: row: 16 (over y, z), col: 8 (over x, core).
Axes of the slice: x: 4, y: 4, z: 4, core: 2. Of those that a mesh axis runs over, the one named last changes fastest.
Arguments:
- interior_residual: float32 [16, 8, 1024, 512], P('row', 'col'), may hold values from -6 to 6
- interface_residual: float32 [16, 8, 2, 512, 512], P('row', 'col'), may hold values from -6 to 6
- owner_face_weight: float32 [16, 8, 2, 512], P('row', 'col'), may hold values from 0.2 to 0.8
- interior_inverse_block: bfloat16 [16, 8, 1024, 1024], P('row', 'col'), may hold values from -0.1875 to 0.1875
- coupling: bfloat16 [16, 8, 1024, 2048], P('row', 'col'), may hold values from -0.125 to 0.125
- interface_block: bfloat16 [16, 8, 2048, 2048], P('row', 'col'), may hold values from -0.125 to 0.125
- corner_trace_basis: bfloat16 [16, 8, 4, 2048], P('row', 'col'), may hold values from -0.5 to 0.5
- coarse_inv: float32 [153, 153], replicated, may hold values from -0.5 to 0.5
- corner_map: int32 [16, 8, 4], replicated, may hold values from 0 to 152, as said below
- contact: int32 [16, 8, 4, 512], P('row', 'col'), may hold values from 0 to 4
Outputs:
- interior_output: float32 [16, 8, 1024, 512], P('row', 'col')
- z_face: float32 [16, 8, 2, 512, 512], P('row', 'col')
- currents: float32 [4, 512], replicated
Inputs may be any that keep to these rules, and one draw needn't show every extreme that they name: `corner_map`: A permutation of the 153 corner numbers of a 17 by 8 + 1 lattice; corners 0..3 of subdomain (i, j) are lattice points (i, j), (i, j+1), (i+1, j), (i+1, j+1), so neighbours agree on shared corners.
All inputs are finite; a program needn't handle non-finite values.
Results may differ from a plain program's by a relative error of at most 0.0042.
Values may be sent and summed in bfloat16 or wider, within the bound.
No kernel may reach another device: no remote copies, remote signals or barrier semaphores. Data moves between devices by JAX's collectives and lax.ppermute only.
A program may use at most 128 MiB of HBM per device.

v0:
```python
import jax
import jax.numpy as jnp
from jax import lax
from jax.experimental import pallas as pl
from jax.experimental.pallas import tpu as pltpu
from jax.sharding import PartitionSpec as P

FACE = 512
RHS = 512
INTERIOR = 1024
NTERM = 4
ROWS = 16
COLS = 8
SENT = FACE + 16
HIGHEST = lax.Precision.HIGHEST
F32 = jnp.float32
BF16 = jnp.bfloat16
VMEM = pl.BlockSpec(memory_space=pltpu.VMEM)
SMEM = pl.BlockSpec(memory_space=pltpu.SMEM)
ANY = pl.BlockSpec(memory_space=pl.ANY)


def mm(a, b):
    return jnp.dot(a, b, preferred_element_type=F32)


def mm_nt(a, b):
    return lax.dot_general(a, b, (((1,), (1,)), ((), ())), preferred_element_type=F32)


def mm_tn(a, b):
    return lax.dot_general(a, b, (((0,), (0,)), ((), ())), preferred_element_type=F32)


def two_terms(a):
    high = a.astype(BF16)
    low = (a - high.astype(F32)).astype(BF16)
    return jnp.concatenate([high, low], axis=0)


def folded(a):
    half = a.shape[0] // 2
    return a[:half] + a[half:]


def column(row):
    return jnp.transpose(jnp.broadcast_to(row, (8, row.shape[1])))[:, :1]


def call(kernel, outs, in_specs, out_specs, scratch=(), after=(), through=None, vmem=16, cost=0):
    n = len(in_specs)
    several = isinstance(outs, tuple)
    outs, out_specs = (outs, out_specs) if several else ((outs,), (out_specs,))
    extra = list(after)
    aliases = {}
    if through is not None:
        aliases = {n + len(extra): len(outs)}
        extra.append(through)
        outs = (*outs, jax.ShapeDtypeStruct(through.shape, through.dtype))
        out_specs = (*out_specs, ANY)
    m = len(outs) - len(aliases)

    def body(*refs):
        rest = refs[n + len(extra) :]
        kernel(*refs[:n], *rest[:m], *rest[len(outs) :])

    run = pl.pallas_call(
        body,
        name=kernel.__name__,
        out_shape=outs,
        in_specs=list(in_specs) + [ANY] * len(extra),
        out_specs=out_specs,
        scratch_shapes=list(scratch),
        input_output_aliases=aliases,
        compiler_params=pltpu.CompilerParams(vmem_limit_bytes=vmem << 20),
        cost_estimate=pl.CostEstimate(flops=1000 + cost * 1_000_000_000, bytes_accessed=1000 + cost * 3_000_000, transcendentals=0),
    )

    def made(*args):
        result = run(*args, *extra)
        return result if several or aliases else result[0]

    return made


def shape(rows, kind, columns=RHS):
    return jax.ShapeDtypeStruct((rows, columns), kind)


def north_kernel(pos, faces, w, out):
    keep = (pos[0] < ROWS - 1).astype(F32)
    out[...] = ((1.0 - column(w[1:2, :])) * keep * faces[1]).astype(BF16)


def north_face(i, faces, w):
    return call(north_kernel, shape(FACE, BF16), [SMEM, VMEM, VMEM], VMEM, cost=4)(i, faces, w)


def east_kernel(pos, faces, w, out, own):
    keep = (pos[0] < COLS - 1).astype(F32)
    c = column(w[0:1, :])
    out[...] = ((1.0 - c) * keep * faces[0]).astype(BF16)
    own[:FACE] = (c * faces[0]).astype(BF16)
    own[FACE:] = (column(w[1:2, :]) * faces[1]).astype(BF16)


def east_face(j, faces, w, after):
    return call(east_kernel, (shape(FACE, BF16), shape(2 * FACE, BF16)), [SMEM, VMEM, VMEM], (VMEM, VMEM), after=after, cost=4)(j, faces, w)


def table_kernel(i, j, cm, cmv, cinv, out, rows, lat):
    n_i, n_j = ROWS, COLS
    corners = cinv.shape[0]
    own_j = j[0]
    east_j = jnp.minimum(own_j + 1, n_j - 1)
    rows[...] = jnp.zeros_like(rows)
    for y in range(4):
        own_i = 4 * y + lax.rem(i[0], 4)
        north_i = jnp.minimum(own_i + 1, n_i - 1)
        for g, (a, b) in enumerate(((own_i, own_j), (own_i, east_j), (north_i, own_j))):
            for c in range(4):
                n = 16 * y + 4 * g + c
                rows[n : n + 1] = cinv[pl.ds(cm[4 * b + c, a], 1), :]
    ids = cmv[...].astype(F32)
    at = lax.broadcasted_iota(jnp.int32, (4 * n_j, n_j + 1), 0)
    col = lax.broadcasted_iota(jnp.int32, (4 * n_j, n_j + 1), 1)
    first = (at == jnp.where(col == n_j, 4 * n_j - 3, 4 * col)).astype(F32)
    last = (at == jnp.where(col == n_j, 4 * n_j - 1, 4 * col + 2)).astype(F32)
    flip = lambda s: lax.dot_general(ids, s, (((0,), (0,)), ((), ())), precision=HIGHEST, preferred_element_type=F32)
    lat[0:n_i] = flip(first)
    lat[n_i : n_i + 1] = flip(last)[n_i - 1 : n_i]
    base = 4 * lax.div(i[0], 4)
    line = jnp.concatenate([lat[pl.ds(base + a, 1), :] for a in range(5)], axis=1)
    slots = lax.broadcasted_iota(jnp.int32, (corners, 5 * (n_j + 1)), 0).astype(F32)
    out[:, :45] = jnp.dot(rows[...], (slots == line).astype(F32), precision=HIGHEST, preferred_element_type=F32)
    out[:, 45:] = jnp.zeros((64, 3), F32)


def table(i, j, corner_map, coarse_inv, after):
    cm = corner_map.transpose(1, 2, 0).reshape(4 * COLS, ROWS)
    return call(
        table_kernel,
        jax.ShapeDtypeStruct((64, 48), F32),
        [SMEM, SMEM, SMEM, VMEM, VMEM],
        VMEM,
        [pltpu.VMEM((64, coarse_inv.shape[0]), F32), pltpu.VMEM((24, COLS + 1), F32)],
        after=after,
        cost=0,
    )(i, j, cm, cm, coarse_inv)


def early_a_kernel(coup, r, own, basis, contact, p, g, bt):
    labels = lax.broadcasted_iota(jnp.int32, (NTERM, FACE), 0) + 1
    marks = jnp.concatenate([(contact[f : f + 1, :] == labels).astype(F32) for f in range(4)], axis=1)
    bt[...] = jnp.concatenate([basis[...].astype(F32), marks], axis=0).astype(BF16)
    g[...] = mm_nt(bt[...], coup[...])
    for c in range(2):
        at = slice(512 * c, 512 * c + 512)
        p[at] = r[at] - mm(coup[at, : 2 * FACE], own[...])


def early_b_kernel(g, inv, coup, r, k, q):
    m = folded(mm(two_terms(g[...]), inv[...]))
    m2 = two_terms(m)
    k[...] = -folded(mm(m2, coup[...]))
    high = r[...].astype(BF16)
    low = (r[...] - high.astype(F32)).astype(BF16)
    q[...] = folded(mm(m2, high)) + mm(m2[:8], low)


def early_c_kernel(bt, block, own, k, qr, h, q, k_out):
    k2 = two_terms(k[...] + mm(bt[...], block[...]))
    q[...] = qr[...] + folded(mm(k2[:, : 2 * FACE], own[...]))
    k_out[...] = k2[:, 2 * FACE :]
    for c in range(4):
        at = slice(512 * c, 512 * c + 512)
        h[at] = mm(block[at, : 2 * FACE], own[...])


def corner_kernel(q, k, west, south, out):
    out[...] = q[...] + folded(mm(k[:, :FACE], west[...]) + mm(k[:, FACE:], south[...]))


def tail(basis, keep):
    return (jnp.concatenate([basis.astype(F32), jnp.zeros((12, FACE), F32)], axis=0) * keep).astype(BF16)


def inner_kernel(coup, p, west, south, t):
    for c in range(2):
        at = slice(c * 512, (c + 1) * 512)
        t[at] = (p[at] - (mm(coup[at, 2 * FACE : 3 * FACE], west[...]) + mm(coup[at, 3 * FACE :], south[...]))).astype(BF16)


def result(f, coup, block, h, ub, west, south):
    at = slice(f * FACE, (f + 1) * FACE)
    own_n = 2 * FACE
    return h[at] + mm(block[at, own_n : 3 * FACE], west[...]) + mm(block[at, 3 * FACE :], south[...]) + mm_tn(coup[:, at], ub[...])


def tail(basis, f, keep):
    rows = basis[:, f * FACE : (f + 1) * FACE].astype(F32)
    return (jnp.concatenate([rows, jnp.zeros((12, FACE), F32)], axis=0) * keep).astype(BF16)


def solve_kernel(pos, coup, inv, block, t, h, west, south, basis, x_h, sent, ub, xbuf, sem):
    rows = 512
    copies = []
    for c in range(2):
        at = slice(c * rows, (c + 1) * rows)
        x = mm(inv[at], t[...])
        xbuf[at] = x
        ub[at] = x.astype(BF16)
        copies.append(pltpu.make_async_copy(xbuf.at[pl.ds(c * rows, rows)], x_h.at[pl.ds(c * rows, rows)], sem.at[c]))
        copies[c].start()
    keep = (pos[0] > 0).astype(F32)
    sent[:FACE] = (result(3, coup, block, h, ub, west, south) * keep).astype(BF16)
    sent[FACE:] = tail(basis, 3, keep)
    for copy in copies:
        copy.wait()


def west_kernel(pos, coup, block, h, ub, west, south, basis, sent):
    keep = (pos[0] > 0).astype(F32)
    sent[:FACE] = (result(2, coup, block, h, ub, west, south) * keep).astype(BF16)
    sent[FACE:] = tail(basis, 2, keep)


def kept_kernel(coup, block, h, ub, west, south, kept):
    for f in range(2):
        kept[f * FACE : (f + 1) * FACE] = result(f, coup, block, h, ub, west, south)


def pair_kernel(pos, mine, theirs, out):
    first = lax.rem(pos[0], 2) == 0
    a, b = mine[...], theirs[...]
    low = jnp.where(first, a, b)
    high = jnp.where(first, b, a)
    for r in range(2):
        out[3 * r : 3 * r + 1] = low[2 * r : 2 * r + 1]
        out[3 * r + 1 : 3 * r + 2] = low[2 * r + 1 : 2 * r + 2] + high[2 * r : 2 * r + 1]
        out[3 * r + 2 : 3 * r + 3] = high[2 * r + 1 : 2 * r + 2]
    out[6:10] = low[4:8] + high[4:8]


def placed(at, blocks, slots):
    for k, block in enumerate(blocks):
        slots[at ^ k] = block[...]


def summed(slots, n):
    return (slots[0, n : n + 4] + slots[1, n : n + 4]) + (slots[2, n : n + 4] + slots[3, n : n + 4])


def rows_kernel(pos, b0, b1, b2, b3, out, slots):
    placed(lax.rem(pos[0], 4), (b0, b1, b2, b3), slots)
    out[0:3] = slots[0, 0:3]
    for b in range(1, 4):
        out[3 * b : 3 * b + 3] = slots[b - 1, 3:6] + slots[b, 0:3]
    out[12:15] = slots[3, 3:6]
    out[15:19] = summed(slots, 6)


def columns_kernel(i, j, b0, b1, b2, b3, e, o0, o1, o2, o3, slots, full, shares):
    placed(lax.div(j[0], 2), (b0, b1, b2, b3), slots)
    full[40:] = jnp.zeros((8, RHS), F32)
    for r in range(5):
        for c in range(9):
            b = min(c // 2, 3)
            n = 3 * r + c - 2 * b
            row = slots[b, n : n + 1]
            if c % 2 == 0 and 0 < c < 8:
                row = slots[b - 1, 3 * r + 2 : 3 * r + 3] + row
            full[9 * r + c : 9 * r + c + 1] = row
    e2, q2 = two_terms(e[...]), two_terms(full[...])
    all_shares = folded(mm(e2, q2[:48])) + mm(e2[:64], q2[48:])
    total = summed(slots, 15)
    for y in range(4):
        shares[y] = all_shares[16 * y : 16 * y + 16]
        shares[y, 12:16] = total
    at = lax.div(i[0], 4)
    for k, out in enumerate((o0, o1, o2, o3)):
        out[...] = shares[at ^ k]


def final_kernel(pos, b0, b1, b2, b3, kept, from_east, from_north, w, basis, z, cur, slots, zbuf, sem):
    placed(lax.div(pos[0], 4), (b0, b1, b2, b3), slots)
    cur[...] = summed(slots, 12) / FACE
    cc = (slots[0] + slots[1]) + (slots[2] + slots[3])
    copies = []
    for f, got in enumerate((from_east, from_north)):
        wr = w[f : f + 1, :]
        mine = basis[:, f * FACE : (f + 1) * FACE].astype(F32) * wr
        other = got[FACE:].astype(F32)[:4] * (1.0 - wr)
        x = jnp.concatenate([mine, other], axis=0)
        c = jnp.concatenate([cc[0:4], cc[4 + 4 * f : 8 + 4 * f]], axis=0)
        xh, ch = x.astype(BF16).astype(F32), c.astype(BF16).astype(F32)
        pad = jnp.zeros((8, RHS), F32)
        left = jnp.concatenate([xh, x - xh, xh, pad], axis=0).astype(BF16)
        right = jnp.concatenate([ch, ch, c - ch, pad], axis=0).astype(BF16)
        wc = column(wr)
        for n in range(2):
            rows = slice(n * 256, (n + 1) * 256)
            part = wc[rows] * kept[f * FACE + n * 256 : f * FACE + (n + 1) * 256] + (1.0 - wc[rows]) * got[rows].astype(F32)
            zbuf[f, rows] = part + mm_tn(left[:, rows], right)
            here = pl.ds(n * 256, 256)
            copy = pltpu.make_async_copy(zbuf.at[f, here], z.at[f, here], sem.at[2 * f + n])
            copy.start()
            copies.append(copy)
    for copy in copies:
        copy.wait()


def final(at, blocks, kept, from_east, from_north, w, basis):
    return call(
        final_kernel,
        (jax.ShapeDtypeStruct((2, FACE, RHS), F32), shape(NTERM, F32)),
        [SMEM] + [VMEM] * 9,
        (ANY, VMEM),
        [
            pltpu.VMEM((4, 16, RHS), F32),
            pltpu.VMEM((2, FACE, RHS), F32),
            pltpu.SemaphoreType.DMA((4,)),
        ],
    )(at, *blocks, kept, from_east, from_north, w, basis)


def along(x, axis, d):
    n = lax.axis_size(axis)
    return lax.ppermute(x, axis, [(s, (s + d) % n) for s in range(n)])


def exchanged(x, axis, stride, k):
    return lax.ppermute(x, axis, [(d ^ (k * stride), d) for d in range(lax.axis_size(axis))])


def four(x, axis, stride):
    return [x] + [exchanged(x, axis, stride, k) for k in (1, 2, 3)]


def local(
    interior_residual,
    interface_residual,
    owner_face_weight,
    interior_inverse_block,
    coupling,
    interface_block,
    corner_trace_basis,
    coarse_inv,
    corner_map,
    contact,
):
    i = lax.axis_index("row").astype(jnp.int32).reshape(1)
    j = lax.axis_index("col").astype(jnp.int32).reshape(1)
    faces_in = interface_residual[0, 0]
    r = interior_residual[0, 0]
    w = owner_face_weight[0, 0]
    inv, coup, block = interior_inverse_block[0, 0], coupling[0, 0], interface_block[0, 0]
    basis = corner_trace_basis[0, 0]

    to_north = north_face(i, faces_in, w)
    south = lax.ppermute(to_north, "row", [(s, s + 1) for s in range(ROWS - 1)])
    to_east, own = east_face(j, faces_in, w, (to_north,))
    west = along(to_east, "col", 1)
    e = table(i, j, corner_map, coarse_inv, (own,))
    p, g, bt = call(
        early_a_kernel,
        (shape(INTERIOR, F32), shape(8, F32, INTERIOR), shape(8, BF16, 4 * FACE)),
        [VMEM] * 5,
        (VMEM,) * 3,
        after=(e,),
        cost=10,
    )(coup, r, own, basis, contact[0, 0])
    k, q = call(early_b_kernel, (shape(8, F32, 4 * FACE), shape(8, F32)), [VMEM] * 4, (VMEM,) * 2, cost=10)(g, inv, coup, r)
    h, q, k = call(
        early_c_kernel,
        (shape(4 * FACE, F32), shape(8, F32), shape(16, BF16, 2 * FACE)),
        [VMEM] * 5,
        (VMEM,) * 3,
        cost=10,
    )(bt, block, own, k, q)

    sums = call(corner_kernel, shape(8, F32), [VMEM] * 4, VMEM)(q, k, west, south)
    other = lax.ppermute(sums, "col", [(s, s ^ 1) for s in range(COLS)])
    t = call(inner_kernel, shape(INTERIOR, BF16), [VMEM] * 4, VMEM, after=(sums,), cost=1)(coup, p, west, south)
    sums = call(pair_kernel, shape(10, F32), [SMEM, VMEM, VMEM], VMEM, after=(t,))(j, sums, other)
    blocks = four(sums, "row", 1)
    x, to_south, ub = call(
        solve_kernel,
        (shape(INTERIOR, F32), shape(SENT, BF16), shape(INTERIOR, BF16)),
        [SMEM] + [VMEM] * 8,
        (ANY, VMEM, VMEM),
        [pltpu.VMEM((INTERIOR, RHS), F32), pltpu.SemaphoreType.DMA((2,))],
        after=(sums,),
        cost=4,
    )(i, coup, inv, block, t, h, west, south, basis)
    from_north = along(to_south, "row", -1)
    sums = call(
        rows_kernel, shape(19, F32), [SMEM] + [VMEM] * 4, VMEM, [pltpu.VMEM((4, 10, RHS), F32)], after=(to_south,)
    )(i, *blocks)
    blocks = four(sums, "col", 2)
    to_west = call(west_kernel, shape(SENT, BF16), [SMEM] + [VMEM] * 7, VMEM, after=(sums,), cost=1)(
        j, coup, block, h, ub, west, south, basis
    )
    from_east = along(to_west, "col", -1)
    shares = call(
        columns_kernel,
        (shape(16, F32),) * 4,
        [SMEM, SMEM] + [VMEM] * 5,
        (VMEM,) * 4,
        [pltpu.VMEM((4, 19, RHS), F32), pltpu.VMEM((48, RHS), F32), pltpu.VMEM((4, 16, RHS), F32)],
        after=(to_west,),
    )(i, j, *blocks, e)
    kept = call(kept_kernel, shape(2 * FACE, F32), [VMEM] * 6, VMEM, after=(shares[0],), cost=30)(
        coup, block, h, ub, west, south
    )
    blocks = [shares[0]] + [exchanged(shares[k], "row", 4, k) for k in (1, 2, 3)]
    z, currents = final(i, blocks, kept, from_east, from_north, w, basis)
    return x[None, None], z[None, None], currents


def solution(mesh):
    return jax.shard_map(
        local,
        mesh=mesh,
        in_specs=(
            P("row", "col", None, None),
            P("row", "col", None, None, None),
            P("row", "col", None, None),
            P("row", "col", None, None),
            P("row", "col", None, None),
            P("row", "col", None, None),
            P("row", "col", None, None),
            P(),
            P(),
            P("row", "col", None, None),
        ),
        out_specs=(P("row", "col", None, None), P("row", "col", None, None, None), P()),
        check_vma=False,
    )
```

profile of v0, /device:TPU:0, one launch (start us, length us, event | category | flops | bytes accessed | tf_op | source)
XLA Modules:
  0.0 54.8 jit_solution(11685436207508282737)
XLA Ops:
  0.6 0.7 %copy-done.5 = f32[1,1,2,512]{3,2,1,0:T(2,128)S(1)} copy-done((f32[1,1,2,512]{3,2,1,0:T(2,128)S(1)}, f32[1,1,2,512]{3,2,1,0:T(2,128)}, u32[]{:S(2)}) %copy-start.5) | copy-done | bytes 4120
  1.3 1.6 %copy-done.7 = f32[1,1,2,512,512]{4,3,2,1,0:T(8,128)S(1)} copy-done((f32[1,1,2,512,512]{4,3,2,1,0:T(8,128)S(1)}, f32[1,1,2,512,512]{4,3,2,1,0:T(8,128)}, u32[]{:S(2)}) %copy-start.7) | copy-done | bytes 2097176
  2.9 0.3 north_kernel.1.refs_3_
  3.2 4.1 %collective-permute-start.1 = (bf16[512,512]{1,0:T(8,128)(2,1)S(1)}, bf16[512,512]{1,0:T(8,128)(2,1)S(1)}, u32[]{:S(2)}, u32[]{:S(2)}) collective-permute-start(bf16[512,512]{1,0:T(8,128)(2,1)S(1)} %north_kernel.1.refs_3_), channel_id=1, source_target_pairs={{0,8},{8,16},{16,24},{24,32},{32,40},{40,48},{48,56},{56,64},{64,7... | collective-permute-start | bytes 1572872 | tf_op jit(solution)/shard_map/ppermute | solution.py:361
  7.3 0.0 copy-start.2
  7.3 0.0 copy-start.4
  7.3 0.0 copy-start
  7.3 0.0 copy-start.3
  7.3 0.0 copy-start.9
  7.3 0.0 copy-start.10
  7.4 0.5 east_kernel.1
  7.8 0.0 collective-permute-start
  7.9 0.3 copy-done.2
  8.2 1.3 %table_kernel.1.refs_5_.refs_6_ = f32[64,48]{1,0:T(8,128)S(1)} custom-call(s32[1]{0:T(128)} %bitcast.refs_0_, s32[1]{0:T(128)} %bitcast.5.refs_0_.refs_1_, s32[32,16]{1,0:T(8,128)S(1)} %bitcast.33, s32[32,16]{1,0:T(8,128)S(1)} %bitcast.34, f32[153,153]{1,0:T(8,128)S(1)} %copy-done.2, bf16[1024,512]{1,0:T(8,128)(2,1)S(1)} %get-tuple-element.22.refs_5_.refs_2_), custom_call_target="tpu_custom_call" | custom-call | flops 1000 | bytes 1000 | tf_op jit(solution)/shard_map/table_kernel/pallas_call | solution.py:80
  9.6 0.0 copy-done
  9.6 0.7 %copy-done.9 = f32[1,1,1024,512]{3,2,1,0:T(8,128)S(1)} copy-done((f32[1,1,1024,512]{3,2,1,0:T(8,128)S(1)}, f32[1,1,1024,512]{3,2,1,0:T(8,128)}, u32[]{:S(2)}) %copy-start.9) | copy-done | bytes 2097176
  10.3 2.4 %early_a_kernel.1 = (f32[1024,512]{1,0:T(8,128)S(1)}, f32[8,1024]{1,0:T(8,128)S(1)}, bf16[8,2048]{1,0:T(8,128)(2,1)S(1)}) custom-call(bf16[1024,2048]{1,0:T(8,128)(2,1)S(1)} %bitcast.15, f32[1024,512]{1,0:T(8,128)S(1)} %bitcast.40, bf16[1024,512]{1,0:T(8,128)(2,1)S(1)} %get-tuple-element.22.refs_5_.refs_2_, bf16[4,2048]{1,0:T(4,128)(2,1)S(1)} %bitcast.29, ...), custom_call_target="tpu_custom_call" | custom-call | flops 10000001024 | bytes 30001000 | tf_op jit(solution)/shard_map/early_a_kernel/pallas_call | solution.py:80
  12.7 0.0 slice-start.1
  12.7 1.4 %early_b_kernel.1 = (f32[8,2048]{1,0:T(8,128)S(1)}, f32[8,512]{1,0:T(8,128)S(1)}) custom-call(f32[8,1024]{1,0:T(8,128)S(1)} %get-tuple-element.26.refs_0_, bf16[1024,1024]{1,0:T(8,128)(2,1)S(1)} %bitcast.27, bf16[1024,2048]{1,0:T(8,128)(2,1)S(1)} %bitcast.16, f32[1024,512]{1,0:T(8,128)S(1)} %bitcast.41), custom_call_target="tpu_custom_call" | custom-call | flops 10000001024 | bytes 30001000 | tf_op jit(solution)/shard_map/early_b_kernel/pallas_call | solution.py:80
  14.0 0.9 %slice-done.1 = s8[4194304]{0:T(1024)(128)(4,1)S(1)} async-done(((s8[8388608]{0:T(1024)(128)(4,1)}), s8[4194304]{0:T(1024)(128)(4,1)S(1)}, s32[]{:S(2)}) %slice-start.1) | async-done | bytes 4194328
  15.0 3.6 %early_c_kernel.1 = (f32[2048,512]{1,0:T(8,128)S(1)}, f32[8,512]{1,0:T(8,128)S(1)}, bf16[16,1024]{1,0:T(8,128)(2,1)S(1)}) custom-call(bf16[8,2048]{1,0:T(8,128)(2,1)S(1)} %get-tuple-element.25.refs_0_, bf16[2048,2048]{1,0:T(8,128)(2,1)S(1)} %bitcast.23, bf16[1024,512]{1,0:T(8,128)(2,1)S(1)} %get-tuple-element.22.refs_5_.refs_2_, ...), custom_call_target="tpu_custom_call" | custom-call | flops 10000001024 | bytes 30001000 | tf_op jit(solution)/shard_map/early_c_kernel/pallas_call | solution.py:80
  18.6 0.0 collective-permute-done.refs_2_.refs_6_.refs_5_.refs_4_
  18.6 0.0 collective-permute-done.1.refs_3_.refs_7_.refs_6_.refs_5_
  18.6 0.2 corner_kernel.1.refs_4_.refs_1_
  18.8 0.6 %collective-permute-start.2 = (f32[8,512]{1,0:T(8,128)S(1)}, f32[8,512]{1,0:T(8,128)S(1)}, u32[]{:S(2)}, u32[]{:S(2)}) collective-permute-start(f32[8,512]{1,0:T(8,128)S(1)} %corner_kernel.1.refs_4_.refs_1_), channel_id=1, source_target_pairs={{0,1},{1,0},{2,3},{3,2},{4,5},{5,4},{6,7},{7,6},{8,9},{9,8},{10,11... | collective-permute-start | bytes 49160 | tf_op jit(solution)/shard_map/ppermute | solution.py:383
  19.4 1.3 %inner_kernel.1.refs_3_.refs_4_ = bf16[1024,512]{1,0:T(8,128)(2,1)S(1)} custom-call(bf16[1024,2048]{1,0:T(8,128)(2,1)S(1)} %bitcast.17, f32[1024,512]{1,0:T(8,128)S(1)} %get-tuple-element.23.refs_1_, bf16[512,512]{1,0:T(8,128)(2,1)S(1)} %collective-permute-done.refs_2_.refs_6_.refs_5_.refs_4_, ...), custom_call_target="tpu_custom_call" | custom-call | flops 1000001024 | bytes 3001000 | tf_op jit(solution)/shard_map/inner_kernel/pallas_call | solution.py:80
  20.8 2.0 %collective-permute-start.3 = (f32[10,512]{1,0:T(8,128)S(1)}, f32[10,512]{1,0:T(8,128)S(1)}, u32[]{:S(2)}, u32[]{:S(2)}) collective-permute-start(f32[10,512]{1,0:T(8,128)S(1)} %pair_kernel.1.refs_9_.refs_1_), channel_id=1, source_target_pairs={{8,0},{0,8},{24,16},{16,24},{40,32},{32,40},{56,48},{48,56},{72,64... | collective-permute-start | bytes 61448 | tf_op jit(solution)/shard_map/ppermute | solution.py:333
  22.7 3.4 %collective-permute-start.4 = (f32[10,512]{1,0:T(8,128)S(1)}, f32[10,512]{1,0:T(8,128)S(1)}, u32[]{:S(2)}, u32[]{:S(2)}) collective-permute-start(f32[10,512]{1,0:T(8,128)S(1)} %pair_kernel.1.refs_9_.refs_1_), channel_id=1, source_target_pairs={{16,0},{24,8},{0,16},{8,24},{48,32},{56,40},{32,48},{40,56},{80,64... | collective-permute-start | bytes 61448 | tf_op jit(solution)/shard_map/ppermute | solution.py:333
  26.1 0.0 collective-permute-start.5
  26.1 3.0 %solve_kernel.1 = (f32[1024,512]{1,0:T(8,128)}, bf16[528,512]{1,0:T(8,128)(2,1)S(1)}, bf16[1024,512]{1,0:T(8,128)(2,1)S(1)}) custom-call(s32[1]{0:T(128)} %bitcast.refs_0_, bf16[1024,2048]{1,0:T(8,128)(2,1)S(1)} %bitcast.18, bf16[1024,1024]{1,0:T(8,128)(2,1)S(1)} %bitcast.28, bf16[2048,2048]{1,0:T(8,128)(2,1)S(1)} %bitcast.24, ...), custom_call_target="tpu_custom_call" | custom-call | flops 4000001024 | bytes 12001000 | tf_op jit(solution)/shard_map/solve_kernel/pallas_call | solution.py:80
  29.1 5.8 %collective-permute-start.13 = (bf16[528,512]{1,0:T(8,128)(2,1)S(1)}, bf16[528,512]{1,0:T(8,128)(2,1)S(1)}, u32[]{:S(2)}, u32[]{:S(2)}) collective-permute-start(bf16[528,512]{1,0:T(8,128)(2,1)S(1)} %get-tuple-element.33.refs_5_), channel_id=1, source_target_pairs={{0,120},{8,0},{16,8},{24,16},{32,24},{40,32},{48,40},{56,48},{64,5... | collective-permute-start | bytes 1622024 | tf_op jit(solution)/shard_map/ppermute | solution.py:329
  34.9 1.6 %collective-permute-start.6 = (f32[19,512]{1,0:T(8,128)S(1)}, f32[19,512]{1,0:T(8,128)S(1)}, u32[]{:S(2)}, u32[]{:S(2)}) collective-permute-start(f32[19,512]{1,0:T(8,128)S(1)} %rows_kernel.1.refs_8_.refs_2_), channel_id=1, source_target_pairs={{2,0},{3,1},{0,2},{1,3},{6,4},{7,5},{4,6},{5,7},{10,8},{11,9},{8,1... | collective-permute-start | bytes 116744 | tf_op jit(solution)/shard_map/ppermute | solution.py:333
  36.5 2.7 %collective-permute-start.7 = (f32[19,512]{1,0:T(8,128)S(1)}, f32[19,512]{1,0:T(8,128)S(1)}, u32[]{:S(2)}, u32[]{:S(2)}) collective-permute-start(f32[19,512]{1,0:T(8,128)S(1)} %rows_kernel.1.refs_8_.refs_2_), channel_id=1, source_target_pairs={{4,0},{5,1},{6,2},{7,3},{0,4},{1,5},{2,6},{3,7},{12,8},{13,9},{14,... | collective-permute-start | bytes 116744 | tf_op jit(solution)/shard_map/ppermute | solution.py:333
  39.2 0.5 collective-permute-start.8
  39.7 1.3 %west_kernel.1.refs_7_ = bf16[528,512]{1,0:T(8,128)(2,1)S(1)} custom-call(s32[1]{0:T(128)} %bitcast.5.refs_0_.refs_1_, bf16[1024,2048]{1,0:T(8,128)(2,1)S(1)} %bitcast.19, bf16[2048,2048]{1,0:T(8,128)(2,1)S(1)} %bitcast.25, f32[2048,512]{1,0:T(8,128)S(1)} %get-tuple-element.31.refs_5_.refs_3_.refs_2_, ...), custom_call_target="tpu_custom_call" | custom-call | flops 1000001024 | bytes 3001000 | tf_op jit(solution)/shard_map/west_kernel/pallas_call | solution.py:80
  41.0 0.9 %collective-permute-start.12 = (bf16[528,512]{1,0:T(8,128)(2,1)S(1)}, bf16[528,512]{1,0:T(8,128)(2,1)S(1)}, u32[]{:S(2)}, u32[]{:S(2)}) collective-permute-start(bf16[528,512]{1,0:T(8,128)(2,1)S(1)} %west_kernel.1.refs_7_), channel_id=1, source_target_pairs={{0,7},{1,0},{2,1},{3,2},{4,3},{5,4},{6,5},{7,6},{8,15},{9,8},{10,9... | collective-permute-start | bytes 1622024 | tf_op jit(solution)/shard_map/ppermute | solution.py:329
  41.9 0.0 collective-permute-done.6.refs_3_
  41.9 0.2 collective-permute-done.7.refs_4_
  42.1 2.4 %collective-permute-done.8.refs_5_ = f32[19,512]{1,0:T(8,128)S(1)} collective-permute-done((f32[19,512]{1,0:T(8,128)S(1)}, f32[19,512]{1,0:T(8,128)S(1)}, u32[]{:S(2)}, u32[]{:S(2)}) %collective-permute-start.8) | collective-permute-done | bytes 38944 | tf_op jit(solution)/shard_map/ppermute | solution.py:333
  44.5 0.2 columns_kernel.1
  44.8 0.1 collective-permute-start.9
  44.9 2.2 %collective-permute-start.10 = (f32[16,512]{1,0:T(8,128)S(1)}, f32[16,512]{1,0:T(8,128)S(1)}, u32[]{:S(2)}, u32[]{:S(2)}) collective-permute-start(f32[16,512]{1,0:T(8,128)S(1)} %get-tuple-element.37), channel_id=1, source_target_pairs={{64,0},{72,8},{80,16},{88,24},{96,32},{104,40},{112,48},{120,56},{... | collective-permute-start | bytes 98312 | tf_op jit(solution)/shard_map/ppermute | solution.py:333
  47.1 2.5 %collective-permute-start.11 = (f32[16,512]{1,0:T(8,128)S(1)}, f32[16,512]{1,0:T(8,128)S(1)}, u32[]{:S(2)}, u32[]{:S(2)}) collective-permute-start(f32[16,512]{1,0:T(8,128)S(1)} %get-tuple-element.38), channel_id=1, source_target_pairs={{96,0},{104,8},{112,16},{120,24},{64,32},{72,40},{80,48},{88,56},{... | collective-permute-start | bytes 98312 | tf_op jit(solution)/shard_map/ppermute | solution.py:333
  49.5 2.3 %kept_kernel.1.refs_5_ = f32[1024,512]{1,0:T(8,128)S(1)} custom-call(bf16[1024,2048]{1,0:T(8,128)(2,1)S(1)} %bitcast.20, bf16[2048,2048]{1,0:T(8,128)(2,1)S(1)} %bitcast.26, f32[2048,512]{1,0:T(8,128)S(1)} %get-tuple-element.31.refs_5_.refs_3_.refs_2_, bf16[1024,512]{1,0:T(8,128)(2,1)S(1)} %get-tuple-element.34.refs_4_.refs_3_, ...), custom_call_target="tpu_custom_call" | custom-call | flops 30000001024 | bytes 90001000 | tf_op jit(solution)/shard_map/kept_kernel/pallas_call | solution.py:80
  51.9 0.3 collective-permute-done.11.refs_4_
  52.2 0.0 collective-permute-done.13.refs_7_
  52.2 0.0 collective-permute-done.12.refs_6_
  52.2 2.5 %final_kernel.1 = (f32[2,512,512]{2,1,0:T(8,128)}, f32[4,512]{1,0:T(4,128)}) custom-call(s32[1]{0:T(128)} %bitcast.refs_0_, f32[16,512]{1,0:T(8,128)S(1)} %get-tuple-element.35.refs_6_.refs_1_, f32[16,512]{1,0:T(8,128)S(1)} %collective-permute-done.9.refs_2_, f32[16,512]{1,0:T(8,128)S(1)} %collective-permute-done.10.refs_3_, ...), custom_call_target="tpu_custom_call" | custom-call | flops 1000 | bytes 1000 | tf_op jit(solution)/shard_map/final_kernel/pallas_call | solution.py:80
  (22 shorter events, 0.1 us)
Async XLA Ops:
  0.6 0.7 %copy-start.5 = (f32[1,1,2,512]{3,2,1,0:T(2,128)S(1)}, f32[1,1,2,512]{3,2,1,0:T(2,128)}, u32[]{:S(2)}) copy-start(f32[1,1,2,512]{3,2,1,0:T(2,128)} %param.12) | copy-start | bytes 12292
  1.3 1.6 %copy-start.7 = (f32[1,1,2,512,512]{4,3,2,1,0:T(8,128)S(1)}, f32[1,1,2,512,512]{4,3,2,1,0:T(8,128)}, u32[]{:S(2)}) copy-start(f32[1,1,2,512,512]{4,3,2,1,0:T(8,128)} %param.11) | copy-start | bytes 6291460
  2.9 4.4 %copy-start.6 = (f32[1,1,2,512]{3,2,1,0:T(2,128)S(1)}, f32[1,1,2,512]{3,2,1,0:T(2,128)}, u32[]{:S(2)}) copy-start(f32[1,1,2,512]{3,2,1,0:T(2,128)} %param.12) | copy-start | bytes 12292
  2.9 4.4 %copy-start.8 = (f32[1,1,2,512,512]{4,3,2,1,0:T(8,128)S(1)}, f32[1,1,2,512,512]{4,3,2,1,0:T(8,128)}, u32[]{:S(2)}) copy-start(f32[1,1,2,512,512]{4,3,2,1,0:T(8,128)} %param.11) | copy-start | bytes 6291460
  3.2 15.4 %collective-permute-start.1 = (bf16[512,512]{1,0:T(8,128)(2,1)S(1)}, bf16[512,512]{1,0:T(8,128)(2,1)S(1)}, u32[]{:S(2)}, u32[]{:S(2)}) collective-permute-start(bf16[512,512]{1,0:T(8,128)(2,1)S(1)} %north_kernel.1.refs_3_), channel_id=1, source_target_pairs={{0,8},{8,16},{16,24},{24,32},{32,40},{40,48},{48,56},{56,64},{64,7... | collective-permute-start | bytes 1572872 | tf_op jit(solution)/shard_map/ppermute | solution.py:361
  7.3 0.9 %copy-start.2 = (f32[153,153]{1,0:T(8,128)S(1)}, f32[153,153]{1,0:T(8,128)}, u32[]{:S(2)}) copy-start(f32[153,153]{1,0:T(8,128)} %refs_4_.1) | copy-start | bytes 280912
  7.3 0.9 %copy-start.4 = (s32[16,8,4]{0,2,1:T(4,128)S(1)}, s32[16,8,4]{0,2,1:T(4,128)}, u32[]{:S(2)}) copy-start(s32[16,8,4]{0,2,1:T(4,128)} %param.18) | copy-start | bytes 6148
  7.3 2.3 %copy-start = (bf16[1,1,1024,2048]{3,2,1,0:T(8,128)(2,1)S(1)}, bf16[1,1,1024,2048]{3,2,1,0:T(8,128)(2,1)}, u32[]{:S(2)}) copy-start(bf16[1,1,1024,2048]{3,2,1,0:T(8,128)(2,1)} %param.14) | copy-start | bytes 12582916
  7.3 2.3 %copy-start.3 = (bf16[1,1,4,2048]{3,2,1,0:T(4,128)(2,1)S(1)}, bf16[1,1,4,2048]{3,2,1,0:T(4,128)(2,1)}, u32[]{:S(2)}) copy-start(bf16[1,1,4,2048]{3,2,1,0:T(4,128)(2,1)} %param.16) | copy-start | bytes 49156
  7.3 2.9 %copy-start.9 = (f32[1,1,1024,512]{3,2,1,0:T(8,128)S(1)}, f32[1,1,1024,512]{3,2,1,0:T(8,128)}, u32[]{:S(2)}) copy-start(f32[1,1,1024,512]{3,2,1,0:T(8,128)} %param.10) | copy-start | bytes 6291460
  7.3 2.9 %copy-start.10 = (s32[1,1,4,512]{3,2,1,0:T(4,128)S(1)}, s32[1,1,4,512]{3,2,1,0:T(4,128)}, u32[]{:S(2)}) copy-start(s32[1,1,4,512]{3,2,1,0:T(4,128)} %param.19) | copy-start | bytes 24580
  7.8 10.7 %collective-permute-start = (bf16[512,512]{1,0:T(8,128)(2,1)S(1)}, bf16[512,512]{1,0:T(8,128)(2,1)S(1)}, u32[]{:S(2)}, u32[]{:S(2)}) collective-permute-start(bf16[512,512]{1,0:T(8,128)(2,1)S(1)} %get-tuple-element.24), channel_id=1, source_target_pairs={{0,1},{1,2},{2,3},{3,4},{4,5},{5,6},{6,7},{7,0},{8,9},{9,10},{10,1... | collective-permute-start | bytes 1572872 | tf_op jit(solution)/shard_map/ppermute | solution.py:329
  10.3 2.4 %copy-start.1 = (bf16[1,1,1024,1024]{3,2,1,0:T(8,128)(2,1)S(1)}, bf16[1,1,1024,1024]{3,2,1,0:T(8,128)(2,1)}, u32[]{:S(2)}) copy-start(bf16[1,1,1024,1024]{3,2,1,0:T(8,128)(2,1)} %param.13) | copy-start | bytes 6291460
  10.3 3.8 %slice-start = ((s8[8388608]{0:T(1024)(128)(4,1)}), s8[4194304]{0:T(1024)(128)(4,1)S(1)}, s32[]{:S(2)}) async-start(s8[8388608]{0:T(1024)(128)(4,1)} %bitcast.21), calls=%async_computation | async-start | bytes 8388608
  12.7 2.3 %slice-start.1 = ((s8[8388608]{0:T(1024)(128)(4,1)}), s8[4194304]{0:T(1024)(128)(4,1)S(1)}, s32[]{:S(2)}) async-start(s8[8388608]{0:T(1024)(128)(4,1)} %bitcast.21), calls=%async_computation.1 | async-start | bytes 8388608
  18.8 1.9 %collective-permute-start.2 = (f32[8,512]{1,0:T(8,128)S(1)}, f32[8,512]{1,0:T(8,128)S(1)}, u32[]{:S(2)}, u32[]{:S(2)}) collective-permute-start(f32[8,512]{1,0:T(8,128)S(1)} %corner_kernel.1.refs_4_.refs_1_), channel_id=1, source_target_pairs={{0,1},{1,0},{2,3},{3,2},{4,5},{5,4},{6,7},{7,6},{8,9},{9,8},{10,11... | collective-permute-start | bytes 49160 | tf_op jit(solution)/shard_map/ppermute | solution.py:383
  20.8 14.1 %collective-permute-start.3 = (f32[10,512]{1,0:T(8,128)S(1)}, f32[10,512]{1,0:T(8,128)S(1)}, u32[]{:S(2)}, u32[]{:S(2)}) collective-permute-start(f32[10,512]{1,0:T(8,128)S(1)} %pair_kernel.1.refs_9_.refs_1_), channel_id=1, source_target_pairs={{8,0},{0,8},{24,16},{16,24},{40,32},{32,40},{56,48},{48,56},{72,64... | collective-permute-start | bytes 61448 | tf_op jit(solution)/shard_map/ppermute | solution.py:333
  22.7 12.1 %collective-permute-start.4 = (f32[10,512]{1,0:T(8,128)S(1)}, f32[10,512]{1,0:T(8,128)S(1)}, u32[]{:S(2)}, u32[]{:S(2)}) collective-permute-start(f32[10,512]{1,0:T(8,128)S(1)} %pair_kernel.1.refs_9_.refs_1_), channel_id=1, source_target_pairs={{16,0},{24,8},{0,16},{8,24},{48,32},{56,40},{32,48},{40,56},{80,64... | collective-permute-start | bytes 61448 | tf_op jit(solution)/shard_map/ppermute | solution.py:333
  26.1 8.8 %collective-permute-start.5 = (f32[10,512]{1,0:T(8,128)S(1)}, f32[10,512]{1,0:T(8,128)S(1)}, u32[]{:S(2)}, u32[]{:S(2)}) collective-permute-start(f32[10,512]{1,0:T(8,128)S(1)} %pair_kernel.1.refs_9_.refs_1_), channel_id=1, source_target_pairs={{24,0},{16,8},{8,16},{0,24},{56,32},{48,40},{40,48},{32,56},{88,64... | collective-permute-start | bytes 61448 | tf_op jit(solution)/shard_map/ppermute | solution.py:333
  29.1 23.1 %collective-permute-start.13 = (bf16[528,512]{1,0:T(8,128)(2,1)S(1)}, bf16[528,512]{1,0:T(8,128)(2,1)S(1)}, u32[]{:S(2)}, u32[]{:S(2)}) collective-permute-start(bf16[528,512]{1,0:T(8,128)(2,1)S(1)} %get-tuple-element.33.refs_5_), channel_id=1, source_target_pairs={{0,120},{8,0},{16,8},{24,16},{32,24},{40,32},{48,40},{56,48},{64,5... | collective-permute-start | bytes 1622024 | tf_op jit(solution)/shard_map/ppermute | solution.py:329
  34.9 7.0 %collective-permute-start.6 = (f32[19,512]{1,0:T(8,128)S(1)}, f32[19,512]{1,0:T(8,128)S(1)}, u32[]{:S(2)}, u32[]{:S(2)}) collective-permute-start(f32[19,512]{1,0:T(8,128)S(1)} %rows_kernel.1.refs_8_.refs_2_), channel_id=1, source_target_pairs={{2,0},{3,1},{0,2},{1,3},{6,4},{7,5},{4,6},{5,7},{10,8},{11,9},{8,1... | collective-permute-start | bytes 116744 | tf_op jit(solution)/shard_map/ppermute | solution.py:333
  36.5 5.6 %collective-permute-start.7 = (f32[19,512]{1,0:T(8,128)S(1)}, f32[19,512]{1,0:T(8,128)S(1)}, u32[]{:S(2)}, u32[]{:S(2)}) collective-permute-start(f32[19,512]{1,0:T(8,128)S(1)} %rows_kernel.1.refs_8_.refs_2_), channel_id=1, source_target_pairs={{4,0},{5,1},{6,2},{7,3},{0,4},{1,5},{2,6},{3,7},{12,8},{13,9},{14,... | collective-permute-start | bytes 116744 | tf_op jit(solution)/shard_map/ppermute | solution.py:333
  39.2 5.3 %collective-permute-start.8 = (f32[19,512]{1,0:T(8,128)S(1)}, f32[19,512]{1,0:T(8,128)S(1)}, u32[]{:S(2)}, u32[]{:S(2)}) collective-permute-start(f32[19,512]{1,0:T(8,128)S(1)} %rows_kernel.1.refs_8_.refs_2_), channel_id=1, source_target_pairs={{6,0},{7,1},{4,2},{5,3},{2,4},{3,5},{0,6},{1,7},{14,8},{15,9},{12,... | collective-permute-start | bytes 116744 | tf_op jit(solution)/shard_map/ppermute | solution.py:333
  41.0 11.2 %collective-permute-start.12 = (bf16[528,512]{1,0:T(8,128)(2,1)S(1)}, bf16[528,512]{1,0:T(8,128)(2,1)S(1)}, u32[]{:S(2)}, u32[]{:S(2)}) collective-permute-start(bf16[528,512]{1,0:T(8,128)(2,1)S(1)} %west_kernel.1.refs_7_), channel_id=1, source_target_pairs={{0,7},{1,0},{2,1},{3,2},{4,3},{5,4},{6,5},{7,6},{8,15},{9,8},{10,9... | collective-permute-start | bytes 1622024 | tf_op jit(solution)/shard_map/ppermute | solution.py:329
  44.8 7.1 %collective-permute-start.9 = (f32[16,512]{1,0:T(8,128)S(1)}, f32[16,512]{1,0:T(8,128)S(1)}, u32[]{:S(2)}, u32[]{:S(2)}) collective-permute-start(f32[16,512]{1,0:T(8,128)S(1)} %get-tuple-element.36), channel_id=1, source_target_pairs={{32,0},{40,8},{48,16},{56,24},{0,32},{8,40},{16,48},{24,56},{96,64... | collective-permute-start | bytes 98312 | tf_op jit(solution)/shard_map/ppermute | solution.py:333
  44.9 7.1 %collective-permute-start.10 = (f32[16,512]{1,0:T(8,128)S(1)}, f32[16,512]{1,0:T(8,128)S(1)}, u32[]{:S(2)}, u32[]{:S(2)}) collective-permute-start(f32[16,512]{1,0:T(8,128)S(1)} %get-tuple-element.37), channel_id=1, source_target_pairs={{64,0},{72,8},{80,16},{88,24},{96,32},{104,40},{112,48},{120,56},{... | collective-permute-start | bytes 98312 | tf_op jit(solution)/shard_map/ppermute | solution.py:333
  47.1 5.1 %collective-permute-start.11 = (f32[16,512]{1,0:T(8,128)S(1)}, f32[16,512]{1,0:T(8,128)S(1)}, u32[]{:S(2)}, u32[]{:S(2)}) collective-permute-start(f32[16,512]{1,0:T(8,128)S(1)} %get-tuple-element.38), channel_id=1, source_target_pairs={{96,0},{104,8},{112,16},{120,24},{64,32},{72,40},{80,48},{88,56},{... | collective-permute-start | bytes 98312 | tf_op jit(solution)/shard_map/ppermute | solution.py:333
where the time goes:
time: 55 us; the launch traced here: 54.8 us
  starting transfers between devices  26.3 us (48%)
  Pallas kernels  20.3 us (37%)
  local copies, waits for them, and re-layouts  4.29 us (8%)
  waiting for transfers between devices  2.92 us (5%)
  between operations  1.06 us (2%)
    pallas_call x15, Pallas kernels, made(): result = run(*args, *extra)  20.3 us
    ppermute x9, starting transfers between devices, exchanged(): lax.ppermute(x, axis, [(d ^ k * stride, d) for d in range(lax.axis_size(a...  14.9 us
    ppermute x3, starting transfers between devices, along(): return lax.ppermute(x, axis, [(s, (s + d) % n) for s in range(n)])  6.69 us
    unnamed x26, local copies, waits for them, and re-layouts  4.29 us
    ppermute x1, starting transfers between devices, local(): south = lax.ppermute(to_north, 'row', [(s, s + 1) for s in range(ROWS - 1)])  4.07 us
    ppermute x9, waiting for transfers between devices, exchanged(): lax.ppermute(x, axis, [(d ^ k * stride, d) for d in range(lax.axis_size(a...  2.91 us
  transfers between devices with their start and end apart: 14, of which 3 were waited for; matrix products, arithmetic and copies ran while one was open for 0% of the time, Pallas kernels for 32%

commit v1 on v0

--- a/solution.py
+++ b/solution.py
@@ -87,13 +87,35 @@
     return jax.ShapeDtypeStruct((rows, columns), kind)
 
 
-def north_kernel(pos, faces, w, out):
+def north_kernel(pos, faces, weights, out, face, w, sem):
+    parts, rows = 4, FACE // 4
+    get_w = pltpu.make_async_copy(weights, w, sem.at[parts])
+    get_w.start()
+    copies = [
+        pltpu.make_async_copy(faces.at[1, pl.ds(c * rows, rows)], face.at[pl.ds(c * rows, rows)], sem.at[c])
+        for c in range(parts)
+    ]
+    for copy in copies:
+        copy.start()
+    get_w.wait()
     keep = (pos[0] < ROWS - 1).astype(F32)
-    out[...] = ((1.0 - column(w[1:2, :])) * keep * faces[1]).astype(BF16)
+    scale = (1.0 - column(w[1:2, :])) * keep
+    for c, copy in enumerate(copies):
+        copy.wait()
+        at = slice(c * rows, (c + 1) * rows)
+        out[at] = (scale[at] * face[at]).astype(BF16)
 
 
 def north_face(i, faces, w):
-    return call(north_kernel, shape(FACE, BF16), [SMEM, VMEM, VMEM], VMEM, cost=4)(i, faces, w)
+    return call(
+        north_kernel,
+        shape(FACE, BF16),
+        [SMEM, ANY, ANY],
+        VMEM,
+        [pltpu.VMEM((FACE, RHS), F32), pltpu.VMEM((2, FACE), F32), pltpu.SemaphoreType.DMA((5,))],
+        vmem=52,
+        cost=4,
+    )(i, faces, w)
 
 
 def east_kernel(pos, faces, w, out, own):
@@ -145,7 +167,6 @@
         VMEM,
         [pltpu.VMEM((64, coarse_inv.shape[0]), F32), pltpu.VMEM((24, COLS + 1), F32)],
         after=after,
-        cost=0,
     )(i, j, cm, cm, coarse_inv)
 
 
@@ -393,7 +414,7 @@
         after=(sums,),
         cost=4,
     )(i, coup, inv, block, t, h, west, south, basis)
-    from_north = along(to_south, "row", -1)
+    from_north = lax.ppermute(to_south, "row", [(s + 1, s) for s in range(ROWS - 1)])
     sums = call(
         rows_kernel, shape(19, F32), [SMEM] + [VMEM] * 4, VMEM, [pltpu.VMEM((4, 10, RHS), F32)], after=(to_south,)
     )(i, *blocks)

time: 55 us -> 56.4 us (1.025)
  waiting for transfers between devices: 2.92 us -> 6.45 us
  starting transfers between devices: 26.3 us -> 24.5 us
  local copies, waits for them, and re-layouts: 4.29 us -> 2.7 us
  Pallas kernels: 20.3 us -> 21.5 us
    ppermute x3 -> x2, starting transfers between devices: 6.69 us -> 0.71 us  [along(): return lax.ppermute(x, axis, [(s, (s + d) % n) for s in range(n)])]
    ppermute x9, waiting for transfers between devices: 2.91 us -> 6.44 us  [exchanged(): lax.ppermute(x, axis, [(d ^ k * stride, d) for d in range(lax.axis_size(a...]
    ppermute x9, starting transfers between devices: 14.9 us -> 17.9 us  [exchanged(): lax.ppermute(x, axis, [(d ^ k * stride, d) for d in range(lax.axis_size(a...]
    unnamed x26 -> x24, local copies, waits for them, and re-layouts: 4.29 us -> 2.7 us
    ppermute x0 -> x1, starting transfers between devices: none -> 1.29 us  [local(): lax.ppermute(to_south, 'row', [(s + 1, s) for s in range(ROWS - 1)])]
    pallas_call x15, Pallas kernels: 20.3 us -> 21.5 us  [made(): result = run(*args, *extra)]
  transfers between devices with their start and end apart: 14 -> 14, of which waited for: 3 -> 4; matrix products, arithmetic and copies ran while one was open for 0% -> 0% of each run, Pallas kernels for 32% -> 31%
where the time goes in v1:
time: 56.4 us; the launch traced here: 56.2 us
  starting transfers between devices  24.5 us (43%)
  Pallas kernels  21.5 us (38%)
  waiting for transfers between devices  6.45 us (11%)
  local copies, waits for them, and re-layouts  2.7 us (5%)
  between operations  1.07 us (2%)
    pallas_call x15, Pallas kernels, made(): result = run(*args, *extra)  21.5 us
    ppermute x9, starting transfers between devices, exchanged(): lax.ppermute(x, axis, [(d ^ k * stride, d) for d in range(lax.axis_size(a...  17.9 us
    ppermute x9, waiting for transfers between devices, exchanged(): lax.ppermute(x, axis, [(d ^ k * stride, d) for d in range(lax.axis_size(a...  6.44 us
    ppermute x1, starting transfers between devices, local(): south = lax.ppermute(to_north, 'row', [(s, s + 1) for s in range(ROWS - 1)])  3.94 us
    unnamed x24, local copies, waits for them, and re-layouts  2.7 us
    ppermute x1, starting transfers between devices, local(): lax.ppermute(to_south, 'row', [(s + 1, s) for s in range(ROWS - 1)])  1.29 us
  transfers between devices with their start and end apart: 14, of which 4 were waited for; matrix products, arithmetic and copies ran while one was open for 0% of the time, Pallas kernels for 31%

profile of v1, /device:TPU:0, one launch (start us, length us, event | category | flops | bytes accessed | tf_op | source)
XLA Modules:
  0.0 56.2 jit_solution(3047883091690132627)
XLA Ops:
  0.6 0.7 %copy-done.5 = f32[1,1,2,512]{3,2,1,0:T(2,128)S(1)} copy-done((f32[1,1,2,512]{3,2,1,0:T(2,128)S(1)}, f32[1,1,2,512]{3,2,1,0:T(2,128)}, u32[]{:S(2)}) %copy-start.5) | copy-done | bytes 4120
  1.3 1.5 %north_kernel.1.refs_3_ = bf16[512,512]{1,0:T(8,128)(2,1)S(1)} custom-call(s32[1]{0:T(128)} %bitcast.refs_0_, f32[2,512,512]{2,1,0:T(8,128)} %bitcast.38, f32[2,512]{1,0:T(2,128)S(1)} %bitcast.35), custom_call_target="tpu_custom_call" | custom-call | flops 4000001024 | bytes 12001000 | tf_op jit(solution)/shard_map/north_kernel/pallas_call | solution.py:80
  2.8 3.9 %collective-permute-start.1 = (bf16[512,512]{1,0:T(8,128)(2,1)S(1)}, bf16[512,512]{1,0:T(8,128)(2,1)S(1)}, u32[]{:S(2)}, u32[]{:S(2)}) collective-permute-start(bf16[512,512]{1,0:T(8,128)(2,1)S(1)} %north_kernel.1.refs_3_), channel_id=1, source_target_pairs={{0,8},{8,16},{16,24},{24,32},{32,40},{40,48},{48,56},{56,64},{64,7... | collective-permute-start | bytes 1572872 | tf_op jit(solution)/shard_map/ppermute | solution.py:382
  6.8 0.0 copy-start.2
  6.8 0.0 copy-start.4
  6.8 0.0 copy-start
  6.8 0.0 copy-start.3
  6.8 0.0 copy-start.8
  6.9 0.0 copy-start.9
  6.9 0.5 east_kernel.1
  7.4 0.0 collective-permute-start
  7.4 0.3 copy-done.2
  7.7 1.3 %table_kernel.1.refs_5_.refs_6_ = f32[64,48]{1,0:T(8,128)S(1)} custom-call(s32[1]{0:T(128)} %bitcast.refs_0_, s32[1]{0:T(128)} %bitcast.5.refs_0_.refs_1_, s32[32,16]{1,0:T(8,128)S(1)} %bitcast.33, s32[32,16]{1,0:T(8,128)S(1)} %bitcast.34, f32[153,153]{1,0:T(8,128)S(1)} %copy-done.2, bf16[1024,512]{1,0:T(8,128)(2,1)S(1)} %get-tuple-element.22.refs_5_.refs_2_), custom_call_target="tpu_custom_call" | custom-call | flops 1000 | bytes 1000 | tf_op jit(solution)/shard_map/table_kernel/pallas_call | solution.py:80
  9.1 0.0 copy-done
  9.1 0.7 %copy-done.8 = f32[1,1,1024,512]{3,2,1,0:T(8,128)S(1)} copy-done((f32[1,1,1024,512]{3,2,1,0:T(8,128)S(1)}, f32[1,1,1024,512]{3,2,1,0:T(8,128)}, u32[]{:S(2)}) %copy-start.8) | copy-done | bytes 2097176
  9.8 2.4 %early_a_kernel.1 = (f32[1024,512]{1,0:T(8,128)S(1)}, f32[8,1024]{1,0:T(8,128)S(1)}, bf16[8,2048]{1,0:T(8,128)(2,1)S(1)}) custom-call(bf16[1024,2048]{1,0:T(8,128)(2,1)S(1)} %bitcast.15, f32[1024,512]{1,0:T(8,128)S(1)} %bitcast.40, bf16[1024,512]{1,0:T(8,128)(2,1)S(1)} %get-tuple-element.22.refs_5_.refs_2_, bf16[4,2048]{1,0:T(4,128)(2,1)S(1)} %bitcast.29, ...), custom_call_target="tpu_custom_call" | custom-call | flops 10000001024 | bytes 30001000 | tf_op jit(solution)/shard_map/early_a_kernel/pallas_call | solution.py:80
  12.2 0.0 slice-start.1
  12.2 1.4 %early_b_kernel.1 = (f32[8,2048]{1,0:T(8,128)S(1)}, f32[8,512]{1,0:T(8,128)S(1)}) custom-call(f32[8,1024]{1,0:T(8,128)S(1)} %get-tuple-element.26.refs_0_, bf16[1024,1024]{1,0:T(8,128)(2,1)S(1)} %bitcast.27, bf16[1024,2048]{1,0:T(8,128)(2,1)S(1)} %bitcast.16, f32[1024,512]{1,0:T(8,128)S(1)} %bitcast.41), custom_call_target="tpu_custom_call" | custom-call | flops 10000001024 | bytes 30001000 | tf_op jit(solution)/shard_map/early_b_kernel/pallas_call | solution.py:80
  13.6 0.9 %slice-done.1 = s8[4194304]{0:T(1024)(128)(4,1)S(1)} async-done(((s8[8388608]{0:T(1024)(128)(4,1)}), s8[4194304]{0:T(1024)(128)(4,1)S(1)}, s32[]{:S(2)}) %slice-start.1) | async-done | bytes 4194328
  14.5 3.6 %early_c_kernel.1 = (f32[2048,512]{1,0:T(8,128)S(1)}, f32[8,512]{1,0:T(8,128)S(1)}, bf16[16,1024]{1,0:T(8,128)(2,1)S(1)}) custom-call(bf16[8,2048]{1,0:T(8,128)(2,1)S(1)} %get-tuple-element.25.refs_0_, bf16[2048,2048]{1,0:T(8,128)(2,1)S(1)} %bitcast.23, bf16[1024,512]{1,0:T(8,128)(2,1)S(1)} %get-tuple-element.22.refs_5_.refs_2_, ...), custom_call_target="tpu_custom_call" | custom-call | flops 10000001024 | bytes 30001000 | tf_op jit(solution)/shard_map/early_c_kernel/pallas_call | solution.py:80
  18.1 0.0 collective-permute-done.refs_2_.refs_6_.refs_5_.refs_4_
  18.1 0.2 corner_kernel.1.refs_4_.refs_1_
  18.3 0.6 %collective-permute-start.2 = (f32[8,512]{1,0:T(8,128)S(1)}, f32[8,512]{1,0:T(8,128)S(1)}, u32[]{:S(2)}, u32[]{:S(2)}) collective-permute-start(f32[8,512]{1,0:T(8,128)S(1)} %corner_kernel.1.refs_4_.refs_1_), channel_id=1, source_target_pairs={{0,1},{1,0},{2,3},{3,2},{4,5},{5,4},{6,7},{7,6},{8,9},{9,8},{10,11... | collective-permute-start | bytes 49160 | tf_op jit(solution)/shard_map/ppermute | solution.py:404
  18.9 1.3 %inner_kernel.1.refs_3_.refs_4_ = bf16[1024,512]{1,0:T(8,128)(2,1)S(1)} custom-call(bf16[1024,2048]{1,0:T(8,128)(2,1)S(1)} %bitcast.17, f32[1024,512]{1,0:T(8,128)S(1)} %get-tuple-element.23.refs_1_, bf16[512,512]{1,0:T(8,128)(2,1)S(1)} %collective-permute-done.refs_2_.refs_6_.refs_5_.refs_4_, ...), custom_call_target="tpu_custom_call" | custom-call | flops 1000001024 | bytes 3001000 | tf_op jit(solution)/shard_map/inner_kernel/pallas_call | solution.py:80
  20.3 2.0 %collective-permute-start.3 = (f32[10,512]{1,0:T(8,128)S(1)}, f32[10,512]{1,0:T(8,128)S(1)}, u32[]{:S(2)}, u32[]{:S(2)}) collective-permute-start(f32[10,512]{1,0:T(8,128)S(1)} %pair_kernel.1.refs_9_.refs_1_), channel_id=1, source_target_pairs={{8,0},{0,8},{24,16},{16,24},{40,32},{32,40},{56,48},{48,56},{72,64... | collective-permute-start | bytes 61448 | tf_op jit(solution)/shard_map/ppermute | solution.py:354
  22.2 3.4 %collective-permute-start.4 = (f32[10,512]{1,0:T(8,128)S(1)}, f32[10,512]{1,0:T(8,128)S(1)}, u32[]{:S(2)}, u32[]{:S(2)}) collective-permute-start(f32[10,512]{1,0:T(8,128)S(1)} %pair_kernel.1.refs_9_.refs_1_), channel_id=1, source_target_pairs={{16,0},{24,8},{0,16},{8,24},{48,32},{56,40},{32,48},{40,56},{80,64... | collective-permute-start | bytes 61448 | tf_op jit(solution)/shard_map/ppermute | solution.py:354
  25.6 0.0 collective-permute-start.5
  25.6 3.0 %solve_kernel.1 = (f32[1024,512]{1,0:T(8,128)}, bf16[528,512]{1,0:T(8,128)(2,1)S(1)}, bf16[1024,512]{1,0:T(8,128)(2,1)S(1)}) custom-call(s32[1]{0:T(128)} %bitcast.refs_0_, bf16[1024,2048]{1,0:T(8,128)(2,1)S(1)} %bitcast.18, bf16[1024,1024]{1,0:T(8,128)(2,1)S(1)} %bitcast.28, bf16[2048,2048]{1,0:T(8,128)(2,1)S(1)} %bitcast.24, ...), custom_call_target="tpu_custom_call" | custom-call | flops 4000001024 | bytes 12001000 | tf_op jit(solution)/shard_map/solve_kernel/pallas_call | solution.py:80
  28.6 1.3 %collective-permute-start.13 = (bf16[528,512]{1,0:T(8,128)(2,1)S(1)}, bf16[528,512]{1,0:T(8,128)(2,1)S(1)}, u32[]{:S(2)}, u32[]{:S(2)}) collective-permute-start(bf16[528,512]{1,0:T(8,128)(2,1)S(1)} %get-tuple-element.33.refs_5_), channel_id=1, source_target_pairs={{8,0},{16,8},{24,16},{32,24},{40,32},{48,40},{56,48},{64,56},{72,6... | collective-permute-start | bytes 1622024 | tf_op jit(solution)/shard_map/ppermute | solution.py:417
  29.9 0.0 collective-permute-done.3.refs_2_
  29.9 0.8 %collective-permute-done.5.refs_4_ = f32[10,512]{1,0:T(8,128)S(1)} collective-permute-done((f32[10,512]{1,0:T(8,128)S(1)}, f32[10,512]{1,0:T(8,128)S(1)}, u32[]{:S(2)}, u32[]{:S(2)}) %collective-permute-start.5) | collective-permute-done | bytes 20512 | tf_op jit(solution)/shard_map/ppermute | solution.py:354
  30.8 1.6 %collective-permute-start.6 = (f32[19,512]{1,0:T(8,128)S(1)}, f32[19,512]{1,0:T(8,128)S(1)}, u32[]{:S(2)}, u32[]{:S(2)}) collective-permute-start(f32[19,512]{1,0:T(8,128)S(1)} %rows_kernel.1.refs_8_.refs_2_), channel_id=1, source_target_pairs={{2,0},{3,1},{0,2},{1,3},{6,4},{7,5},{4,6},{5,7},{10,8},{11,9},{8,1... | collective-permute-start | bytes 116744 | tf_op jit(solution)/shard_map/ppermute | solution.py:354
  32.4 2.7 %collective-permute-start.7 = (f32[19,512]{1,0:T(8,128)S(1)}, f32[19,512]{1,0:T(8,128)S(1)}, u32[]{:S(2)}, u32[]{:S(2)}) collective-permute-start(f32[19,512]{1,0:T(8,128)S(1)} %rows_kernel.1.refs_8_.refs_2_), channel_id=1, source_target_pairs={{4,0},{5,1},{6,2},{7,3},{0,4},{1,5},{2,6},{3,7},{12,8},{13,9},{14,... | collective-permute-start | bytes 116744 | tf_op jit(solution)/shard_map/ppermute | solution.py:354
  35.1 0.5 collective-permute-start.8
  35.6 1.3 %west_kernel.1.refs_7_ = bf16[528,512]{1,0:T(8,128)(2,1)S(1)} custom-call(s32[1]{0:T(128)} %bitcast.5.refs_0_.refs_1_, bf16[1024,2048]{1,0:T(8,128)(2,1)S(1)} %bitcast.19, bf16[2048,2048]{1,0:T(8,128)(2,1)S(1)} %bitcast.25, f32[2048,512]{1,0:T(8,128)S(1)} %get-tuple-element.31.refs_5_.refs_3_.refs_2_, ...), custom_call_target="tpu_custom_call" | custom-call | flops 1000001024 | bytes 3001000 | tf_op jit(solution)/shard_map/west_kernel/pallas_call | solution.py:80
  36.8 0.7 %collective-permute-start.12 = (bf16[528,512]{1,0:T(8,128)(2,1)S(1)}, bf16[528,512]{1,0:T(8,128)(2,1)S(1)}, u32[]{:S(2)}, u32[]{:S(2)}) collective-permute-start(bf16[528,512]{1,0:T(8,128)(2,1)S(1)} %west_kernel.1.refs_7_), channel_id=1, source_target_pairs={{0,7},{1,0},{2,1},{3,2},{4,3},{5,4},{6,5},{7,6},{8,15},{9,8},{10,9... | collective-permute-start | bytes 1622024 | tf_op jit(solution)/shard_map/ppermute | solution.py:350
  37.5 0.0 collective-permute-done.6.refs_3_
  37.5 0.5 collective-permute-done.7.refs_4_
  38.0 2.4 %collective-permute-done.8.refs_5_ = f32[19,512]{1,0:T(8,128)S(1)} collective-permute-done((f32[19,512]{1,0:T(8,128)S(1)}, f32[19,512]{1,0:T(8,128)S(1)}, u32[]{:S(2)}, u32[]{:S(2)}) %collective-permute-start.8) | collective-permute-done | bytes 38944 | tf_op jit(solution)/shard_map/ppermute | solution.py:354
  40.4 0.2 columns_kernel.1
  40.6 4.6 %collective-permute-start.9 = (f32[16,512]{1,0:T(8,128)S(1)}, f32[16,512]{1,0:T(8,128)S(1)}, u32[]{:S(2)}, u32[]{:S(2)}) collective-permute-start(f32[16,512]{1,0:T(8,128)S(1)} %get-tuple-element.36), channel_id=1, source_target_pairs={{32,0},{40,8},{48,16},{56,24},{0,32},{8,40},{16,48},{24,56},{96,64... | collective-permute-start | bytes 98312 | tf_op jit(solution)/shard_map/ppermute | solution.py:354
  45.2 3.2 %collective-permute-start.10 = (f32[16,512]{1,0:T(8,128)S(1)}, f32[16,512]{1,0:T(8,128)S(1)}, u32[]{:S(2)}, u32[]{:S(2)}) collective-permute-start(f32[16,512]{1,0:T(8,128)S(1)} %get-tuple-element.37), channel_id=1, source_target_pairs={{64,0},{72,8},{80,16},{88,24},{96,32},{104,40},{112,48},{120,56},{... | collective-permute-start | bytes 98312 | tf_op jit(solution)/shard_map/ppermute | solution.py:354
  48.4 2.3 %kept_kernel.1.refs_5_ = f32[1024,512]{1,0:T(8,128)S(1)} custom-call(bf16[1024,2048]{1,0:T(8,128)(2,1)S(1)} %bitcast.20, bf16[2048,2048]{1,0:T(8,128)(2,1)S(1)} %bitcast.26, f32[2048,512]{1,0:T(8,128)S(1)} %get-tuple-element.31.refs_5_.refs_3_.refs_2_, bf16[1024,512]{1,0:T(8,128)(2,1)S(1)} %get-tuple-element.34.refs_4_.refs_3_, ...), custom_call_target="tpu_custom_call" | custom-call | flops 30000001024 | bytes 90001000 | tf_op jit(solution)/shard_map/kept_kernel/pallas_call | solution.py:80
  50.8 0.0 collective-permute-done.10.refs_3_
  50.8 2.7 %collective-permute-done.11.refs_4_ = f32[16,512]{1,0:T(8,128)S(1)} collective-permute-done((f32[16,512]{1,0:T(8,128)S(1)}, f32[16,512]{1,0:T(8,128)S(1)}, u32[]{:S(2)}, u32[]{:S(2)}) %collective-permute-start.11) | collective-permute-done | bytes 32800 | tf_op jit(solution)/shard_map/ppermute | solution.py:354
  53.6 0.0 collective-permute-done.13.refs_7_
  53.6 0.0 collective-permute-done.12.refs_6_
  53.6 2.5 %final_kernel.1 = (f32[2,512,512]{2,1,0:T(8,128)}, f32[4,512]{1,0:T(4,128)}) custom-call(s32[1]{0:T(128)} %bitcast.refs_0_, f32[16,512]{1,0:T(8,128)S(1)} %get-tuple-element.35.refs_6_.refs_1_, f32[16,512]{1,0:T(8,128)S(1)} %collective-permute-done.9.refs_2_, f32[16,512]{1,0:T(8,128)S(1)} %collective-permute-done.10.refs_3_, ...), custom_call_target="tpu_custom_call" | custom-call | flops 1000 | bytes 1000 | tf_op jit(solution)/shard_map/final_kernel/pallas_call | solution.py:80
  (20 shorter events, 0.1 us)
Async XLA Ops:
  0.6 0.7 %copy-start.5 = (f32[1,1,2,512]{3,2,1,0:T(2,128)S(1)}, f32[1,1,2,512]{3,2,1,0:T(2,128)}, u32[]{:S(2)}) copy-start(f32[1,1,2,512]{3,2,1,0:T(2,128)} %param.12) | copy-start | bytes 12292
  1.3 5.5 %copy-start.6 = (f32[1,1,2,512]{3,2,1,0:T(2,128)S(1)}, f32[1,1,2,512]{3,2,1,0:T(2,128)}, u32[]{:S(2)}) copy-start(f32[1,1,2,512]{3,2,1,0:T(2,128)} %param.12) | copy-start | bytes 12292
  1.3 5.5 %copy-start.7 = (f32[1,1,2,512,512]{4,3,2,1,0:T(8,128)S(1)}, f32[1,1,2,512,512]{4,3,2,1,0:T(8,128)}, u32[]{:S(2)}) copy-start(f32[1,1,2,512,512]{4,3,2,1,0:T(8,128)} %param.11) | copy-start | bytes 6291460
  2.8 15.3 %collective-permute-start.1 = (bf16[512,512]{1,0:T(8,128)(2,1)S(1)}, bf16[512,512]{1,0:T(8,128)(2,1)S(1)}, u32[]{:S(2)}, u32[]{:S(2)}) collective-permute-start(bf16[512,512]{1,0:T(8,128)(2,1)S(1)} %north_kernel.1.refs_3_), channel_id=1, source_target_pairs={{0,8},{8,16},{16,24},{24,32},{32,40},{40,48},{48,56},{56,64},{64,7... | collective-permute-start | bytes 1572872 | tf_op jit(solution)/shard_map/ppermute | solution.py:382
  6.8 0.9 %copy-start.2 = (f32[153,153]{1,0:T(8,128)S(1)}, f32[153,153]{1,0:T(8,128)}, u32[]{:S(2)}) copy-start(f32[153,153]{1,0:T(8,128)} %refs_4_.1) | copy-start | bytes 280912
  6.8 0.9 %copy-start.4 = (s32[16,8,4]{0,2,1:T(4,128)S(1)}, s32[16,8,4]{0,2,1:T(4,128)}, u32[]{:S(2)}) copy-start(s32[16,8,4]{0,2,1:T(4,128)} %param.18) | copy-start | bytes 6148
  6.8 2.3 %copy-start = (bf16[1,1,1024,2048]{3,2,1,0:T(8,128)(2,1)S(1)}, bf16[1,1,1024,2048]{3,2,1,0:T(8,128)(2,1)}, u32[]{:S(2)}) copy-start(bf16[1,1,1024,2048]{3,2,1,0:T(8,128)(2,1)} %param.14) | copy-start | bytes 12582916
  6.8 2.3 %copy-start.3 = (bf16[1,1,4,2048]{3,2,1,0:T(4,128)(2,1)S(1)}, bf16[1,1,4,2048]{3,2,1,0:T(4,128)(2,1)}, u32[]{:S(2)}) copy-start(bf16[1,1,4,2048]{3,2,1,0:T(4,128)(2,1)} %param.16) | copy-start | bytes 49156
  6.8 2.9 %copy-start.8 = (f32[1,1,1024,512]{3,2,1,0:T(8,128)S(1)}, f32[1,1,1024,512]{3,2,1,0:T(8,128)}, u32[]{:S(2)}) copy-start(f32[1,1,1024,512]{3,2,1,0:T(8,128)} %param.10) | copy-start | bytes 6291460
  6.9 2.9 %copy-start.9 = (s32[1,1,4,512]{3,2,1,0:T(4,128)S(1)}, s32[1,1,4,512]{3,2,1,0:T(4,128)}, u32[]{:S(2)}) copy-start(s32[1,1,4,512]{3,2,1,0:T(4,128)} %param.19) | copy-start | bytes 24580
  7.4 10.7 %collective-permute-start = (bf16[512,512]{1,0:T(8,128)(2,1)S(1)}, bf16[512,512]{1,0:T(8,128)(2,1)S(1)}, u32[]{:S(2)}, u32[]{:S(2)}) collective-permute-start(bf16[512,512]{1,0:T(8,128)(2,1)S(1)} %get-tuple-element.24), channel_id=1, source_target_pairs={{0,1},{1,2},{2,3},{3,4},{4,5},{5,6},{6,7},{7,0},{8,9},{9,10},{10,1... | collective-permute-start | bytes 1572872 | tf_op jit(solution)/shard_map/ppermute | solution.py:350
  9.8 2.4 %copy-start.1 = (bf16[1,1,1024,1024]{3,2,1,0:T(8,128)(2,1)S(1)}, bf16[1,1,1024,1024]{3,2,1,0:T(8,128)(2,1)}, u32[]{:S(2)}) copy-start(bf16[1,1,1024,1024]{3,2,1,0:T(8,128)(2,1)} %param.13) | copy-start | bytes 6291460
  9.8 3.8 %slice-start = ((s8[8388608]{0:T(1024)(128)(4,1)}), s8[4194304]{0:T(1024)(128)(4,1)S(1)}, s32[]{:S(2)}) async-start(s8[8388608]{0:T(1024)(128)(4,1)} %bitcast.21), calls=%async_computation | async-start | bytes 8388608
  12.2 2.3 %slice-start.1 = ((s8[8388608]{0:T(1024)(128)(4,1)}), s8[4194304]{0:T(1024)(128)(4,1)S(1)}, s32[]{:S(2)}) async-start(s8[8388608]{0:T(1024)(128)(4,1)} %bitcast.21), calls=%async_computation.1 | async-start | bytes 8388608
  18.3 1.9 %collective-permute-start.2 = (f32[8,512]{1,0:T(8,128)S(1)}, f32[8,512]{1,0:T(8,128)S(1)}, u32[]{:S(2)}, u32[]{:S(2)}) collective-permute-start(f32[8,512]{1,0:T(8,128)S(1)} %corner_kernel.1.refs_4_.refs_1_), channel_id=1, source_target_pairs={{0,1},{1,0},{2,3},{3,2},{4,5},{5,4},{6,7},{7,6},{8,9},{9,8},{10,11... | collective-permute-start | bytes 49160 | tf_op jit(solution)/shard_map/ppermute | solution.py:404
  20.3 9.7 %collective-permute-start.3 = (f32[10,512]{1,0:T(8,128)S(1)}, f32[10,512]{1,0:T(8,128)S(1)}, u32[]{:S(2)}, u32[]{:S(2)}) collective-permute-start(f32[10,512]{1,0:T(8,128)S(1)} %pair_kernel.1.refs_9_.refs_1_), channel_id=1, source_target_pairs={{8,0},{0,8},{24,16},{16,24},{40,32},{32,40},{56,48},{48,56},{72,64... | collective-permute-start | bytes 61448 | tf_op jit(solution)/shard_map/ppermute | solution.py:354
  22.2 7.7 %collective-permute-start.4 = (f32[10,512]{1,0:T(8,128)S(1)}, f32[10,512]{1,0:T(8,128)S(1)}, u32[]{:S(2)}, u32[]{:S(2)}) collective-permute-start(f32[10,512]{1,0:T(8,128)S(1)} %pair_kernel.1.refs_9_.refs_1_), channel_id=1, source_target_pairs={{16,0},{24,8},{0,16},{8,24},{48,32},{56,40},{32,48},{40,56},{80,64... | collective-permute-start | bytes 61448 | tf_op jit(solution)/shard_map/ppermute | solution.py:354
  25.6 5.1 %collective-permute-start.5 = (f32[10,512]{1,0:T(8,128)S(1)}, f32[10,512]{1,0:T(8,128)S(1)}, u32[]{:S(2)}, u32[]{:S(2)}) collective-permute-start(f32[10,512]{1,0:T(8,128)S(1)} %pair_kernel.1.refs_9_.refs_1_), channel_id=1, source_target_pairs={{24,0},{16,8},{8,16},{0,24},{56,32},{48,40},{40,48},{32,56},{88,64... | collective-permute-start | bytes 61448 | tf_op jit(solution)/shard_map/ppermute | solution.py:354
  28.6 25.0 %collective-permute-start.13 = (bf16[528,512]{1,0:T(8,128)(2,1)S(1)}, bf16[528,512]{1,0:T(8,128)(2,1)S(1)}, u32[]{:S(2)}, u32[]{:S(2)}) collective-permute-start(bf16[528,512]{1,0:T(8,128)(2,1)S(1)} %get-tuple-element.33.refs_5_), channel_id=1, source_target_pairs={{8,0},{16,8},{24,16},{32,24},{40,32},{48,40},{56,48},{64,56},{72,6... | collective-permute-start | bytes 1622024 | tf_op jit(solution)/shard_map/ppermute | solution.py:417
  30.8 6.7 %collective-permute-start.6 = (f32[19,512]{1,0:T(8,128)S(1)}, f32[19,512]{1,0:T(8,128)S(1)}, u32[]{:S(2)}, u32[]{:S(2)}) collective-permute-start(f32[19,512]{1,0:T(8,128)S(1)} %rows_kernel.1.refs_8_.refs_2_), channel_id=1, source_target_pairs={{2,0},{3,1},{0,2},{1,3},{6,4},{7,5},{4,6},{5,7},{10,8},{11,9},{8,1... | collective-permute-start | bytes 116744 | tf_op jit(solution)/shard_map/ppermute | solution.py:354
  32.4 5.6 %collective-permute-start.7 = (f32[19,512]{1,0:T(8,128)S(1)}, f32[19,512]{1,0:T(8,128)S(1)}, u32[]{:S(2)}, u32[]{:S(2)}) collective-permute-start(f32[19,512]{1,0:T(8,128)S(1)} %rows_kernel.1.refs_8_.refs_2_), channel_id=1, source_target_pairs={{4,0},{5,1},{6,2},{7,3},{0,4},{1,5},{2,6},{3,7},{12,8},{13,9},{14,... | collective-permute-start | bytes 116744 | tf_op jit(solution)/shard_map/ppermute | solution.py:354
  35.1 5.3 %collective-permute-start.8 = (f32[19,512]{1,0:T(8,128)S(1)}, f32[19,512]{1,0:T(8,128)S(1)}, u32[]{:S(2)}, u32[]{:S(2)}) collective-permute-start(f32[19,512]{1,0:T(8,128)S(1)} %rows_kernel.1.refs_8_.refs_2_), channel_id=1, source_target_pairs={{6,0},{7,1},{4,2},{5,3},{2,4},{3,5},{0,6},{1,7},{14,8},{15,9},{12,... | collective-permute-start | bytes 116744 | tf_op jit(solution)/shard_map/ppermute | solution.py:354
  36.8 16.7 %collective-permute-start.12 = (bf16[528,512]{1,0:T(8,128)(2,1)S(1)}, bf16[528,512]{1,0:T(8,128)(2,1)S(1)}, u32[]{:S(2)}, u32[]{:S(2)}) collective-permute-start(bf16[528,512]{1,0:T(8,128)(2,1)S(1)} %west_kernel.1.refs_7_), channel_id=1, source_target_pairs={{0,7},{1,0},{2,1},{3,2},{4,3},{5,4},{6,5},{7,6},{8,15},{9,8},{10,9... | collective-permute-start | bytes 1622024 | tf_op jit(solution)/shard_map/ppermute | solution.py:350
  40.6 10.2 %collective-permute-start.9 = (f32[16,512]{1,0:T(8,128)S(1)}, f32[16,512]{1,0:T(8,128)S(1)}, u32[]{:S(2)}, u32[]{:S(2)}) collective-permute-start(f32[16,512]{1,0:T(8,128)S(1)} %get-tuple-element.36), channel_id=1, source_target_pairs={{32,0},{40,8},{48,16},{56,24},{0,32},{8,40},{16,48},{24,56},{96,64... | collective-permute-start | bytes 98312 | tf_op jit(solution)/shard_map/ppermute | solution.py:354
  45.2 5.6 %collective-permute-start.10 = (f32[16,512]{1,0:T(8,128)S(1)}, f32[16,512]{1,0:T(8,128)S(1)}, u32[]{:S(2)}, u32[]{:S(2)}) collective-permute-start(f32[16,512]{1,0:T(8,128)S(1)} %get-tuple-element.37), channel_id=1, source_target_pairs={{64,0},{72,8},{80,16},{88,24},{96,32},{104,40},{112,48},{120,56},{... | collective-permute-start | bytes 98312 | tf_op jit(solution)/shard_map/ppermute | solution.py:354
  48.4 5.1 %collective-permute-start.11 = (f32[16,512]{1,0:T(8,128)S(1)}, f32[16,512]{1,0:T(8,128)S(1)}, u32[]{:S(2)}, u32[]{:S(2)}) collective-permute-start(f32[16,512]{1,0:T(8,128)S(1)} %get-tuple-element.38), channel_id=1, source_target_pairs={{96,0},{104,8},{112,16},{120,24},{64,32},{72,40},{80,48},{88,56},{... | collective-permute-start | bytes 98312 | tf_op jit(solution)/shard_map/ppermute | solution.py:354

commit v2 on v1

--- a/solution.py
+++ b/solution.py
@@ -379,7 +379,7 @@
     basis = corner_trace_basis[0, 0]
 
     to_north = north_face(i, faces_in, w)
-    south = lax.ppermute(to_north, "row", [(s, s + 1) for s in range(ROWS - 1)])
+    south = along(to_north, "row", 1)
     to_east, own = east_face(j, faces_in, w, (to_north,))
     west = along(to_east, "col", 1)
     e = table(i, j, corner_map, coarse_inv, (own,))
@@ -414,7 +414,7 @@
         after=(sums,),
         cost=4,
     )(i, coup, inv, block, t, h, west, south, basis)
-    from_north = lax.ppermute(to_south, "row", [(s + 1, s) for s in range(ROWS - 1)])
+    from_north = along(to_south, "row", -1)
     sums = call(
         rows_kernel, shape(19, F32), [SMEM] + [VMEM] * 4, VMEM, [pltpu.VMEM((4, 10, RHS), F32)], after=(to_south,)
     )(i, *blocks)

time: 56.4 us -> 52.7 us (0.934)
  starting transfers between devices: 24.5 us -> 19.1 us
  waiting for transfers between devices: 6.45 us -> 8.12 us
    ppermute x2 -> x0, starting transfers between devices: 5.23 us -> none  [the longest x1 3.94 us: local(): south = lax.ppermute(to_north, 'row', [(s, s + 1) for s in range(ROWS - 1)])]
    ppermute x2 -> x4, waiting for transfers between devices: 0.01 us -> 5.2 us  [along(): return lax.ppermute(x, axis, [(s, (s + d) % n) for s in range(n)])]
    ppermute x2 -> x4, starting transfers between devices: 0.71 us -> 4.82 us  [along(): return lax.ppermute(x, axis, [(s, (s + d) % n) for s in range(n)])]
    ppermute x9, starting transfers between devices: 17.9 us -> 14.3 us  [exchanged(): lax.ppermute(x, axis, [(d ^ k * stride, d) for d in range(lax.axis_size(a...]
    ppermute x9, waiting for transfers between devices: 6.44 us -> 2.92 us  [exchanged(): lax.ppermute(x, axis, [(d ^ k * stride, d) for d in range(lax.axis_size(a...]
    ppermute x1, starting transfers between devices: 0.61 us -> 0.01 us  [local(): other = lax.ppermute(sums, 'col', [(s, s ^ 1) for s in range(COLS)])]
  transfers between devices with their start and end apart: 14 -> 14, of which waited for: 4 -> 4; matrix products, arithmetic and copies ran while one was open for 0% -> 0% of each run, Pallas kernels for 31% -> 33%
where the time goes in v2:
time: 52.7 us; the launch traced here: 52.5 us
  Pallas kernels  21.5 us (41%)
  starting transfers between devices  19.1 us (36%)
  waiting for transfers between devices  8.12 us (15%)
  local copies, waits for them, and re-layouts  2.71 us (5%)
  between operations  1.02 us (2%)
    pallas_call x15, Pallas kernels, made(): result = run(*args, *extra)  21.5 us
    ppermute x9, starting transfers between devices, exchanged(): lax.ppermute(x, axis, [(d ^ k * stride, d) for d in range(lax.axis_size(a...  14.3 us
    ppermute x4, waiting for transfers between devices, along(): return lax.ppermute(x, axis, [(s, (s + d) % n) for s in range(n)])  5.2 us
    ppermute x4, starting transfers between devices, along(): return lax.ppermute(x, axis, [(s, (s + d) % n) for s in range(n)])  4.82 us
    ppermute x9, waiting for transfers between devices, exchanged(): lax.ppermute(x, axis, [(d ^ k * stride, d) for d in range(lax.axis_size(a...  2.92 us
    unnamed x24, local copies, waits for them, and re-layouts  2.71 us
  transfers between devices with their start and end apart: 14, of which 4 were waited for; matrix products, arithmetic and copies ran while one was open for 0% of the time, Pallas kernels for 33%

profile of v2, /device:TPU:0, one launch (start us, length us, event | category | flops | bytes accessed | tf_op | source)
XLA Modules:
  0.0 52.5 jit_solution(4311717253147029902)
XLA Ops:
  0.6 0.7 %copy-done.5 = f32[1,1,2,512]{3,2,1,0:T(2,128)S(1)} copy-done((f32[1,1,2,512]{3,2,1,0:T(2,128)S(1)}, f32[1,1,2,512]{3,2,1,0:T(2,128)}, u32[]{:S(2)}) %copy-start.5) | copy-done | bytes 4120
  1.3 1.5 %north_kernel.1.refs_3_ = bf16[512,512]{1,0:T(8,128)(2,1)S(1)} custom-call(s32[1]{0:T(128)} %bitcast.refs_0_, f32[2,512,512]{2,1,0:T(8,128)} %bitcast.38, f32[2,512]{1,0:T(2,128)S(1)} %bitcast.35), custom_call_target="tpu_custom_call" | custom-call | flops 4000001024 | bytes 12001000 | tf_op jit(solution)/shard_map/north_kernel/pallas_call | solution.py:80
  2.8 2.1 %collective-permute-start.1 = (bf16[512,512]{1,0:T(8,128)(2,1)S(1)}, bf16[512,512]{1,0:T(8,128)(2,1)S(1)}, u32[]{:S(2)}, u32[]{:S(2)}) collective-permute-start(bf16[512,512]{1,0:T(8,128)(2,1)S(1)} %north_kernel.1.refs_3_), channel_id=1, source_target_pairs={{0,8},{8,16},{16,24},{24,32},{32,40},{40,48},{48,56},{56,64},{64,7... | collective-permute-start | bytes 1572872 | tf_op jit(solution)/shard_map/ppermute | solution.py:350
  4.9 0.0 copy-start
  4.9 0.0 copy-start.3
  4.9 0.0 copy-start.8
  4.9 0.0 copy-start.9
  5.0 0.5 east_kernel.1
  5.4 0.0 collective-permute-start
  5.5 0.4 copy-done.2
  5.8 1.3 %table_kernel.1.refs_5_.refs_6_ = f32[64,48]{1,0:T(8,128)S(1)} custom-call(s32[1]{0:T(128)} %bitcast.refs_0_, s32[1]{0:T(128)} %bitcast.5.refs_0_.refs_1_, s32[32,16]{1,0:T(8,128)S(1)} %bitcast.33, s32[32,16]{1,0:T(8,128)S(1)} %bitcast.34, f32[153,153]{1,0:T(8,128)S(1)} %copy-done.2, bf16[1024,512]{1,0:T(8,128)(2,1)S(1)} %get-tuple-element.22.refs_5_.refs_2_), custom_call_target="tpu_custom_call" | custom-call | flops 1000 | bytes 1000 | tf_op jit(solution)/shard_map/table_kernel/pallas_call | solution.py:80
  7.2 0.0 copy-done
  7.2 0.7 %copy-done.8 = f32[1,1,1024,512]{3,2,1,0:T(8,128)S(1)} copy-done((f32[1,1,1024,512]{3,2,1,0:T(8,128)S(1)}, f32[1,1,1024,512]{3,2,1,0:T(8,128)}, u32[]{:S(2)}) %copy-start.8) | copy-done | bytes 2097176
  7.9 2.4 %early_a_kernel.1 = (f32[1024,512]{1,0:T(8,128)S(1)}, f32[8,1024]{1,0:T(8,128)S(1)}, bf16[8,2048]{1,0:T(8,128)(2,1)S(1)}) custom-call(bf16[1024,2048]{1,0:T(8,128)(2,1)S(1)} %bitcast.15, f32[1024,512]{1,0:T(8,128)S(1)} %bitcast.40, bf16[1024,512]{1,0:T(8,128)(2,1)S(1)} %get-tuple-element.22.refs_5_.refs_2_, bf16[4,2048]{1,0:T(4,128)(2,1)S(1)} %bitcast.29, ...), custom_call_target="tpu_custom_call" | custom-call | flops 10000001024 | bytes 30001000 | tf_op jit(solution)/shard_map/early_a_kernel/pallas_call | solution.py:80
  10.3 0.0 slice-start.1
  10.3 1.4 %early_b_kernel.1 = (f32[8,2048]{1,0:T(8,128)S(1)}, f32[8,512]{1,0:T(8,128)S(1)}) custom-call(f32[8,1024]{1,0:T(8,128)S(1)} %get-tuple-element.26.refs_0_, bf16[1024,1024]{1,0:T(8,128)(2,1)S(1)} %bitcast.27, bf16[1024,2048]{1,0:T(8,128)(2,1)S(1)} %bitcast.16, f32[1024,512]{1,0:T(8,128)S(1)} %bitcast.41), custom_call_target="tpu_custom_call" | custom-call | flops 10000001024 | bytes 30001000 | tf_op jit(solution)/shard_map/early_b_kernel/pallas_call | solution.py:80
  11.7 0.9 %slice-done.1 = s8[4194304]{0:T(1024)(128)(4,1)S(1)} async-done(((s8[8388608]{0:T(1024)(128)(4,1)}), s8[4194304]{0:T(1024)(128)(4,1)S(1)}, s32[]{:S(2)}) %slice-start.1) | async-done | bytes 4194328
  12.6 3.6 %early_c_kernel.1 = (f32[2048,512]{1,0:T(8,128)S(1)}, f32[8,512]{1,0:T(8,128)S(1)}, bf16[16,1024]{1,0:T(8,128)(2,1)S(1)}) custom-call(bf16[8,2048]{1,0:T(8,128)(2,1)S(1)} %get-tuple-element.25.refs_0_, bf16[2048,2048]{1,0:T(8,128)(2,1)S(1)} %bitcast.23, bf16[1024,512]{1,0:T(8,128)(2,1)S(1)} %get-tuple-element.22.refs_5_.refs_2_, ...), custom_call_target="tpu_custom_call" | custom-call | flops 10000001024 | bytes 30001000 | tf_op jit(solution)/shard_map/early_c_kernel/pallas_call | solution.py:80
  16.2 0.0 collective-permute-done.refs_2_.refs_6_.refs_5_.refs_4_
  16.2 5.2 %collective-permute-done.1.refs_3_.refs_7_.refs_6_.refs_5_ = bf16[512,512]{1,0:T(8,128)(2,1)S(1)} collective-permute-done((bf16[512,512]{1,0:T(8,128)(2,1)S(1)}, bf16[512,512]{1,0:T(8,128)(2,1)S(1)}, u32[]{:S(2)}, u32[]{:S(2)}) %collective-permute-start.1) | collective-permute-done | bytes 524320 | tf_op jit(solution)/shard_map/ppermute | solution.py:350
  21.4 0.2 corner_kernel.1.refs_4_.refs_1_
  21.6 0.0 collective-permute-start.2
  21.6 1.3 %inner_kernel.1.refs_3_.refs_4_ = bf16[1024,512]{1,0:T(8,128)(2,1)S(1)} custom-call(bf16[1024,2048]{1,0:T(8,128)(2,1)S(1)} %bitcast.17, f32[1024,512]{1,0:T(8,128)S(1)} %get-tuple-element.23.refs_1_, bf16[512,512]{1,0:T(8,128)(2,1)S(1)} %collective-permute-done.refs_2_.refs_6_.refs_5_.refs_4_, ...), custom_call_target="tpu_custom_call" | custom-call | flops 1000001024 | bytes 3001000 | tf_op jit(solution)/shard_map/inner_kernel/pallas_call | solution.py:80
  22.9 0.0 collective-permute-done.2.refs_2_
  23.0 0.1 collective-permute-start.3
  23.1 0.7 %collective-permute-start.4 = (f32[10,512]{1,0:T(8,128)S(1)}, f32[10,512]{1,0:T(8,128)S(1)}, u32[]{:S(2)}, u32[]{:S(2)}) collective-permute-start(f32[10,512]{1,0:T(8,128)S(1)} %pair_kernel.1.refs_9_.refs_1_), channel_id=1, source_target_pairs={{16,0},{24,8},{0,16},{8,24},{48,32},{56,40},{32,48},{40,56},{80,64... | collective-permute-start | bytes 61448 | tf_op jit(solution)/shard_map/ppermute | solution.py:354
  23.8 3.9 %collective-permute-start.5 = (f32[10,512]{1,0:T(8,128)S(1)}, f32[10,512]{1,0:T(8,128)S(1)}, u32[]{:S(2)}, u32[]{:S(2)}) collective-permute-start(f32[10,512]{1,0:T(8,128)S(1)} %pair_kernel.1.refs_9_.refs_1_), channel_id=1, source_target_pairs={{24,0},{16,8},{8,16},{0,24},{56,32},{48,40},{40,48},{32,56},{88,64... | collective-permute-start | bytes 61448 | tf_op jit(solution)/shard_map/ppermute | solution.py:354
  27.7 3.0 %solve_kernel.1 = (f32[1024,512]{1,0:T(8,128)}, bf16[528,512]{1,0:T(8,128)(2,1)S(1)}, bf16[1024,512]{1,0:T(8,128)(2,1)S(1)}) custom-call(s32[1]{0:T(128)} %bitcast.refs_0_, bf16[1024,2048]{1,0:T(8,128)(2,1)S(1)} %bitcast.18, bf16[1024,1024]{1,0:T(8,128)(2,1)S(1)} %bitcast.28, bf16[2048,2048]{1,0:T(8,128)(2,1)S(1)} %bitcast.24, ...), custom_call_target="tpu_custom_call" | custom-call | flops 4000001024 | bytes 12001000 | tf_op jit(solution)/shard_map/solve_kernel/pallas_call | solution.py:80
  30.7 1.8 %collective-permute-start.13 = (bf16[528,512]{1,0:T(8,128)(2,1)S(1)}, bf16[528,512]{1,0:T(8,128)(2,1)S(1)}, u32[]{:S(2)}, u32[]{:S(2)}) collective-permute-start(bf16[528,512]{1,0:T(8,128)(2,1)S(1)} %get-tuple-element.33.refs_5_), channel_id=1, source_target_pairs={{0,120},{8,0},{16,8},{24,16},{32,24},{40,32},{48,40},{56,48},{64,5... | collective-permute-start | bytes 1622024 | tf_op jit(solution)/shard_map/ppermute | solution.py:350
  32.5 0.0 collective-permute-done.3.refs_2_
  32.5 0.0 collective-permute-done.4.refs_3_
  32.6 1.6 %collective-permute-start.6 = (f32[19,512]{1,0:T(8,128)S(1)}, f32[19,512]{1,0:T(8,128)S(1)}, u32[]{:S(2)}, u32[]{:S(2)}) collective-permute-start(f32[19,512]{1,0:T(8,128)S(1)} %rows_kernel.1.refs_8_.refs_2_), channel_id=1, source_target_pairs={{2,0},{3,1},{0,2},{1,3},{6,4},{7,5},{4,6},{5,7},{10,8},{11,9},{8,1... | collective-permute-start | bytes 116744 | tf_op jit(solution)/shard_map/ppermute | solution.py:354
  34.2 2.7 %collective-permute-start.7 = (f32[19,512]{1,0:T(8,128)S(1)}, f32[19,512]{1,0:T(8,128)S(1)}, u32[]{:S(2)}, u32[]{:S(2)}) collective-permute-start(f32[19,512]{1,0:T(8,128)S(1)} %rows_kernel.1.refs_8_.refs_2_), channel_id=1, source_target_pairs={{4,0},{5,1},{6,2},{7,3},{0,4},{1,5},{2,6},{3,7},{12,8},{13,9},{14,... | collective-permute-start | bytes 116744 | tf_op jit(solution)/shard_map/ppermute | solution.py:354
  36.9 0.5 collective-permute-start.8
  37.4 1.3 %west_kernel.1.refs_7_ = bf16[528,512]{1,0:T(8,128)(2,1)S(1)} custom-call(s32[1]{0:T(128)} %bitcast.5.refs_0_.refs_1_, bf16[1024,2048]{1,0:T(8,128)(2,1)S(1)} %bitcast.19, bf16[2048,2048]{1,0:T(8,128)(2,1)S(1)} %bitcast.25, f32[2048,512]{1,0:T(8,128)S(1)} %get-tuple-element.31.refs_5_.refs_3_.refs_2_, ...), custom_call_target="tpu_custom_call" | custom-call | flops 1000001024 | bytes 3001000 | tf_op jit(solution)/shard_map/west_kernel/pallas_call | solution.py:80
  38.6 0.9 %collective-permute-start.12 = (bf16[528,512]{1,0:T(8,128)(2,1)S(1)}, bf16[528,512]{1,0:T(8,128)(2,1)S(1)}, u32[]{:S(2)}, u32[]{:S(2)}) collective-permute-start(bf16[528,512]{1,0:T(8,128)(2,1)S(1)} %west_kernel.1.refs_7_), channel_id=1, source_target_pairs={{0,7},{1,0},{2,1},{3,2},{4,3},{5,4},{6,5},{7,6},{8,15},{9,8},{10,9... | collective-permute-start | bytes 1622024 | tf_op jit(solution)/shard_map/ppermute | solution.py:350
  39.6 0.2 collective-permute-done.7.refs_4_
  39.8 2.4 %collective-permute-done.8.refs_5_ = f32[19,512]{1,0:T(8,128)S(1)} collective-permute-done((f32[19,512]{1,0:T(8,128)S(1)}, f32[19,512]{1,0:T(8,128)S(1)}, u32[]{:S(2)}, u32[]{:S(2)}) %collective-permute-start.8) | collective-permute-done | bytes 38944 | tf_op jit(solution)/shard_map/ppermute | solution.py:354
  42.2 0.2 columns_kernel.1
  42.5 0.1 collective-permute-start.9
  42.5 2.2 %collective-permute-start.10 = (f32[16,512]{1,0:T(8,128)S(1)}, f32[16,512]{1,0:T(8,128)S(1)}, u32[]{:S(2)}, u32[]{:S(2)}) collective-permute-start(f32[16,512]{1,0:T(8,128)S(1)} %get-tuple-element.37), channel_id=1, source_target_pairs={{64,0},{72,8},{80,16},{88,24},{96,32},{104,40},{112,48},{120,56},{... | collective-permute-start | bytes 98312 | tf_op jit(solution)/shard_map/ppermute | solution.py:354
  44.7 2.5 %collective-permute-start.11 = (f32[16,512]{1,0:T(8,128)S(1)}, f32[16,512]{1,0:T(8,128)S(1)}, u32[]{:S(2)}, u32[]{:S(2)}) collective-permute-start(f32[16,512]{1,0:T(8,128)S(1)} %get-tuple-element.38), channel_id=1, source_target_pairs={{96,0},{104,8},{112,16},{120,24},{64,32},{72,40},{80,48},{88,56},{... | collective-permute-start | bytes 98312 | tf_op jit(solution)/shard_map/ppermute | solution.py:354
  47.2 2.3 %kept_kernel.1.refs_5_ = f32[1024,512]{1,0:T(8,128)S(1)} custom-call(bf16[1024,2048]{1,0:T(8,128)(2,1)S(1)} %bitcast.20, bf16[2048,2048]{1,0:T(8,128)(2,1)S(1)} %bitcast.26, f32[2048,512]{1,0:T(8,128)S(1)} %get-tuple-element.31.refs_5_.refs_3_.refs_2_, bf16[1024,512]{1,0:T(8,128)(2,1)S(1)} %get-tuple-element.34.refs_4_.refs_3_, ...), custom_call_target="tpu_custom_call" | custom-call | flops 30000001024 | bytes 90001000 | tf_op jit(solution)/shard_map/kept_kernel/pallas_call | solution.py:80
  49.6 0.0 collective-permute-done.9.refs_2_
  49.6 0.0 collective-permute-done.10.refs_3_
  49.6 0.3 collective-permute-done.11.refs_4_
  49.9 0.0 collective-permute-done.12.refs_6_
  49.9 2.5 %final_kernel.1 = (f32[2,512,512]{2,1,0:T(8,128)}, f32[4,512]{1,0:T(4,128)}) custom-call(s32[1]{0:T(128)} %bitcast.refs_0_, f32[16,512]{1,0:T(8,128)S(1)} %get-tuple-element.35.refs_6_.refs_1_, f32[16,512]{1,0:T(8,128)S(1)} %collective-permute-done.9.refs_2_, f32[16,512]{1,0:T(8,128)S(1)} %collective-permute-done.10.refs_3_, ...), custom_call_target="tpu_custom_call" | custom-call | flops 1000 | bytes 1000 | tf_op jit(solution)/shard_map/final_kernel/pallas_call | solution.py:80
  (20 shorter events, 0.1 us)
Async XLA Ops:
  0.6 0.7 %copy-start.5 = (f32[1,1,2,512]{3,2,1,0:T(2,128)S(1)}, f32[1,1,2,512]{3,2,1,0:T(2,128)}, u32[]{:S(2)}) copy-start(f32[1,1,2,512]{3,2,1,0:T(2,128)} %param.12) | copy-start | bytes 12292
  1.3 3.6 %copy-start.6 = (f32[1,1,2,512]{3,2,1,0:T(2,128)S(1)}, f32[1,1,2,512]{3,2,1,0:T(2,128)}, u32[]{:S(2)}) copy-start(f32[1,1,2,512]{3,2,1,0:T(2,128)} %param.12) | copy-start | bytes 12292
  1.3 3.6 %copy-start.7 = (f32[1,1,2,512,512]{4,3,2,1,0:T(8,128)S(1)}, f32[1,1,2,512,512]{4,3,2,1,0:T(8,128)}, u32[]{:S(2)}) copy-start(f32[1,1,2,512,512]{4,3,2,1,0:T(8,128)} %param.11) | copy-start | bytes 6291460
  2.8 18.6 %collective-permute-start.1 = (bf16[512,512]{1,0:T(8,128)(2,1)S(1)}, bf16[512,512]{1,0:T(8,128)(2,1)S(1)}, u32[]{:S(2)}, u32[]{:S(2)}) collective-permute-start(bf16[512,512]{1,0:T(8,128)(2,1)S(1)} %north_kernel.1.refs_3_), channel_id=1, source_target_pairs={{0,8},{8,16},{16,24},{24,32},{32,40},{40,48},{48,56},{56,64},{64,7... | collective-permute-start | bytes 1572872 | tf_op jit(solution)/shard_map/ppermute | solution.py:350
  4.9 0.9 %copy-start.2 = (f32[153,153]{1,0:T(8,128)S(1)}, f32[153,153]{1,0:T(8,128)}, u32[]{:S(2)}) copy-start(f32[153,153]{1,0:T(8,128)} %refs_4_.1) | copy-start | bytes 280912
  4.9 0.9 %copy-start.4 = (s32[16,8,4]{0,2,1:T(4,128)S(1)}, s32[16,8,4]{0,2,1:T(4,128)}, u32[]{:S(2)}) copy-start(s32[16,8,4]{0,2,1:T(4,128)} %param.18) | copy-start | bytes 6148
  4.9 2.3 %copy-start = (bf16[1,1,1024,2048]{3,2,1,0:T(8,128)(2,1)S(1)}, bf16[1,1,1024,2048]{3,2,1,0:T(8,128)(2,1)}, u32[]{:S(2)}) copy-start(bf16[1,1,1024,2048]{3,2,1,0:T(8,128)(2,1)} %param.14) | copy-start | bytes 12582916
  4.9 2.3 %copy-start.3 = (bf16[1,1,4,2048]{3,2,1,0:T(4,128)(2,1)S(1)}, bf16[1,1,4,2048]{3,2,1,0:T(4,128)(2,1)}, u32[]{:S(2)}) copy-start(bf16[1,1,4,2048]{3,2,1,0:T(4,128)(2,1)} %param.16) | copy-start | bytes 49156
  4.9 2.9 %copy-start.8 = (f32[1,1,1024,512]{3,2,1,0:T(8,128)S(1)}, f32[1,1,1024,512]{3,2,1,0:T(8,128)}, u32[]{:S(2)}) copy-start(f32[1,1,1024,512]{3,2,1,0:T(8,128)} %param.10) | copy-start | bytes 6291460
  4.9 2.9 %copy-start.9 = (s32[1,1,4,512]{3,2,1,0:T(4,128)S(1)}, s32[1,1,4,512]{3,2,1,0:T(4,128)}, u32[]{:S(2)}) copy-start(s32[1,1,4,512]{3,2,1,0:T(4,128)} %param.19) | copy-start | bytes 24580
  5.4 10.7 %collective-permute-start = (bf16[512,512]{1,0:T(8,128)(2,1)S(1)}, bf16[512,512]{1,0:T(8,128)(2,1)S(1)}, u32[]{:S(2)}, u32[]{:S(2)}) collective-permute-start(bf16[512,512]{1,0:T(8,128)(2,1)S(1)} %get-tuple-element.24), channel_id=1, source_target_pairs={{0,1},{1,2},{2,3},{3,4},{4,5},{5,6},{6,7},{7,0},{8,9},{9,10},{10,1... | collective-permute-start | bytes 1572872 | tf_op jit(solution)/shard_map/ppermute | solution.py:350
  7.9 2.4 %copy-start.1 = (bf16[1,1,1024,1024]{3,2,1,0:T(8,128)(2,1)S(1)}, bf16[1,1,1024,1024]{3,2,1,0:T(8,128)(2,1)}, u32[]{:S(2)}) copy-start(bf16[1,1,1024,1024]{3,2,1,0:T(8,128)(2,1)} %param.13) | copy-start | bytes 6291460
  7.9 3.8 %slice-start = ((s8[8388608]{0:T(1024)(128)(4,1)}), s8[4194304]{0:T(1024)(128)(4,1)S(1)}, s32[]{:S(2)}) async-start(s8[8388608]{0:T(1024)(128)(4,1)} %bitcast.21), calls=%async_computation | async-start | bytes 8388608
  10.3 2.3 %slice-start.1 = ((s8[8388608]{0:T(1024)(128)(4,1)}), s8[4194304]{0:T(1024)(128)(4,1)S(1)}, s32[]{:S(2)}) async-start(s8[8388608]{0:T(1024)(128)(4,1)} %bitcast.21), calls=%async_computation.1 | async-start | bytes 8388608
  21.6 1.3 %collective-permute-start.2 = (f32[8,512]{1,0:T(8,128)S(1)}, f32[8,512]{1,0:T(8,128)S(1)}, u32[]{:S(2)}, u32[]{:S(2)}) collective-permute-start(f32[8,512]{1,0:T(8,128)S(1)} %corner_kernel.1.refs_4_.refs_1_), channel_id=1, source_target_pairs={{0,1},{1,0},{2,3},{3,2},{4,5},{5,4},{6,7},{7,6},{8,9},{9,8},{10,11... | collective-permute-start | bytes 49160 | tf_op jit(solution)/shard_map/ppermute | solution.py:404
  23.0 9.6 %collective-permute-start.3 = (f32[10,512]{1,0:T(8,128)S(1)}, f32[10,512]{1,0:T(8,128)S(1)}, u32[]{:S(2)}, u32[]{:S(2)}) collective-permute-start(f32[10,512]{1,0:T(8,128)S(1)} %pair_kernel.1.refs_9_.refs_1_), channel_id=1, source_target_pairs={{8,0},{0,8},{24,16},{16,24},{40,32},{32,40},{56,48},{48,56},{72,64... | collective-permute-start | bytes 61448 | tf_op jit(solution)/shard_map/ppermute | solution.py:354
  23.1 9.5 %collective-permute-start.4 = (f32[10,512]{1,0:T(8,128)S(1)}, f32[10,512]{1,0:T(8,128)S(1)}, u32[]{:S(2)}, u32[]{:S(2)}) collective-permute-start(f32[10,512]{1,0:T(8,128)S(1)} %pair_kernel.1.refs_9_.refs_1_), channel_id=1, source_target_pairs={{16,0},{24,8},{0,16},{8,24},{48,32},{56,40},{32,48},{40,56},{80,64... | collective-permute-start | bytes 61448 | tf_op jit(solution)/shard_map/ppermute | solution.py:354
  23.8 8.8 %collective-permute-start.5 = (f32[10,512]{1,0:T(8,128)S(1)}, f32[10,512]{1,0:T(8,128)S(1)}, u32[]{:S(2)}, u32[]{:S(2)}) collective-permute-start(f32[10,512]{1,0:T(8,128)S(1)} %pair_kernel.1.refs_9_.refs_1_), channel_id=1, source_target_pairs={{24,0},{16,8},{8,16},{0,24},{56,32},{48,40},{40,48},{32,56},{88,64... | collective-permute-start | bytes 61448 | tf_op jit(solution)/shard_map/ppermute | solution.py:354
  30.7 19.1 %collective-permute-start.13 = (bf16[528,512]{1,0:T(8,128)(2,1)S(1)}, bf16[528,512]{1,0:T(8,128)(2,1)S(1)}, u32[]{:S(2)}, u32[]{:S(2)}) collective-permute-start(bf16[528,512]{1,0:T(8,128)(2,1)S(1)} %get-tuple-element.33.refs_5_), channel_id=1, source_target_pairs={{0,120},{8,0},{16,8},{24,16},{32,24},{40,32},{48,40},{56,48},{64,5... | collective-permute-start | bytes 1622024 | tf_op jit(solution)/shard_map/ppermute | solution.py:350
  32.6 7.0 %collective-permute-start.6 = (f32[19,512]{1,0:T(8,128)S(1)}, f32[19,512]{1,0:T(8,128)S(1)}, u32[]{:S(2)}, u32[]{:S(2)}) collective-permute-start(f32[19,512]{1,0:T(8,128)S(1)} %rows_kernel.1.refs_8_.refs_2_), channel_id=1, source_target_pairs={{2,0},{3,1},{0,2},{1,3},{6,4},{7,5},{4,6},{5,7},{10,8},{11,9},{8,1... | collective-permute-start | bytes 116744 | tf_op jit(solution)/shard_map/ppermute | solution.py:354
  34.2 5.6 %collective-permute-start.7 = (f32[19,512]{1,0:T(8,128)S(1)}, f32[19,512]{1,0:T(8,128)S(1)}, u32[]{:S(2)}, u32[]{:S(2)}) collective-permute-start(f32[19,512]{1,0:T(8,128)S(1)} %rows_kernel.1.refs_8_.refs_2_), channel_id=1, source_target_pairs={{4,0},{5,1},{6,2},{7,3},{0,4},{1,5},{2,6},{3,7},{12,8},{13,9},{14,... | collective-permute-start | bytes 116744 | tf_op jit(solution)/shard_map/ppermute | solution.py:354
  36.9 5.3 %collective-permute-start.8 = (f32[19,512]{1,0:T(8,128)S(1)}, f32[19,512]{1,0:T(8,128)S(1)}, u32[]{:S(2)}, u32[]{:S(2)}) collective-permute-start(f32[19,512]{1,0:T(8,128)S(1)} %rows_kernel.1.refs_8_.refs_2_), channel_id=1, source_target_pairs={{6,0},{7,1},{4,2},{5,3},{2,4},{3,5},{0,6},{1,7},{14,8},{15,9},{12,... | collective-permute-start | bytes 116744 | tf_op jit(solution)/shard_map/ppermute | solution.py:354
  38.6 11.2 %collective-permute-start.12 = (bf16[528,512]{1,0:T(8,128)(2,1)S(1)}, bf16[528,512]{1,0:T(8,128)(2,1)S(1)}, u32[]{:S(2)}, u32[]{:S(2)}) collective-permute-start(bf16[528,512]{1,0:T(8,128)(2,1)S(1)} %west_kernel.1.refs_7_), channel_id=1, source_target_pairs={{0,7},{1,0},{2,1},{3,2},{4,3},{5,4},{6,5},{7,6},{8,15},{9,8},{10,9... | collective-permute-start | bytes 1622024 | tf_op jit(solution)/shard_map/ppermute | solution.py:350
  42.5 7.1 %collective-permute-start.9 = (f32[16,512]{1,0:T(8,128)S(1)}, f32[16,512]{1,0:T(8,128)S(1)}, u32[]{:S(2)}, u32[]{:S(2)}) collective-permute-start(f32[16,512]{1,0:T(8,128)S(1)} %get-tuple-element.36), channel_id=1, source_target_pairs={{32,0},{40,8},{48,16},{56,24},{0,32},{8,40},{16,48},{24,56},{96,64... | collective-permute-start | bytes 98312 | tf_op jit(solution)/shard_map/ppermute | solution.py:354
  42.5 7.1 %collective-permute-start.10 = (f32[16,512]{1,0:T(8,128)S(1)}, f32[16,512]{1,0:T(8,128)S(1)}, u32[]{:S(2)}, u32[]{:S(2)}) collective-permute-start(f32[16,512]{1,0:T(8,128)S(1)} %get-tuple-element.37), channel_id=1, source_target_pairs={{64,0},{72,8},{80,16},{88,24},{96,32},{104,40},{112,48},{120,56},{... | collective-permute-start | bytes 98312 | tf_op jit(solution)/shard_map/ppermute | solution.py:354
  44.7 5.1 %collective-permute-start.11 = (f32[16,512]{1,0:T(8,128)S(1)}, f32[16,512]{1,0:T(8,128)S(1)}, u32[]{:S(2)}, u32[]{:S(2)}) collective-permute-start(f32[16,512]{1,0:T(8,128)S(1)} %get-tuple-element.38), channel_id=1, source_target_pairs={{96,0},{104,8},{112,16},{120,24},{64,32},{72,40},{80,48},{88,56},{... | collective-permute-start | bytes 98312 | tf_op jit(solution)/shard_map/ppermute | solution.py:354

commit v3 on v2

--- a/solution.py
+++ b/solution.py
@@ -198,24 +198,30 @@
         h[at] = mm(block[at, : 2 * FACE], own[...])
 
 
-def corner_kernel(q, k, west, south, out):
-    out[...] = q[...] + folded(mm(k[:, :FACE], west[...]) + mm(k[:, FACE:], south[...]))
-
-
-def tail(basis, keep):
-    return (jnp.concatenate([basis.astype(F32), jnp.zeros((12, FACE), F32)], axis=0) * keep).astype(BF16)
-
-
-def inner_kernel(coup, p, west, south, t):
+def west_terms_kernel(coup, block, p, h, q, k, west, p_out, h_out, q_out):
+    own_n, with_west = 2 * FACE, 3 * FACE
+    for c in range(2):
+        at = slice(512 * c, 512 * c + 512)
+        p_out[at] = p[at] - mm(coup[at, own_n:with_west], west[...])
+    for c in range(4):
+        at = slice(512 * c, 512 * c + 512)
+        h_out[at] = h[at] + mm(block[at, own_n:with_west], west[...])
+    q_out[...] = q[...] + folded(mm(k[:, :FACE], west[...]))
+
+
+def corner_kernel(q, k, south, out):
+    out[...] = q[...] + folded(mm(k[:, FACE:], south[...]))
+
+
+def inner_kernel(coup, p, south, t):
     for c in range(2):
         at = slice(c * 512, (c + 1) * 512)
-        t[at] = (p[at] - (mm(coup[at, 2 * FACE : 3 * FACE], west[...]) + mm(coup[at, 3 * FACE :], south[...]))).astype(BF16)
-
-
-def result(f, coup, block, h, ub, west, south):
+        t[at] = (p[at] - mm(coup[at, 3 * FACE :], south[...])).astype(BF16)
+
+
+def result(f, coup, block, h, ub, south):
     at = slice(f * FACE, (f + 1) * FACE)
-    own_n = 2 * FACE
-    return h[at] + mm(block[at, own_n : 3 * FACE], west[...]) + mm(block[at, 3 * FACE :], south[...]) + mm_tn(coup[:, at], ub[...])
+    return h[at] + mm(block[at, 3 * FACE :], south[...]) + mm_tn(coup[:, at], ub[...])
 
 
 def tail(basis, f, keep):
@@ -223,7 +229,7 @@
     return (jnp.concatenate([rows, jnp.zeros((12, FACE), F32)], axis=0) * keep).astype(BF16)
 
 
-def solve_kernel(pos, coup, inv, block, t, h, west, south, basis, x_h, sent, ub, xbuf, sem):
+def solve_kernel(pos, coup, inv, block, t, h, south, basis, x_h, sent, ub, xbuf, sem):
     rows = 512
     copies = []
     for c in range(2):
@@ -234,21 +240,21 @@
         copies.append(pltpu.make_async_copy(xbuf.at[pl.ds(c * rows, rows)], x_h.at[pl.ds(c * rows, rows)], sem.at[c]))
         copies[c].start()
     keep = (pos[0] > 0).astype(F32)
-    sent[:FACE] = (result(3, coup, block, h, ub, west, south) * keep).astype(BF16)
+    sent[:FACE] = (result(3, coup, block, h, ub, south) * keep).astype(BF16)
     sent[FACE:] = tail(basis, 3, keep)
     for copy in copies:
         copy.wait()
 
 
-def west_kernel(pos, coup, block, h, ub, west, south, basis, sent):
+def west_kernel(pos, coup, block, h, ub, south, basis, sent):
     keep = (pos[0] > 0).astype(F32)
-    sent[:FACE] = (result(2, coup, block, h, ub, west, south) * keep).astype(BF16)
+    sent[:FACE] = (result(2, coup, block, h, ub, south) * keep).astype(BF16)
     sent[FACE:] = tail(basis, 2, keep)
 
 
-def kept_kernel(coup, block, h, ub, west, south, kept):
+def kept_kernel(coup, block, h, ub, south, kept):
     for f in range(2):
-        kept[f * FACE : (f + 1) * FACE] = result(f, coup, block, h, ub, west, south)
+        kept[f * FACE : (f + 1) * FACE] = result(f, coup, block, h, ub, south)
 
 
 def pair_kernel(pos, mine, theirs, out):
@@ -304,7 +310,7 @@
 
 
 def final_kernel(pos, b0, b1, b2, b3, kept, from_east, from_north, w, basis, z, cur, slots, zbuf, sem):
-    placed(lax.div(pos[0], 4), (b0, b1, b2, b3), slots)
+    placed(lax.div(pos[0], 4), (b0, b3, b2, b1), slots)
     cur[...] = summed(slots, 12) / FACE
     cc = (slots[0] + slots[1]) + (slots[2] + slots[3])
     copies = []
@@ -355,7 +361,8 @@
 
 
 def four(x, axis, stride):
-    return [x] + [exchanged(x, axis, stride, k) for k in (1, 2, 3)]
+    far, middle, near = [exchanged(x, axis, stride, k) for k in (3, 2, 1)]
+    return [x, near, middle, far]
 
 
 def local(
@@ -400,27 +407,35 @@
         cost=10,
     )(bt, block, own, k, q)
 
-    sums = call(corner_kernel, shape(8, F32), [VMEM] * 4, VMEM)(q, k, west, south)
+    p, h, q = call(
+        west_terms_kernel,
+        (shape(INTERIOR, F32), shape(4 * FACE, F32), shape(8, F32)),
+        [VMEM] * 7,
+        (VMEM,) * 3,
+        cost=2,
+    )(coup, block, p, h, q, k, west)
+
+    sums = call(corner_kernel, shape(8, F32), [VMEM] * 3, VMEM)(q, k, south)
     other = lax.ppermute(sums, "col", [(s, s ^ 1) for s in range(COLS)])
-    t = call(inner_kernel, shape(INTERIOR, BF16), [VMEM] * 4, VMEM, after=(sums,), cost=1)(coup, p, west, south)
+    t = call(inner_kernel, shape(INTERIOR, BF16), [VMEM] * 3, VMEM, after=(sums,), cost=1)(coup, p, south)
     sums = call(pair_kernel, shape(10, F32), [SMEM, VMEM, VMEM], VMEM, after=(t,))(j, sums, other)
     blocks = four(sums, "row", 1)
     x, to_south, ub = call(
         solve_kernel,
         (shape(INTERIOR, F32), shape(SENT, BF16), shape(INTERIOR, BF16)),
-        [SMEM] + [VMEM] * 8,
+        [SMEM] + [VMEM] * 7,
         (ANY, VMEM, VMEM),
         [pltpu.VMEM((INTERIOR, RHS), F32), pltpu.SemaphoreType.DMA((2,))],
         after=(sums,),
         cost=4,
-    )(i, coup, inv, block, t, h, west, south, basis)
+    )(i, coup, inv, block, t, h, south, basis)
     from_north = along(to_south, "row", -1)
     sums = call(
         rows_kernel, shape(19, F32), [SMEM] + [VMEM] * 4, VMEM, [pltpu.VMEM((4, 10, RHS), F32)], after=(to_south,)
     )(i, *blocks)
     blocks = four(sums, "col", 2)
-    to_west = call(west_kernel, shape(SENT, BF16), [SMEM] + [VMEM] * 7, VMEM, after=(sums,), cost=1)(
-        j, coup, block, h, ub, west, south, basis
+    to_west = call(west_kernel, shape(SENT, BF16), [SMEM] + [VMEM] * 6, VMEM, after=(sums,), cost=1)(
+        j, coup, block, h, ub, south, basis
     )
     from_east = along(to_west, "col", -1)
     shares = call(
@@ -431,10 +446,11 @@
         [pltpu.VMEM((4, 19, RHS), F32), pltpu.VMEM((48, RHS), F32), pltpu.VMEM((4, 16, RHS), F32)],
         after=(to_west,),
     )(i, j, *blocks, e)
-    kept = call(kept_kernel, shape(2 * FACE, F32), [VMEM] * 6, VMEM, after=(shares[0],), cost=30)(
-        coup, block, h, ub, west, south
+    kept = call(kept_kernel, shape(2 * FACE, F32), [VMEM] * 5, VMEM, after=(shares[0],), cost=30)(
+        coup, block, h, ub, south
     )
-    blocks = [shares[0]] + [exchanged(shares[k], "row", 4, k) for k in (1, 2, 3)]
+    far, middle, near = [exchanged(shares[k], "row", 4, k) for k in (3, 2, 1)]
+    blocks = [shares[0], far, middle, near]
     z, currents = final(i, blocks, kept, from_east, from_north, w, basis)
     return x[None, None], z[None, None], currents
 

time: 52.7 us -> 49.7 us (0.943)
  starting transfers between devices: 19.1 us -> 17.2 us
  waiting for transfers between devices: 8.12 us -> 7 us
    ppermute x4, waiting for transfers between devices: 5.2 us -> 3.42 us  [along(): return lax.ppermute(x, axis, [(s, (s + d) % n) for s in range(n)])]
    ppermute x9, starting transfers between devices: 14.3 us -> 12.7 us  [exchanged(): lax.ppermute(x, axis, [(d ^ k * stride, d) for d in range(lax.axis_size(a...]
    pallas_call x15 -> x16, Pallas kernels: 21.5 us -> 21.7 us  [made(): result = run(*args, *extra)]
  transfers between devices with their start and end apart: 14 -> 14, of which waited for: 4 -> 5; matrix products, arithmetic and copies ran while one was open for 0% -> 0% of each run, Pallas kernels for 33% -> 35%
where the time goes in v3:
time: 49.7 us; the launch traced here: 49.5 us
  Pallas kernels  21.7 us (44%)
  starting transfers between devices  17.2 us (35%)
  waiting for transfers between devices  7 us (14%)
  local copies, waits for them, and re-layouts  2.71 us (5%)
  between operations  1 us (2%)
    pallas_call x16, Pallas kernels, made(): result = run(*args, *extra)  21.7 us
    ppermute x9, starting transfers between devices, exchanged(): lax.ppermute(x, axis, [(d ^ k * stride, d) for d in range(lax.axis_size(a...  12.7 us
    ppermute x4, starting transfers between devices, along(): return lax.ppermute(x, axis, [(s, (s + d) % n) for s in range(n)])  4.47 us
    ppermute x4, waiting for transfers between devices, along(): return lax.ppermute(x, axis, [(s, (s + d) % n) for s in range(n)])  3.42 us
    ppermute x9, waiting for transfers between devices, exchanged(): lax.ppermute(x, axis, [(d ^ k * stride, d) for d in range(lax.axis_size(a...  3.11 us
    unnamed x24, local copies, waits for them, and re-layouts  2.71 us
  transfers between devices with their start and end apart: 14, of which 5 were waited for; matrix products, arithmetic and copies ran while one was open for 0% of the time, Pallas kernels for 35%

profile of v3, /device:TPU:0, one launch (start us, length us, event | category | flops | bytes accessed | tf_op | source)
XLA Modules:
  0.0 49.5 jit_solution(17295111970160007595)
XLA Ops:
  0.6 0.7 %copy-done.5 = f32[1,1,2,512]{3,2,1,0:T(2,128)S(1)} copy-done((f32[1,1,2,512]{3,2,1,0:T(2,128)S(1)}, f32[1,1,2,512]{3,2,1,0:T(2,128)}, u32[]{:S(2)}) %copy-start.5) | copy-done | bytes 4120
  1.3 1.5 %north_kernel.1.refs_3_ = bf16[512,512]{1,0:T(8,128)(2,1)S(1)} custom-call(s32[1]{0:T(128)} %bitcast.refs_0_, f32[2,512,512]{2,1,0:T(8,128)} %bitcast.40, f32[2,512]{1,0:T(2,128)S(1)} %bitcast.37), custom_call_target="tpu_custom_call" | custom-call | flops 4000001024 | bytes 12001000 | tf_op jit(solution)/shard_map/north_kernel/pallas_call | solution.py:80
  2.8 2.1 %collective-permute-start.1 = (bf16[512,512]{1,0:T(8,128)(2,1)S(1)}, bf16[512,512]{1,0:T(8,128)(2,1)S(1)}, u32[]{:S(2)}, u32[]{:S(2)}) collective-permute-start(bf16[512,512]{1,0:T(8,128)(2,1)S(1)} %north_kernel.1.refs_3_), channel_id=1, source_target_pairs={{0,8},{8,16},{16,24},{24,32},{32,40},{40,48},{48,56},{56,64},{64,7... | collective-permute-start | bytes 1572872 | tf_op jit(solution)/shard_map/ppermute | solution.py:356
  4.9 0.0 copy-start
  4.9 0.0 copy-start.3
  4.9 0.0 copy-start.8
  4.9 0.0 copy-start.9
  5.0 0.5 east_kernel.1
  5.4 0.0 collective-permute-start
  5.5 0.4 copy-done.2
  5.8 1.3 %table_kernel.1.refs_5_.refs_6_ = f32[64,48]{1,0:T(8,128)S(1)} custom-call(s32[1]{0:T(128)} %bitcast.refs_0_, s32[1]{0:T(128)} %bitcast.5.refs_0_.refs_1_, s32[32,16]{1,0:T(8,128)S(1)} %bitcast.35, s32[32,16]{1,0:T(8,128)S(1)} %bitcast.36, f32[153,153]{1,0:T(8,128)S(1)} %copy-done.2, bf16[1024,512]{1,0:T(8,128)(2,1)S(1)} %get-tuple-element.25.refs_5_.refs_2_), custom_call_target="tpu_custom_call" | custom-call | flops 1000 | bytes 1000 | tf_op jit(solution)/shard_map/table_kernel/pallas_call | solution.py:80
  7.2 0.0 copy-done
  7.2 0.7 %copy-done.8 = f32[1,1,1024,512]{3,2,1,0:T(8,128)S(1)} copy-done((f32[1,1,1024,512]{3,2,1,0:T(8,128)S(1)}, f32[1,1,1024,512]{3,2,1,0:T(8,128)}, u32[]{:S(2)}) %copy-start.8) | copy-done | bytes 2097176
  7.9 2.3 %early_a_kernel.1 = (f32[1024,512]{1,0:T(8,128)S(1)}, f32[8,1024]{1,0:T(8,128)S(1)}, bf16[8,2048]{1,0:T(8,128)(2,1)S(1)}) custom-call(bf16[1024,2048]{1,0:T(8,128)(2,1)S(1)} %bitcast.22, f32[1024,512]{1,0:T(8,128)S(1)} %bitcast.42, bf16[1024,512]{1,0:T(8,128)(2,1)S(1)} %get-tuple-element.25.refs_5_.refs_2_, bf16[4,2048]{1,0:T(4,128)(2,1)S(1)} %bitcast.31, ...), custom_call_target="tpu_custom_call" | custom-call | flops 10000001024 | bytes 30001000 | tf_op jit(solution)/shard_map/early_a_kernel/pallas_call | solution.py:80
  10.2 0.0 slice-start.1
  10.3 1.4 %early_b_kernel.1 = (f32[8,2048]{1,0:T(8,128)S(1)}, f32[8,512]{1,0:T(8,128)S(1)}) custom-call(f32[8,1024]{1,0:T(8,128)S(1)} %get-tuple-element.28.refs_0_, bf16[1024,1024]{1,0:T(8,128)(2,1)S(1)} %bitcast.29, bf16[1024,2048]{1,0:T(8,128)(2,1)S(1)} %bitcast.23, f32[1024,512]{1,0:T(8,128)S(1)} %bitcast.43), custom_call_target="tpu_custom_call" | custom-call | flops 10000001024 | bytes 30001000 | tf_op jit(solution)/shard_map/early_b_kernel/pallas_call | solution.py:80
  11.6 0.9 %slice-done.1 = s8[4194304]{0:T(1024)(128)(4,1)S(1)} async-done(((s8[8388608]{0:T(1024)(128)(4,1)}), s8[4194304]{0:T(1024)(128)(4,1)S(1)}, s32[]{:S(2)}) %slice-start.1) | async-done | bytes 4194328
  12.6 3.6 %early_c_kernel.1 = (f32[2048,512]{1,0:T(8,128)S(1)}, f32[8,512]{1,0:T(8,128)S(1)}, bf16[16,1024]{1,0:T(8,128)(2,1)S(1)}) custom-call(bf16[8,2048]{1,0:T(8,128)(2,1)S(1)} %get-tuple-element.27.refs_0_, bf16[2048,2048]{1,0:T(8,128)(2,1)S(1)} %bitcast.17, bf16[1024,512]{1,0:T(8,128)(2,1)S(1)} %get-tuple-element.25.refs_5_.refs_2_, ...), custom_call_target="tpu_custom_call" | custom-call | flops 10000001024 | bytes 30001000 | tf_op jit(solution)/shard_map/early_c_kernel/pallas_call | solution.py:80
  16.1 0.0 collective-permute-done.refs_6_
  16.1 1.8 %west_terms_kernel.1 = (f32[1024,512]{1,0:T(8,128)S(1)}, f32[2048,512]{1,0:T(8,128)S(1)}, f32[8,512]{1,0:T(8,128)S(1)}) custom-call(bf16[1024,2048]{1,0:T(8,128)(2,1)S(1)} %bitcast.24, bf16[2048,2048]{1,0:T(8,128)(2,1)S(1)} %bitcast.18, f32[1024,512]{1,0:T(8,128)S(1)} %get-tuple-element.26.refs_2_, f32[2048,512]{1,0:T(8,128)S(1)} %get-tuple-element.31.refs_3_, ...), custom_call_target="tpu_custom_call" | custom-call | flops 2000001024 | bytes 6001000 | tf_op jit(solution)/shard_map/west_terms_kernel/pallas_call | solution.py:80
  18.0 3.4 %collective-permute-done.1.refs_2_.refs_6_.refs_5_.refs_4_ = bf16[512,512]{1,0:T(8,128)(2,1)S(1)} collective-permute-done((bf16[512,512]{1,0:T(8,128)(2,1)S(1)}, bf16[512,512]{1,0:T(8,128)(2,1)S(1)}, u32[]{:S(2)}, u32[]{:S(2)}) %collective-permute-start.1) | collective-permute-done | bytes 524320 | tf_op jit(solution)/shard_map/ppermute | solution.py:356
  21.4 0.2 corner_kernel.1.refs_3_.refs_1_
  21.6 0.0 collective-permute-start.2
  21.6 0.7 %inner_kernel.1.refs_3_.refs_4_ = bf16[1024,512]{1,0:T(8,128)(2,1)S(1)} custom-call(bf16[1024,2048]{1,0:T(8,128)(2,1)S(1)} %bitcast.25, f32[1024,512]{1,0:T(8,128)S(1)} %get-tuple-element.35.refs_1_, bf16[512,512]{1,0:T(8,128)(2,1)S(1)} %collective-permute-done.1.refs_2_.refs_6_.refs_5_.refs_4_, f32[8,512]{1,0:T(8,128)S(1)} %corner_kernel.1.refs_3_.refs_1_), custom_call_target="tpu_custom_call" | custom-call | flops 1000001024 | bytes 3001000 | tf_op jit(solution)/shard_map/inner_kernel/pallas_call | solution.py:80
  22.3 0.5 collective-permute-done.2.refs_2_
  22.8 0.1 collective-permute-start.5
  22.9 0.8 %collective-permute-start.4 = (f32[10,512]{1,0:T(8,128)S(1)}, f32[10,512]{1,0:T(8,128)S(1)}, u32[]{:S(2)}, u32[]{:S(2)}) collective-permute-start(f32[10,512]{1,0:T(8,128)S(1)} %pair_kernel.1.refs_8_.refs_1_), channel_id=1, source_target_pairs={{16,0},{24,8},{0,16},{8,24},{48,32},{56,40},{32,48},{40,56},{80,64... | collective-permute-start | bytes 61448 | tf_op jit(solution)/shard_map/ppermute | solution.py:360
  23.7 3.3 %collective-permute-start.3 = (f32[10,512]{1,0:T(8,128)S(1)}, f32[10,512]{1,0:T(8,128)S(1)}, u32[]{:S(2)}, u32[]{:S(2)}) collective-permute-start(f32[10,512]{1,0:T(8,128)S(1)} %pair_kernel.1.refs_8_.refs_1_), channel_id=1, source_target_pairs={{8,0},{0,8},{24,16},{16,24},{40,32},{32,40},{56,48},{48,56},{72,64... | collective-permute-start | bytes 61448 | tf_op jit(solution)/shard_map/ppermute | solution.py:360
  27.0 2.8 %solve_kernel.1 = (f32[1024,512]{1,0:T(8,128)}, bf16[528,512]{1,0:T(8,128)(2,1)S(1)}, bf16[1024,512]{1,0:T(8,128)(2,1)S(1)}) custom-call(s32[1]{0:T(128)} %bitcast.refs_0_, bf16[1024,2048]{1,0:T(8,128)(2,1)S(1)} %bitcast.26, bf16[1024,1024]{1,0:T(8,128)(2,1)S(1)} %bitcast.30, bf16[2048,2048]{1,0:T(8,128)(2,1)S(1)} %bitcast.19, ...), custom_call_target="tpu_custom_call" | custom-call | flops 4000001024 | bytes 12001000 | tf_op jit(solution)/shard_map/solve_kernel/pallas_call | solution.py:80
  29.7 1.8 %collective-permute-start.13 = (bf16[528,512]{1,0:T(8,128)(2,1)S(1)}, bf16[528,512]{1,0:T(8,128)(2,1)S(1)}, u32[]{:S(2)}, u32[]{:S(2)}) collective-permute-start(bf16[528,512]{1,0:T(8,128)(2,1)S(1)} %get-tuple-element.39.refs_5_), channel_id=1, source_target_pairs={{0,120},{8,0},{16,8},{24,16},{32,24},{40,32},{48,40},{56,48},{64,5... | collective-permute-start | bytes 1622024 | tf_op jit(solution)/shard_map/ppermute | solution.py:356
  31.6 0.0 collective-permute-done.5.refs_4_
  31.6 3.0 %collective-permute-start.8 = (f32[19,512]{1,0:T(8,128)S(1)}, f32[19,512]{1,0:T(8,128)S(1)}, u32[]{:S(2)}, u32[]{:S(2)}) collective-permute-start(f32[19,512]{1,0:T(8,128)S(1)} %rows_kernel.1.refs_7_.refs_2_), channel_id=1, source_target_pairs={{6,0},{7,1},{4,2},{5,3},{2,4},{3,5},{0,6},{1,7},{14,8},{15,9},{12,... | collective-permute-start | bytes 116744 | tf_op jit(solution)/shard_map/ppermute | solution.py:360
  34.6 0.8 %collective-permute-start.7 = (f32[19,512]{1,0:T(8,128)S(1)}, f32[19,512]{1,0:T(8,128)S(1)}, u32[]{:S(2)}, u32[]{:S(2)}) collective-permute-start(f32[19,512]{1,0:T(8,128)S(1)} %rows_kernel.1.refs_7_.refs_2_), channel_id=1, source_target_pairs={{4,0},{5,1},{6,2},{7,3},{0,4},{1,5},{2,6},{3,7},{12,8},{13,9},{14,... | collective-permute-start | bytes 116744 | tf_op jit(solution)/shard_map/ppermute | solution.py:360
  35.4 0.5 %collective-permute-start.6 = (f32[19,512]{1,0:T(8,128)S(1)}, f32[19,512]{1,0:T(8,128)S(1)}, u32[]{:S(2)}, u32[]{:S(2)}) collective-permute-start(f32[19,512]{1,0:T(8,128)S(1)} %rows_kernel.1.refs_7_.refs_2_), channel_id=1, source_target_pairs={{2,0},{3,1},{0,2},{1,3},{6,4},{7,5},{4,6},{5,7},{10,8},{11,9},{8,1... | collective-permute-start | bytes 116744 | tf_op jit(solution)/shard_map/ppermute | solution.py:360
  36.0 1.0 %west_kernel.1.refs_7_ = bf16[528,512]{1,0:T(8,128)(2,1)S(1)} custom-call(s32[1]{0:T(128)} %bitcast.5.refs_0_.refs_1_, bf16[1024,2048]{1,0:T(8,128)(2,1)S(1)} %bitcast.27, bf16[2048,2048]{1,0:T(8,128)(2,1)S(1)} %bitcast.20, f32[2048,512]{1,0:T(8,128)S(1)} %get-tuple-element.37.refs_5_.refs_3_.refs_2_, ...), custom_call_target="tpu_custom_call" | custom-call | flops 1000001024 | bytes 3001000 | tf_op jit(solution)/shard_map/west_kernel/pallas_call | solution.py:80
  37.0 0.6 %collective-permute-start.12 = (bf16[528,512]{1,0:T(8,128)(2,1)S(1)}, bf16[528,512]{1,0:T(8,128)(2,1)S(1)}, u32[]{:S(2)}, u32[]{:S(2)}) collective-permute-start(bf16[528,512]{1,0:T(8,128)(2,1)S(1)} %west_kernel.1.refs_7_), channel_id=1, source_target_pairs={{0,7},{1,0},{2,1},{3,2},{4,3},{5,4},{6,5},{7,6},{8,15},{9,8},{10,9... | collective-permute-start | bytes 1622024 | tf_op jit(solution)/shard_map/ppermute | solution.py:356
  37.5 0.0 collective-permute-done.8.refs_5_
  37.5 2.7 %collective-permute-done.7.refs_4_ = f32[19,512]{1,0:T(8,128)S(1)} collective-permute-done((f32[19,512]{1,0:T(8,128)S(1)}, f32[19,512]{1,0:T(8,128)S(1)}, u32[]{:S(2)}, u32[]{:S(2)}) %collective-permute-start.7) | collective-permute-done | bytes 38944 | tf_op jit(solution)/shard_map/ppermute | solution.py:360
  40.2 0.2 columns_kernel.1
  40.5 0.8 %collective-permute-start.9 = (f32[16,512]{1,0:T(8,128)S(1)}, f32[16,512]{1,0:T(8,128)S(1)}, u32[]{:S(2)}, u32[]{:S(2)}) collective-permute-start(f32[16,512]{1,0:T(8,128)S(1)} %get-tuple-element.42), channel_id=1, source_target_pairs={{96,0},{104,8},{112,16},{120,24},{64,32},{72,40},{80,48},{88,56},{... | collective-permute-start | bytes 98312 | tf_op jit(solution)/shard_map/ppermute | solution.py:360
  41.3 1.1 %collective-permute-start.10 = (f32[16,512]{1,0:T(8,128)S(1)}, f32[16,512]{1,0:T(8,128)S(1)}, u32[]{:S(2)}, u32[]{:S(2)}) collective-permute-start(f32[16,512]{1,0:T(8,128)S(1)} %get-tuple-element.43), channel_id=1, source_target_pairs={{64,0},{72,8},{80,16},{88,24},{96,32},{104,40},{112,48},{120,56},{... | collective-permute-start | bytes 98312 | tf_op jit(solution)/shard_map/ppermute | solution.py:360
  42.4 2.2 %collective-permute-start.11 = (f32[16,512]{1,0:T(8,128)S(1)}, f32[16,512]{1,0:T(8,128)S(1)}, u32[]{:S(2)}, u32[]{:S(2)}) collective-permute-start(f32[16,512]{1,0:T(8,128)S(1)} %get-tuple-element.44), channel_id=1, source_target_pairs={{32,0},{40,8},{48,16},{56,24},{0,32},{8,40},{16,48},{24,56},{96,64... | collective-permute-start | bytes 98312 | tf_op jit(solution)/shard_map/ppermute | solution.py:360
  44.7 1.8 %kept_kernel.1.refs_5_ = f32[1024,512]{1,0:T(8,128)S(1)} custom-call(bf16[1024,2048]{1,0:T(8,128)(2,1)S(1)} %bitcast.28, bf16[2048,2048]{1,0:T(8,128)(2,1)S(1)} %bitcast.21, f32[2048,512]{1,0:T(8,128)S(1)} %get-tuple-element.37.refs_5_.refs_3_.refs_2_, bf16[1024,512]{1,0:T(8,128)(2,1)S(1)} %get-tuple-element.40.refs_4_.refs_3_, ...), custom_call_target="tpu_custom_call" | custom-call | flops 30000001024 | bytes 90001000 | tf_op jit(solution)/shard_map/kept_kernel/pallas_call | solution.py:80
  46.5 0.0 collective-permute-done.9.refs_2_
  46.5 0.2 collective-permute-done.10.refs_3_
  46.7 0.2 collective-permute-done.11.refs_4_
  46.9 0.0 collective-permute-done.13.refs_7_
  46.9 2.5 %final_kernel.1 = (f32[2,512,512]{2,1,0:T(8,128)}, f32[4,512]{1,0:T(4,128)}) custom-call(s32[1]{0:T(128)} %bitcast.refs_0_, f32[16,512]{1,0:T(8,128)S(1)} %get-tuple-element.41.refs_5_.refs_1_, f32[16,512]{1,0:T(8,128)S(1)} %collective-permute-done.9.refs_2_, f32[16,512]{1,0:T(8,128)S(1)} %collective-permute-done.10.refs_3_, ...), custom_call_target="tpu_custom_call" | custom-call | flops 1000 | bytes 1000 | tf_op jit(solution)/shard_map/final_kernel/pallas_call | solution.py:80
  (21 shorter events, 0.1 us)
Async XLA Ops:
  0.6 0.7 %copy-start.5 = (f32[1,1,2,512]{3,2,1,0:T(2,128)S(1)}, f32[1,1,2,512]{3,2,1,0:T(2,128)}, u32[]{:S(2)}) copy-start(f32[1,1,2,512]{3,2,1,0:T(2,128)} %param.12) | copy-start | bytes 12292
  1.3 3.6 %copy-start.6 = (f32[1,1,2,512]{3,2,1,0:T(2,128)S(1)}, f32[1,1,2,512]{3,2,1,0:T(2,128)}, u32[]{:S(2)}) copy-start(f32[1,1,2,512]{3,2,1,0:T(2,128)} %param.12) | copy-start | bytes 12292
  1.3 3.6 %copy-start.7 = (f32[1,1,2,512,512]{4,3,2,1,0:T(8,128)S(1)}, f32[1,1,2,512,512]{4,3,2,1,0:T(8,128)}, u32[]{:S(2)}) copy-start(f32[1,1,2,512,512]{4,3,2,1,0:T(8,128)} %param.11) | copy-start | bytes 6291460
  2.8 18.6 %collective-permute-start.1 = (bf16[512,512]{1,0:T(8,128)(2,1)S(1)}, bf16[512,512]{1,0:T(8,128)(2,1)S(1)}, u32[]{:S(2)}, u32[]{:S(2)}) collective-permute-start(bf16[512,512]{1,0:T(8,128)(2,1)S(1)} %north_kernel.1.refs_3_), channel_id=1, source_target_pairs={{0,8},{8,16},{16,24},{24,32},{32,40},{40,48},{48,56},{56,64},{64,7... | collective-permute-start | bytes 1572872 | tf_op jit(solution)/shard_map/ppermute | solution.py:356
  4.9 0.9 %copy-start.2 = (f32[153,153]{1,0:T(8,128)S(1)}, f32[153,153]{1,0:T(8,128)}, u32[]{:S(2)}) copy-start(f32[153,153]{1,0:T(8,128)} %refs_4_.1) | copy-start | bytes 280912
  4.9 0.9 %copy-start.4 = (s32[16,8,4]{0,2,1:T(4,128)S(1)}, s32[16,8,4]{0,2,1:T(4,128)}, u32[]{:S(2)}) copy-start(s32[16,8,4]{0,2,1:T(4,128)} %param.18) | copy-start | bytes 6148
  4.9 2.3 %copy-start = (bf16[1,1,1024,2048]{3,2,1,0:T(8,128)(2,1)S(1)}, bf16[1,1,1024,2048]{3,2,1,0:T(8,128)(2,1)}, u32[]{:S(2)}) copy-start(bf16[1,1,1024,2048]{3,2,1,0:T(8,128)(2,1)} %param.14) | copy-start | bytes 12582916
  4.9 2.3 %copy-start.3 = (bf16[1,1,4,2048]{3,2,1,0:T(4,128)(2,1)S(1)}, bf16[1,1,4,2048]{3,2,1,0:T(4,128)(2,1)}, u32[]{:S(2)}) copy-start(bf16[1,1,4,2048]{3,2,1,0:T(4,128)(2,1)} %param.16) | copy-start | bytes 49156
  4.9 2.9 %copy-start.8 = (f32[1,1,1024,512]{3,2,1,0:T(8,128)S(1)}, f32[1,1,1024,512]{3,2,1,0:T(8,128)}, u32[]{:S(2)}) copy-start(f32[1,1,1024,512]{3,2,1,0:T(8,128)} %param.10) | copy-start | bytes 6291460
  4.9 2.9 %copy-start.9 = (s32[1,1,4,512]{3,2,1,0:T(4,128)S(1)}, s32[1,1,4,512]{3,2,1,0:T(4,128)}, u32[]{:S(2)}) copy-start(s32[1,1,4,512]{3,2,1,0:T(4,128)} %param.19) | copy-start | bytes 24580
  5.4 10.7 %collective-permute-start = (bf16[512,512]{1,0:T(8,128)(2,1)S(1)}, bf16[512,512]{1,0:T(8,128)(2,1)S(1)}, u32[]{:S(2)}, u32[]{:S(2)}) collective-permute-start(bf16[512,512]{1,0:T(8,128)(2,1)S(1)} %get-tuple-element.34), channel_id=1, source_target_pairs={{0,1},{1,2},{2,3},{3,4},{4,5},{5,6},{6,7},{7,0},{8,9},{9,10},{10,1... | collective-permute-start | bytes 1572872 | tf_op jit(solution)/shard_map/ppermute | solution.py:356
  7.9 2.4 %copy-start.1 = (bf16[1,1,1024,1024]{3,2,1,0:T(8,128)(2,1)S(1)}, bf16[1,1,1024,1024]{3,2,1,0:T(8,128)(2,1)}, u32[]{:S(2)}) copy-start(bf16[1,1,1024,1024]{3,2,1,0:T(8,128)(2,1)} %param.13) | copy-start | bytes 6291460
  7.9 3.7 %slice-start = ((s8[8388608]{0:T(1024)(128)(4,1)}), s8[4194304]{0:T(1024)(128)(4,1)S(1)}, s32[]{:S(2)}) async-start(s8[8388608]{0:T(1024)(128)(4,1)} %bitcast.15), calls=%async_computation | async-start | bytes 8388608
  10.2 2.3 %slice-start.1 = ((s8[8388608]{0:T(1024)(128)(4,1)}), s8[4194304]{0:T(1024)(128)(4,1)S(1)}, s32[]{:S(2)}) async-start(s8[8388608]{0:T(1024)(128)(4,1)} %bitcast.15), calls=%async_computation.1 | async-start | bytes 8388608
  21.6 1.2 %collective-permute-start.2 = (f32[8,512]{1,0:T(8,128)S(1)}, f32[8,512]{1,0:T(8,128)S(1)}, u32[]{:S(2)}, u32[]{:S(2)}) collective-permute-start(f32[8,512]{1,0:T(8,128)S(1)} %corner_kernel.1.refs_3_.refs_1_), channel_id=1, source_target_pairs={{0,1},{1,0},{2,3},{3,2},{4,5},{5,4},{6,7},{7,6},{8,9},{9,8},{10,11... | collective-permute-start | bytes 49160 | tf_op jit(solution)/shard_map/ppermute | solution.py:419
  22.8 8.8 %collective-permute-start.5 = (f32[10,512]{1,0:T(8,128)S(1)}, f32[10,512]{1,0:T(8,128)S(1)}, u32[]{:S(2)}, u32[]{:S(2)}) collective-permute-start(f32[10,512]{1,0:T(8,128)S(1)} %pair_kernel.1.refs_8_.refs_1_), channel_id=1, source_target_pairs={{24,0},{16,8},{8,16},{0,24},{56,32},{48,40},{40,48},{32,56},{88,64... | collective-permute-start | bytes 61448 | tf_op jit(solution)/shard_map/ppermute | solution.py:360
  22.9 8.7 %collective-permute-start.4 = (f32[10,512]{1,0:T(8,128)S(1)}, f32[10,512]{1,0:T(8,128)S(1)}, u32[]{:S(2)}, u32[]{:S(2)}) collective-permute-start(f32[10,512]{1,0:T(8,128)S(1)} %pair_kernel.1.refs_8_.refs_1_), channel_id=1, source_target_pairs={{16,0},{24,8},{0,16},{8,24},{48,32},{56,40},{32,48},{40,56},{80,64... | collective-permute-start | bytes 61448 | tf_op jit(solution)/shard_map/ppermute | solution.py:360
  23.7 7.9 %collective-permute-start.3 = (f32[10,512]{1,0:T(8,128)S(1)}, f32[10,512]{1,0:T(8,128)S(1)}, u32[]{:S(2)}, u32[]{:S(2)}) collective-permute-start(f32[10,512]{1,0:T(8,128)S(1)} %pair_kernel.1.refs_8_.refs_1_), channel_id=1, source_target_pairs={{8,0},{0,8},{24,16},{16,24},{40,32},{32,40},{56,48},{48,56},{72,64... | collective-permute-start | bytes 61448 | tf_op jit(solution)/shard_map/ppermute | solution.py:360
  29.7 17.2 %collective-permute-start.13 = (bf16[528,512]{1,0:T(8,128)(2,1)S(1)}, bf16[528,512]{1,0:T(8,128)(2,1)S(1)}, u32[]{:S(2)}, u32[]{:S(2)}) collective-permute-start(bf16[528,512]{1,0:T(8,128)(2,1)S(1)} %get-tuple-element.39.refs_5_), channel_id=1, source_target_pairs={{0,120},{8,0},{16,8},{24,16},{32,24},{40,32},{48,40},{56,48},{64,5... | collective-permute-start | bytes 1622024 | tf_op jit(solution)/shard_map/ppermute | solution.py:356
  31.6 5.9 %collective-permute-start.8 = (f32[19,512]{1,0:T(8,128)S(1)}, f32[19,512]{1,0:T(8,128)S(1)}, u32[]{:S(2)}, u32[]{:S(2)}) collective-permute-start(f32[19,512]{1,0:T(8,128)S(1)} %rows_kernel.1.refs_7_.refs_2_), channel_id=1, source_target_pairs={{6,0},{7,1},{4,2},{5,3},{2,4},{3,5},{0,6},{1,7},{14,8},{15,9},{12,... | collective-permute-start | bytes 116744 | tf_op jit(solution)/shard_map/ppermute | solution.py:360
  34.6 5.6 %collective-permute-start.7 = (f32[19,512]{1,0:T(8,128)S(1)}, f32[19,512]{1,0:T(8,128)S(1)}, u32[]{:S(2)}, u32[]{:S(2)}) collective-permute-start(f32[19,512]{1,0:T(8,128)S(1)} %rows_kernel.1.refs_7_.refs_2_), channel_id=1, source_target_pairs={{4,0},{5,1},{6,2},{7,3},{0,4},{1,5},{2,6},{3,7},{12,8},{13,9},{14,... | collective-permute-start | bytes 116744 | tf_op jit(solution)/shard_map/ppermute | solution.py:360
  35.4 4.8 %collective-permute-start.6 = (f32[19,512]{1,0:T(8,128)S(1)}, f32[19,512]{1,0:T(8,128)S(1)}, u32[]{:S(2)}, u32[]{:S(2)}) collective-permute-start(f32[19,512]{1,0:T(8,128)S(1)} %rows_kernel.1.refs_7_.refs_2_), channel_id=1, source_target_pairs={{2,0},{3,1},{0,2},{1,3},{6,4},{7,5},{4,6},{5,7},{10,8},{11,9},{8,1... | collective-permute-start | bytes 116744 | tf_op jit(solution)/shard_map/ppermute | solution.py:360
  37.0 9.9 %collective-permute-start.12 = (bf16[528,512]{1,0:T(8,128)(2,1)S(1)}, bf16[528,512]{1,0:T(8,128)(2,1)S(1)}, u32[]{:S(2)}, u32[]{:S(2)}) collective-permute-start(bf16[528,512]{1,0:T(8,128)(2,1)S(1)} %west_kernel.1.refs_7_), channel_id=1, source_target_pairs={{0,7},{1,0},{2,1},{3,2},{4,3},{5,4},{6,5},{7,6},{8,15},{9,8},{10,9... | collective-permute-start | bytes 1622024 | tf_op jit(solution)/shard_map/ppermute | solution.py:356
  40.5 6.0 %collective-permute-start.9 = (f32[16,512]{1,0:T(8,128)S(1)}, f32[16,512]{1,0:T(8,128)S(1)}, u32[]{:S(2)}, u32[]{:S(2)}) collective-permute-start(f32[16,512]{1,0:T(8,128)S(1)} %get-tuple-element.42), channel_id=1, source_target_pairs={{96,0},{104,8},{112,16},{120,24},{64,32},{72,40},{80,48},{88,56},{... | collective-permute-start | bytes 98312 | tf_op jit(solution)/shard_map/ppermute | solution.py:360
  41.3 5.4 %collective-permute-start.10 = (f32[16,512]{1,0:T(8,128)S(1)}, f32[16,512]{1,0:T(8,128)S(1)}, u32[]{:S(2)}, u32[]{:S(2)}) collective-permute-start(f32[16,512]{1,0:T(8,128)S(1)} %get-tuple-element.43), channel_id=1, source_target_pairs={{64,0},{72,8},{80,16},{88,24},{96,32},{104,40},{112,48},{120,56},{... | collective-permute-start | bytes 98312 | tf_op jit(solution)/shard_map/ppermute | solution.py:360
  42.4 4.5 %collective-permute-start.11 = (f32[16,512]{1,0:T(8,128)S(1)}, f32[16,512]{1,0:T(8,128)S(1)}, u32[]{:S(2)}, u32[]{:S(2)}) collective-permute-start(f32[16,512]{1,0:T(8,128)S(1)} %get-tuple-element.44), channel_id=1, source_target_pairs={{32,0},{40,8},{48,16},{56,24},{0,32},{8,40},{16,48},{24,56},{96,64... | collective-permute-start | bytes 98312 | tf_op jit(solution)/shard_map/ppermute | solution.py:360

commit v4 on v3

--- a/solution.py
+++ b/solution.py
@@ -47,22 +47,20 @@
     return jnp.transpose(jnp.broadcast_to(row, (8, row.shape[1])))[:, :1]
 
 
-def call(kernel, outs, in_specs, out_specs, scratch=(), after=(), through=None, vmem=16, cost=0):
+def call(kernel, outs, in_specs, out_specs, scratch=(), after=(), into=None, vmem=16, cost=0):
     n = len(in_specs)
     several = isinstance(outs, tuple)
     outs, out_specs = (outs, out_specs) if several else ((outs,), (out_specs,))
     extra = list(after)
     aliases = {}
-    if through is not None:
+    if into is not None:
         aliases = {n + len(extra): len(outs)}
-        extra.append(through)
-        outs = (*outs, jax.ShapeDtypeStruct(through.shape, through.dtype))
+        extra.append(into)
+        outs = (*outs, jax.ShapeDtypeStruct(into.shape, into.dtype))
         out_specs = (*out_specs, ANY)
-    m = len(outs) - len(aliases)
 
     def body(*refs):
-        rest = refs[n + len(extra) :]
-        kernel(*refs[:n], *rest[:m], *rest[len(outs) :])
+        kernel(*refs[:n], *refs[n + len(extra) :])
 
     run = pl.pallas_call(
         body,
@@ -87,35 +85,20 @@
     return jax.ShapeDtypeStruct((rows, columns), kind)
 
 
-def north_kernel(pos, faces, weights, out, face, w, sem):
-    parts, rows = 4, FACE // 4
-    get_w = pltpu.make_async_copy(weights, w, sem.at[parts])
-    get_w.start()
-    copies = [
-        pltpu.make_async_copy(faces.at[1, pl.ds(c * rows, rows)], face.at[pl.ds(c * rows, rows)], sem.at[c])
-        for c in range(parts)
-    ]
-    for copy in copies:
-        copy.start()
-    get_w.wait()
+def load_kernel(faces, face, sem):
+    copy = pltpu.make_async_copy(faces.at[1], face, sem)
+    copy.start()
+    copy.wait()
+
+
+def north_kernel(pos, face, w, out):
     keep = (pos[0] < ROWS - 1).astype(F32)
-    scale = (1.0 - column(w[1:2, :])) * keep
-    for c, copy in enumerate(copies):
-        copy.wait()
-        at = slice(c * rows, (c + 1) * rows)
-        out[at] = (scale[at] * face[at]).astype(BF16)
+    out[...] = ((1.0 - column(w[1:2, :])) * keep * face[...]).astype(BF16)
 
 
 def north_face(i, faces, w):
-    return call(
-        north_kernel,
-        shape(FACE, BF16),
-        [SMEM, ANY, ANY],
-        VMEM,
-        [pltpu.VMEM((FACE, RHS), F32), pltpu.VMEM((2, FACE), F32), pltpu.SemaphoreType.DMA((5,))],
-        vmem=52,
-        cost=4,
-    )(i, faces, w)
+    face = call(load_kernel, shape(FACE, F32), [ANY], VMEM, [pltpu.SemaphoreType.DMA(())], vmem=52, cost=4)(faces)
+    return call(north_kernel, shape(FACE, BF16), [SMEM, VMEM, VMEM], VMEM)(i, face, w)
 
 
 def east_kernel(pos, faces, w, out, own):
@@ -309,46 +292,68 @@
         out[...] = shares[at ^ k]
 
 
-def final_kernel(pos, b0, b1, b2, b3, kept, from_east, from_north, w, basis, z, cur, slots, zbuf, sem):
+def base_kernel(kept, got, w, out):
+    wc = column(w[1:2, :])
+    out[...] = wc * kept[FACE:] + (1.0 - wc) * got[:FACE].astype(F32)
+
+
+def correction(f, cc, got, w, basis):
+    wr = w[f : f + 1, :]
+    mine = basis[:, f * FACE : (f + 1) * FACE].astype(F32) * wr
+    other = got[FACE:].astype(F32)[:4] * (1.0 - wr)
+    x = jnp.concatenate([mine, other], axis=0)
+    c = jnp.concatenate([cc[0:4], cc[4 + 4 * f : 8 + 4 * f]], axis=0)
+    xh, ch = x.astype(BF16).astype(F32), c.astype(BF16).astype(F32)
+    pad = jnp.zeros((8, RHS), F32)
+    left = jnp.concatenate([xh, x - xh, xh, pad], axis=0).astype(BF16)
+    right = jnp.concatenate([ch, ch, c - ch, pad], axis=0).astype(BF16)
+    return left, right
+
+
+def written(f, n, part, zbuf, z, sem):
+    here = pl.ds(n * 128, 128)
+    zbuf[n * 128 : (n + 1) * 128] = part
+    copy = pltpu.make_async_copy(zbuf.at[here], z.at[f, here], sem.at[n])
+    copy.start()
+    return copy
+
+
+def final_north_kernel(pos, b0, b1, b2, b3, base, got, w, basis, z, cur, cc, slots, zbuf, sem):
     placed(lax.div(pos[0], 4), (b0, b3, b2, b1), slots)
     cur[...] = summed(slots, 12) / FACE
-    cc = (slots[0] + slots[1]) + (slots[2] + slots[3])
+    cc[...] = (slots[0] + slots[1]) + (slots[2] + slots[3])
+    left, right = correction(1, cc[...], got, w, basis)
     copies = []
-    for f, got in enumerate((from_east, from_north)):
-        wr = w[f : f + 1, :]
-        mine = basis[:, f * FACE : (f + 1) * FACE].astype(F32) * wr
-        other = got[FACE:].astype(F32)[:4] * (1.0 - wr)
-        x = jnp.concatenate([mine, other], axis=0)
-        c = jnp.concatenate([cc[0:4], cc[4 + 4 * f : 8 + 4 * f]], axis=0)
-        xh, ch = x.astype(BF16).astype(F32), c.astype(BF16).astype(F32)
-        pad = jnp.zeros((8, RHS), F32)
-        left = jnp.concatenate([xh, x - xh, xh, pad], axis=0).astype(BF16)
-        right = jnp.concatenate([ch, ch, c - ch, pad], axis=0).astype(BF16)
-        wc = column(wr)
-        for n in range(2):
-            rows = slice(n * 256, (n + 1) * 256)
-            part = wc[rows] * kept[f * FACE + n * 256 : f * FACE + (n + 1) * 256] + (1.0 - wc[rows]) * got[rows].astype(F32)
-            zbuf[f, rows] = part + mm_tn(left[:, rows], right)
-            here = pl.ds(n * 256, 256)
-            copy = pltpu.make_async_copy(zbuf.at[f, here], z.at[f, here], sem.at[2 * f + n])
-            copy.start()
-            copies.append(copy)
+    for n in range(4):
+        rows = slice(n * 128, (n + 1) * 128)
+        copies.append(written(1, n, base[rows] + mm_tn(left[:, rows], right), zbuf, z, sem))
     for copy in copies:
         copy.wait()
 
 
-def final(at, blocks, kept, from_east, from_north, w, basis):
-    return call(
-        final_kernel,
-        (jax.ShapeDtypeStruct((2, FACE, RHS), F32), shape(NTERM, F32)),
-        [SMEM] + [VMEM] * 9,
-        (ANY, VMEM),
-        [
-            pltpu.VMEM((4, 16, RHS), F32),
-            pltpu.VMEM((2, FACE, RHS), F32),
-            pltpu.SemaphoreType.DMA((4,)),
-        ],
-    )(at, *blocks, kept, from_east, from_north, w, basis)
+def final_east_kernel(cc, kept, got, w, basis, z, zbuf, sem):
+    left, right = correction(0, cc[...], got, w, basis)
+    wc = column(w[0:1, :])
+    copies = []
+    for n in range(4):
+        rows = slice(n * 128, (n + 1) * 128)
+        part = wc[rows] * kept[rows] + (1.0 - wc[rows]) * got[rows].astype(F32)
+        copies.append(written(0, n, part + mm_tn(left[:, rows], right), zbuf, z, sem))
+    for copy in copies:
+        copy.wait()
+
+
+def final(at, blocks, kept, base, from_east, from_north, w, basis):
+    own = [pltpu.VMEM((FACE, RHS), F32), pltpu.SemaphoreType.DMA((4,))]
+    z, currents, cc = call(
+        final_north_kernel,
+        (jax.ShapeDtypeStruct((2, FACE, RHS), F32), shape(NTERM, F32), shape(16, F32)),
+        [SMEM] + [VMEM] * 8,
+        (ANY, VMEM, VMEM),
+        [pltpu.VMEM((4, 16, RHS), F32)] + own,
+    )(at, *blocks, base, from_north, w, basis)
+    (z,) = call(final_east_kernel, (), [VMEM] * 5, (), own, into=z)(cc, kept, from_east, w, basis)
+    return z, currents
 
 
 def along(x, axis, d):
@@ -438,20 +443,21 @@
         j, coup, block, h, ub, south, basis
     )
     from_east = along(to_west, "col", -1)
+    kept = call(kept_kernel, shape(2 * FACE, F32), [VMEM] * 5, VMEM, after=(sums, to_west), cost=30)(
+        coup, block, h, ub, south
+    )
     shares = call(
         columns_kernel,
         (shape(16, F32),) * 4,
         [SMEM, SMEM] + [VMEM] * 5,
         (VMEM,) * 4,
         [pltpu.VMEM((4, 19, RHS), F32), pltpu.VMEM((48, RHS), F32), pltpu.VMEM((4, 16, RHS), F32)],
-        after=(to_west,),
+        after=(kept,),
     )(i, j, *blocks, e)
-    kept = call(kept_kernel, shape(2 * FACE, F32), [VMEM] * 5, VMEM, after=(shares[0],), cost=30)(
-        coup, block, h, ub, south
-    )
     far, middle, near = [exchanged(shares[k], "row", 4, k) for k in (3, 2, 1)]
     blocks = [shares[0], far, middle, near]
-    z, currents = final(i, blocks, kept, from_east, from_north, w, basis)
+    base = call(base_kernel, shape(FACE, F32), [VMEM] * 3, VMEM, after=(shares[0],), cost=60)(kept, from_north, w)
+    z, currents = final(i, blocks, kept, base, from_east, from_north, w, basis)
     return x[None, None], z[None, None], currents
 
 

time: 49.7 us -> 49.9 us (level)
  Pallas kernels: 21.7 us -> 22.9 us
  local copies, waits for them, and re-layouts: 2.71 us -> 2.05 us
    pallas_call x16 -> x19, Pallas kernels: 21.7 us -> 22.9 us  [made(): result = run(*args, *extra)]
    unnamed x24 -> x22, local copies, waits for them, and re-layouts: 2.71 us -> 2.05 us
  transfers between devices with their start and end apart: 14 -> 14, of which waited for: 5 -> 6; matrix products, arithmetic and copies ran while one was open for 0% -> 0% of each run, Pallas kernels for 35% -> 40%
where the time goes in v4:
time: 49.9 us; the launch traced here: 49.8 us
  Pallas kernels  22.9 us (46%)
  starting transfers between devices  17.2 us (34%)
  waiting for transfers between devices  6.61 us (13%)
  local copies, waits for them, and re-layouts  2.05 us (4%)
  between operations  1.03 us (2%)
    pallas_call x19, Pallas kernels, made(): result = run(*args, *extra)  22.9 us
    ppermute x9, starting transfers between devices, exchanged(): lax.ppermute(x, axis, [(d ^ k * stride, d) for d in range(lax.axis_size(a...  12.7 us
    ppermute x4, starting transfers between devices, along(): return lax.ppermute(x, axis, [(s, (s + d) % n) for s in range(n)])  4.47 us
    ppermute x4, waiting for transfers between devices, along(): return lax.ppermute(x, axis, [(s, (s + d) % n) for s in range(n)])  3.43 us
    ppermute x9, waiting for transfers between devices, exchanged(): lax.ppermute(x, axis, [(d ^ k * stride, d) for d in range(lax.axis_size(a...  2.71 us
    unnamed x22, local copies, waits for them, and re-layouts  2.05 us
  transfers between devices with their start and end apart: 14, of which 6 were waited for; matrix products, arithmetic and copies ran while one was open for 0% of the time, Pallas kernels for 40%

profile of v4, /device:TPU:0, one launch (start us, length us, event | category | flops | bytes accessed | tf_op | source)
XLA Modules:
  0.0 49.8 jit_solution(8328806727302451419)
XLA Ops:
  0.7 1.4 %load_kernel.1.refs_1_ = f32[512,512]{1,0:T(8,128)S(1)} custom-call(f32[2,512,512]{2,1,0:T(8,128)} %bitcast.43), custom_call_target="tpu_custom_call" | custom-call | flops 4000001024 | bytes 12001000 | tf_op jit(solution)/shard_map/load_kernel/pallas_call | solution.py:78
  2.1 0.3 north_kernel.1.refs_3_
  2.3 2.1 %collective-permute-start.1 = (bf16[512,512]{1,0:T(8,128)(2,1)S(1)}, bf16[512,512]{1,0:T(8,128)(2,1)S(1)}, u32[]{:S(2)}, u32[]{:S(2)}) collective-permute-start(bf16[512,512]{1,0:T(8,128)(2,1)S(1)} %north_kernel.1.refs_3_), channel_id=1, source_target_pairs={{0,8},{8,16},{16,24},{24,32},{32,40},{40,48},{48,56},{56,64},{64,7... | collective-permute-start | bytes 1572872 | tf_op jit(solution)/shard_map/ppermute | solution.py:361
  4.4 0.0 copy-start.2
  4.4 0.0 copy-start.7
  4.4 0.0 copy-start.8
  4.4 0.5 east_kernel.1
  4.9 0.0 collective-permute-start
  4.9 0.4 copy-done.3
  5.3 1.3 %table_kernel.1.refs_5_.refs_6_ = f32[64,48]{1,0:T(8,128)S(1)} custom-call(s32[1]{0:T(128)} %bitcast.refs_0_, s32[1]{0:T(128)} %bitcast.5.refs_0_.refs_1_, s32[32,16]{1,0:T(8,128)S(1)} %bitcast.36, s32[32,16]{1,0:T(8,128)S(1)} %bitcast.37, f32[153,153]{1,0:T(8,128)S(1)} %copy-done.3, bf16[1024,512]{1,0:T(8,128)(2,1)S(1)} %get-tuple-element.26.refs_5_.refs_2_), custom_call_target="tpu_custom_call" | custom-call | flops 1000 | bytes 1000 | tf_op jit(solution)/shard_map/table_kernel/pallas_call | solution.py:78
  6.7 0.0 copy-done
  6.7 0.7 %copy-done.7 = f32[1,1,1024,512]{3,2,1,0:T(8,128)S(1)} copy-done((f32[1,1,1024,512]{3,2,1,0:T(8,128)S(1)}, f32[1,1,1024,512]{3,2,1,0:T(8,128)}, u32[]{:S(2)}) %copy-start.7) | copy-done | bytes 2097176
  7.4 2.3 %early_a_kernel.1 = (f32[1024,512]{1,0:T(8,128)S(1)}, f32[8,1024]{1,0:T(8,128)S(1)}, bf16[8,2048]{1,0:T(8,128)(2,1)S(1)}) custom-call(bf16[1024,2048]{1,0:T(8,128)(2,1)S(1)} %bitcast.22, f32[1024,512]{1,0:T(8,128)S(1)} %bitcast.45, bf16[1024,512]{1,0:T(8,128)(2,1)S(1)} %get-tuple-element.26.refs_5_.refs_2_, bf16[4,2048]{1,0:T(4,128)(2,1)S(1)} %bitcast.31, ...), custom_call_target="tpu_custom_call" | custom-call | flops 10000001024 | bytes 30001000 | tf_op jit(solution)/shard_map/early_a_kernel/pallas_call | solution.py:78
  9.7 0.0 slice-start.1
  9.8 1.4 %early_b_kernel.1 = (f32[8,2048]{1,0:T(8,128)S(1)}, f32[8,512]{1,0:T(8,128)S(1)}) custom-call(f32[8,1024]{1,0:T(8,128)S(1)} %get-tuple-element.29.refs_0_, bf16[1024,1024]{1,0:T(8,128)(2,1)S(1)} %bitcast.29, bf16[1024,2048]{1,0:T(8,128)(2,1)S(1)} %bitcast.23, f32[1024,512]{1,0:T(8,128)S(1)} %bitcast.46), custom_call_target="tpu_custom_call" | custom-call | flops 10000001024 | bytes 30001000 | tf_op jit(solution)/shard_map/early_b_kernel/pallas_call | solution.py:78
  11.1 0.9 %slice-done.1 = s8[4194304]{0:T(1024)(128)(4,1)S(1)} async-done(((s8[8388608]{0:T(1024)(128)(4,1)}), s8[4194304]{0:T(1024)(128)(4,1)S(1)}, s32[]{:S(2)}) %slice-start.1) | async-done | bytes 4194328
  12.0 3.6 %early_c_kernel.1 = (f32[2048,512]{1,0:T(8,128)S(1)}, f32[8,512]{1,0:T(8,128)S(1)}, bf16[16,1024]{1,0:T(8,128)(2,1)S(1)}) custom-call(bf16[8,2048]{1,0:T(8,128)(2,1)S(1)} %get-tuple-element.28.refs_0_, bf16[2048,2048]{1,0:T(8,128)(2,1)S(1)} %bitcast.17, bf16[1024,512]{1,0:T(8,128)(2,1)S(1)} %get-tuple-element.26.refs_5_.refs_2_, ...), custom_call_target="tpu_custom_call" | custom-call | flops 10000001024 | bytes 30001000 | tf_op jit(solution)/shard_map/early_c_kernel/pallas_call | solution.py:78
  15.6 0.0 collective-permute-done.refs_6_
  15.6 1.8 %west_terms_kernel.1 = (f32[1024,512]{1,0:T(8,128)S(1)}, f32[2048,512]{1,0:T(8,128)S(1)}, f32[8,512]{1,0:T(8,128)S(1)}) custom-call(bf16[1024,2048]{1,0:T(8,128)(2,1)S(1)} %bitcast.24, bf16[2048,2048]{1,0:T(8,128)(2,1)S(1)} %bitcast.18, f32[1024,512]{1,0:T(8,128)S(1)} %get-tuple-element.27.refs_2_, f32[2048,512]{1,0:T(8,128)S(1)} %get-tuple-element.32.refs_3_, ...), custom_call_target="tpu_custom_call" | custom-call | flops 2000001024 | bytes 6001000 | tf_op jit(solution)/shard_map/west_terms_kernel/pallas_call | solution.py:78
  17.5 3.4 %collective-permute-done.1.refs_2_.refs_6_.refs_5_.refs_4_ = bf16[512,512]{1,0:T(8,128)(2,1)S(1)} collective-permute-done((bf16[512,512]{1,0:T(8,128)(2,1)S(1)}, bf16[512,512]{1,0:T(8,128)(2,1)S(1)}, u32[]{:S(2)}, u32[]{:S(2)}) %collective-permute-start.1) | collective-permute-done | bytes 524320 | tf_op jit(solution)/shard_map/ppermute | solution.py:361
  20.9 0.2 corner_kernel.1.refs_3_.refs_1_
  21.1 0.0 collective-permute-start.2
  21.1 0.7 %inner_kernel.1.refs_3_.refs_4_ = bf16[1024,512]{1,0:T(8,128)(2,1)S(1)} custom-call(bf16[1024,2048]{1,0:T(8,128)(2,1)S(1)} %bitcast.25, f32[1024,512]{1,0:T(8,128)S(1)} %get-tuple-element.36.refs_1_, bf16[512,512]{1,0:T(8,128)(2,1)S(1)} %collective-permute-done.1.refs_2_.refs_6_.refs_5_.refs_4_, f32[8,512]{1,0:T(8,128)S(1)} %corner_kernel.1.refs_3_.refs_1_), custom_call_target="tpu_custom_call" | custom-call | flops 1000001024 | bytes 3001000 | tf_op jit(solution)/shard_map/inner_kernel/pallas_call | solution.py:78
  21.8 0.5 collective-permute-done.2.refs_2_
  22.3 0.1 collective-permute-start.5
  22.4 0.8 %collective-permute-start.4 = (f32[10,512]{1,0:T(8,128)S(1)}, f32[10,512]{1,0:T(8,128)S(1)}, u32[]{:S(2)}, u32[]{:S(2)}) collective-permute-start(f32[10,512]{1,0:T(8,128)S(1)} %pair_kernel.1.refs_8_.refs_1_), channel_id=1, source_target_pairs={{16,0},{24,8},{0,16},{8,24},{48,32},{56,40},{32,48},{40,56},{80,64... | collective-permute-start | bytes 61448 | tf_op jit(solution)/shard_map/ppermute | solution.py:365
  23.2 3.3 %collective-permute-start.3 = (f32[10,512]{1,0:T(8,128)S(1)}, f32[10,512]{1,0:T(8,128)S(1)}, u32[]{:S(2)}, u32[]{:S(2)}) collective-permute-start(f32[10,512]{1,0:T(8,128)S(1)} %pair_kernel.1.refs_8_.refs_1_), channel_id=1, source_target_pairs={{8,0},{0,8},{24,16},{16,24},{40,32},{32,40},{56,48},{48,56},{72,64... | collective-permute-start | bytes 61448 | tf_op jit(solution)/shard_map/ppermute | solution.py:365
  26.5 2.8 %solve_kernel.1 = (f32[1024,512]{1,0:T(8,128)}, bf16[528,512]{1,0:T(8,128)(2,1)S(1)}, bf16[1024,512]{1,0:T(8,128)(2,1)S(1)}) custom-call(s32[1]{0:T(128)} %bitcast.refs_0_, bf16[1024,2048]{1,0:T(8,128)(2,1)S(1)} %bitcast.26, bf16[1024,1024]{1,0:T(8,128)(2,1)S(1)} %bitcast.30, bf16[2048,2048]{1,0:T(8,128)(2,1)S(1)} %bitcast.19, ...), custom_call_target="tpu_custom_call" | custom-call | flops 4000001024 | bytes 12001000 | tf_op jit(solution)/shard_map/solve_kernel/pallas_call | solution.py:78
  29.2 1.8 %collective-permute-start.12 = (bf16[528,512]{1,0:T(8,128)(2,1)S(1)}, bf16[528,512]{1,0:T(8,128)(2,1)S(1)}, u32[]{:S(2)}, u32[]{:S(2)}) collective-permute-start(bf16[528,512]{1,0:T(8,128)(2,1)S(1)} %get-tuple-element.40.refs_5_), channel_id=1, source_target_pairs={{0,120},{8,0},{16,8},{24,16},{32,24},{40,32},{48,40},{56,48},{64,5... | collective-permute-start | bytes 1622024 | tf_op jit(solution)/shard_map/ppermute | solution.py:361
  31.1 0.0 collective-permute-done.5.refs_4_
  31.1 0.0 collective-permute-done.4.refs_3_
  31.1 3.0 %collective-permute-start.8 = (f32[19,512]{1,0:T(8,128)S(1)}, f32[19,512]{1,0:T(8,128)S(1)}, u32[]{:S(2)}, u32[]{:S(2)}) collective-permute-start(f32[19,512]{1,0:T(8,128)S(1)} %rows_kernel.1.refs_7_.refs_5_.refs_2_), channel_id=1, source_target_pairs={{6,0},{7,1},{4,2},{5,3},{2,4},{3,5},{0,6},{1,7},{14,8},{15,9},{12,... | collective-permute-start | bytes 116744 | tf_op jit(solution)/shard_map/ppermute | solution.py:365
  34.1 0.8 %collective-permute-start.7 = (f32[19,512]{1,0:T(8,128)S(1)}, f32[19,512]{1,0:T(8,128)S(1)}, u32[]{:S(2)}, u32[]{:S(2)}) collective-permute-start(f32[19,512]{1,0:T(8,128)S(1)} %rows_kernel.1.refs_7_.refs_5_.refs_2_), channel_id=1, source_target_pairs={{4,0},{5,1},{6,2},{7,3},{0,4},{1,5},{2,6},{3,7},{12,8},{13,9},{14,... | collective-permute-start | bytes 116744 | tf_op jit(solution)/shard_map/ppermute | solution.py:365
  34.9 0.5 %collective-permute-start.6 = (f32[19,512]{1,0:T(8,128)S(1)}, f32[19,512]{1,0:T(8,128)S(1)}, u32[]{:S(2)}, u32[]{:S(2)}) collective-permute-start(f32[19,512]{1,0:T(8,128)S(1)} %rows_kernel.1.refs_7_.refs_5_.refs_2_), channel_id=1, source_target_pairs={{2,0},{3,1},{0,2},{1,3},{6,4},{7,5},{4,6},{5,7},{10,8},{11,9},{8,1... | collective-permute-start | bytes 116744 | tf_op jit(solution)/shard_map/ppermute | solution.py:365
  35.5 1.0 %west_kernel.1.refs_6_ = bf16[528,512]{1,0:T(8,128)(2,1)S(1)} custom-call(s32[1]{0:T(128)} %bitcast.5.refs_0_.refs_1_, bf16[1024,2048]{1,0:T(8,128)(2,1)S(1)} %bitcast.27, bf16[2048,2048]{1,0:T(8,128)(2,1)S(1)} %bitcast.20, f32[2048,512]{1,0:T(8,128)S(1)} %get-tuple-element.38.refs_5_.refs_3_.refs_2_, ...), custom_call_target="tpu_custom_call" | custom-call | flops 1000001024 | bytes 3001000 | tf_op jit(solution)/shard_map/west_kernel/pallas_call | solution.py:78
  36.5 0.6 %collective-permute-start.13 = (bf16[528,512]{1,0:T(8,128)(2,1)S(1)}, bf16[528,512]{1,0:T(8,128)(2,1)S(1)}, u32[]{:S(2)}, u32[]{:S(2)}) collective-permute-start(bf16[528,512]{1,0:T(8,128)(2,1)S(1)} %west_kernel.1.refs_6_), channel_id=1, source_target_pairs={{0,7},{1,0},{2,1},{3,2},{4,3},{5,4},{6,5},{7,6},{8,15},{9,8},{10,9... | collective-permute-start | bytes 1622024 | tf_op jit(solution)/shard_map/ppermute | solution.py:361
  37.0 1.8 %kept_kernel.1.refs_7_.refs_0_.refs_1_ = f32[1024,512]{1,0:T(8,128)S(1)} custom-call(bf16[1024,2048]{1,0:T(8,128)(2,1)S(1)} %bitcast.28, bf16[2048,2048]{1,0:T(8,128)(2,1)S(1)} %bitcast.21, f32[2048,512]{1,0:T(8,128)S(1)} %get-tuple-element.38.refs_5_.refs_3_.refs_2_, bf16[1024,512]{1,0:T(8,128)(2,1)S(1)} %get-tuple-element.41.refs_4_.refs_3_, ...), custom_call_target="tpu_custom_call" | custom-call | flops 30000001024 | bytes 90001000 | tf_op jit(solution)/shard_map/kept_kernel/pallas_call | solution.py:78
  38.9 0.9 %collective-permute-done.7.refs_4_ = f32[19,512]{1,0:T(8,128)S(1)} collective-permute-done((f32[19,512]{1,0:T(8,128)S(1)}, f32[19,512]{1,0:T(8,128)S(1)}, u32[]{:S(2)}, u32[]{:S(2)}) %collective-permute-start.7) | collective-permute-done | bytes 38944 | tf_op jit(solution)/shard_map/ppermute | solution.py:365
  39.7 0.2 columns_kernel.1
  40.0 0.8 %collective-permute-start.9 = (f32[16,512]{1,0:T(8,128)S(1)}, f32[16,512]{1,0:T(8,128)S(1)}, u32[]{:S(2)}, u32[]{:S(2)}) collective-permute-start(f32[16,512]{1,0:T(8,128)S(1)} %get-tuple-element.43), channel_id=1, source_target_pairs={{96,0},{104,8},{112,16},{120,24},{64,32},{72,40},{80,48},{88,56},{... | collective-permute-start | bytes 98312 | tf_op jit(solution)/shard_map/ppermute | solution.py:365
  40.8 1.1 %collective-permute-start.10 = (f32[16,512]{1,0:T(8,128)S(1)}, f32[16,512]{1,0:T(8,128)S(1)}, u32[]{:S(2)}, u32[]{:S(2)}) collective-permute-start(f32[16,512]{1,0:T(8,128)S(1)} %get-tuple-element.44), channel_id=1, source_target_pairs={{64,0},{72,8},{80,16},{88,24},{96,32},{104,40},{112,48},{120,56},{... | collective-permute-start | bytes 98312 | tf_op jit(solution)/shard_map/ppermute | solution.py:365
  41.9 2.2 %collective-permute-start.11 = (f32[16,512]{1,0:T(8,128)S(1)}, f32[16,512]{1,0:T(8,128)S(1)}, u32[]{:S(2)}, u32[]{:S(2)}) collective-permute-start(f32[16,512]{1,0:T(8,128)S(1)} %get-tuple-element.45), channel_id=1, source_target_pairs={{32,0},{40,8},{48,16},{56,24},{0,32},{8,40},{16,48},{24,56},{96,64... | collective-permute-start | bytes 98312 | tf_op jit(solution)/shard_map/ppermute | solution.py:365
  44.2 0.4 base_kernel.1.refs_5_
  44.6 0.6 %collective-permute-done.9.refs_2_ = f32[16,512]{1,0:T(8,128)S(1)} collective-permute-done((f32[16,512]{1,0:T(8,128)S(1)}, f32[16,512]{1,0:T(8,128)S(1)}, u32[]{:S(2)}, u32[]{:S(2)}) %collective-permute-start.9) | collective-permute-done | bytes 32800 | tf_op jit(solution)/shard_map/ppermute | solution.py:365
  45.2 1.0 %collective-permute-done.10.refs_3_ = f32[16,512]{1,0:T(8,128)S(1)} collective-permute-done((f32[16,512]{1,0:T(8,128)S(1)}, f32[16,512]{1,0:T(8,128)S(1)}, u32[]{:S(2)}, u32[]{:S(2)}) %collective-permute-start.10) | collective-permute-done | bytes 32800 | tf_op jit(solution)/shard_map/ppermute | solution.py:365
  46.2 0.2 collective-permute-done.11.refs_4_
  46.4 1.8 %final_north_kernel.1 = (f32[2,512,512]{2,1,0:T(8,128)}, f32[4,512]{1,0:T(4,128)}, f32[16,512]{1,0:T(8,128)S(1)}) custom-call(s32[1]{0:T(128)} %bitcast.refs_0_, f32[16,512]{1,0:T(8,128)S(1)} %get-tuple-element.42.refs_3_.refs_1_, f32[16,512]{1,0:T(8,128)S(1)} %collective-permute-done.9.refs_2_, f32[16,512]{1,0:T(8,128)S(1)} %collective-permute-done.10.refs_3_, ...), custom_call_target="tpu_custom_call" | custom-call | flops 1000 | bytes 1000 | tf_op jit(solution)/shard_map/final_north_kernel/pallas_call | solution.py:78
  48.2 1.4 %final_east_kernel.1 = f32[2,512,512]{2,1,0:T(8,128)} custom-call(f32[16,512]{1,0:T(8,128)S(1)} %get-tuple-element.46.refs_0_, f32[1024,512]{1,0:T(8,128)S(1)} %kept_kernel.1.refs_7_.refs_0_.refs_1_, bf16[528,512]{1,0:T(8,128)(2,1)S(1)} %collective-permute-done.13.refs_2_, f32[2,512]{1,0:T(2,128)S(1)} %bitcast.42, ...), custom_call_target="tpu_custom_call", output_to_operand_aliasing={{}: (5, {})} | custom-call | flops 1000 | bytes 1000 | tf_op jit(solution)/shard_map/final_east_kernel/pallas_call | solution.py:78
  (22 shorter events, 0.1 us)
Async XLA Ops:
  0.6 1.4 %copy-start.5 = (f32[1,1,2,512]{3,2,1,0:T(2,128)S(1)}, f32[1,1,2,512]{3,2,1,0:T(2,128)}, u32[]{:S(2)}) copy-start(f32[1,1,2,512]{3,2,1,0:T(2,128)} %param.12) | copy-start | bytes 12292
  0.6 3.8 %copy-start.6 = (f32[1,1,2,512,512]{4,3,2,1,0:T(8,128)S(1)}, f32[1,1,2,512,512]{4,3,2,1,0:T(8,128)}, u32[]{:S(2)}) copy-start(f32[1,1,2,512,512]{4,3,2,1,0:T(8,128)} %param.11) | copy-start | bytes 6291460
  2.3 18.6 %collective-permute-start.1 = (bf16[512,512]{1,0:T(8,128)(2,1)S(1)}, bf16[512,512]{1,0:T(8,128)(2,1)S(1)}, u32[]{:S(2)}, u32[]{:S(2)}) collective-permute-start(bf16[512,512]{1,0:T(8,128)(2,1)S(1)} %north_kernel.1.refs_3_), channel_id=1, source_target_pairs={{0,8},{8,16},{16,24},{24,32},{32,40},{40,48},{48,56},{56,64},{64,7... | collective-permute-start | bytes 1572872 | tf_op jit(solution)/shard_map/ppermute | solution.py:361
  4.4 0.9 %copy-start.3 = (f32[153,153]{1,0:T(8,128)S(1)}, f32[153,153]{1,0:T(8,128)}, u32[]{:S(2)}) copy-start(f32[153,153]{1,0:T(8,128)} %refs_4_.1) | copy-start | bytes 280912
  4.4 0.9 %copy-start.4 = (s32[16,8,4]{0,2,1:T(4,128)S(1)}, s32[16,8,4]{0,2,1:T(4,128)}, u32[]{:S(2)}) copy-start(s32[16,8,4]{0,2,1:T(4,128)} %param.18) | copy-start | bytes 6148
  4.4 2.3 %copy-start = (bf16[1,1,1024,2048]{3,2,1,0:T(8,128)(2,1)S(1)}, bf16[1,1,1024,2048]{3,2,1,0:T(8,128)(2,1)}, u32[]{:S(2)}) copy-start(bf16[1,1,1024,2048]{3,2,1,0:T(8,128)(2,1)} %param.14) | copy-start | bytes 12582916
  4.4 2.3 %copy-start.2 = (bf16[1,1,4,2048]{3,2,1,0:T(4,128)(2,1)S(1)}, bf16[1,1,4,2048]{3,2,1,0:T(4,128)(2,1)}, u32[]{:S(2)}) copy-start(bf16[1,1,4,2048]{3,2,1,0:T(4,128)(2,1)} %param.16) | copy-start | bytes 49156
  4.4 3.0 %copy-start.7 = (f32[1,1,1024,512]{3,2,1,0:T(8,128)S(1)}, f32[1,1,1024,512]{3,2,1,0:T(8,128)}, u32[]{:S(2)}) copy-start(f32[1,1,1024,512]{3,2,1,0:T(8,128)} %param.10) | copy-start | bytes 6291460
  4.4 3.0 %copy-start.8 = (s32[1,1,4,512]{3,2,1,0:T(4,128)S(1)}, s32[1,1,4,512]{3,2,1,0:T(4,128)}, u32[]{:S(2)}) copy-start(s32[1,1,4,512]{3,2,1,0:T(4,128)} %param.19) | copy-start | bytes 24580
  4.9 10.7 %collective-permute-start = (bf16[512,512]{1,0:T(8,128)(2,1)S(1)}, bf16[512,512]{1,0:T(8,128)(2,1)S(1)}, u32[]{:S(2)}, u32[]{:S(2)}) collective-permute-start(bf16[512,512]{1,0:T(8,128)(2,1)S(1)} %get-tuple-element.35), channel_id=1, source_target_pairs={{0,1},{1,2},{2,3},{3,4},{4,5},{5,6},{6,7},{7,0},{8,9},{9,10},{10,1... | collective-permute-start | bytes 1572872 | tf_op jit(solution)/shard_map/ppermute | solution.py:361
  7.4 2.3 %copy-start.1 = (bf16[1,1,1024,1024]{3,2,1,0:T(8,128)(2,1)S(1)}, bf16[1,1,1024,1024]{3,2,1,0:T(8,128)(2,1)}, u32[]{:S(2)}) copy-start(bf16[1,1,1024,1024]{3,2,1,0:T(8,128)(2,1)} %param.13) | copy-start | bytes 6291460
  7.4 3.7 %slice-start = ((s8[8388608]{0:T(1024)(128)(4,1)}), s8[4194304]{0:T(1024)(128)(4,1)S(1)}, s32[]{:S(2)}) async-start(s8[8388608]{0:T(1024)(128)(4,1)} %bitcast.15), calls=%async_computation | async-start | bytes 8388608
  9.7 2.3 %slice-start.1 = ((s8[8388608]{0:T(1024)(128)(4,1)}), s8[4194304]{0:T(1024)(128)(4,1)S(1)}, s32[]{:S(2)}) async-start(s8[8388608]{0:T(1024)(128)(4,1)} %bitcast.15), calls=%async_computation.1 | async-start | bytes 8388608
  21.1 1.2 %collective-permute-start.2 = (f32[8,512]{1,0:T(8,128)S(1)}, f32[8,512]{1,0:T(8,128)S(1)}, u32[]{:S(2)}, u32[]{:S(2)}) collective-permute-start(f32[8,512]{1,0:T(8,128)S(1)} %corner_kernel.1.refs_3_.refs_1_), channel_id=1, source_target_pairs={{0,1},{1,0},{2,3},{3,2},{4,5},{5,4},{6,7},{7,6},{8,9},{9,8},{10,11... | collective-permute-start | bytes 49160 | tf_op jit(solution)/shard_map/ppermute | solution.py:424
  22.3 8.8 %collective-permute-start.5 = (f32[10,512]{1,0:T(8,128)S(1)}, f32[10,512]{1,0:T(8,128)S(1)}, u32[]{:S(2)}, u32[]{:S(2)}) collective-permute-start(f32[10,512]{1,0:T(8,128)S(1)} %pair_kernel.1.refs_8_.refs_1_), channel_id=1, source_target_pairs={{24,0},{16,8},{8,16},{0,24},{56,32},{48,40},{40,48},{32,56},{88,64... | collective-permute-start | bytes 61448 | tf_op jit(solution)/shard_map/ppermute | solution.py:365
  22.4 8.7 %collective-permute-start.4 = (f32[10,512]{1,0:T(8,128)S(1)}, f32[10,512]{1,0:T(8,128)S(1)}, u32[]{:S(2)}, u32[]{:S(2)}) collective-permute-start(f32[10,512]{1,0:T(8,128)S(1)} %pair_kernel.1.refs_8_.refs_1_), channel_id=1, source_target_pairs={{16,0},{24,8},{0,16},{8,24},{48,32},{56,40},{32,48},{40,56},{80,64... | collective-permute-start | bytes 61448 | tf_op jit(solution)/shard_map/ppermute | solution.py:365
  23.2 7.9 %collective-permute-start.3 = (f32[10,512]{1,0:T(8,128)S(1)}, f32[10,512]{1,0:T(8,128)S(1)}, u32[]{:S(2)}, u32[]{:S(2)}) collective-permute-start(f32[10,512]{1,0:T(8,128)S(1)} %pair_kernel.1.refs_8_.refs_1_), channel_id=1, source_target_pairs={{8,0},{0,8},{24,16},{16,24},{40,32},{32,40},{56,48},{48,56},{72,64... | collective-permute-start | bytes 61448 | tf_op jit(solution)/shard_map/ppermute | solution.py:365
  29.2 14.9 %collective-permute-start.12 = (bf16[528,512]{1,0:T(8,128)(2,1)S(1)}, bf16[528,512]{1,0:T(8,128)(2,1)S(1)}, u32[]{:S(2)}, u32[]{:S(2)}) collective-permute-start(bf16[528,512]{1,0:T(8,128)(2,1)S(1)} %get-tuple-element.40.refs_5_), channel_id=1, source_target_pairs={{0,120},{8,0},{16,8},{24,16},{32,24},{40,32},{48,40},{56,48},{64,5... | collective-permute-start | bytes 1622024 | tf_op jit(solution)/shard_map/ppermute | solution.py:361
  31.1 7.7 %collective-permute-start.8 = (f32[19,512]{1,0:T(8,128)S(1)}, f32[19,512]{1,0:T(8,128)S(1)}, u32[]{:S(2)}, u32[]{:S(2)}) collective-permute-start(f32[19,512]{1,0:T(8,128)S(1)} %rows_kernel.1.refs_7_.refs_5_.refs_2_), channel_id=1, source_target_pairs={{6,0},{7,1},{4,2},{5,3},{2,4},{3,5},{0,6},{1,7},{14,8},{15,9},{12,... | collective-permute-start | bytes 116744 | tf_op jit(solution)/shard_map/ppermute | solution.py:365
  34.1 5.6 %collective-permute-start.7 = (f32[19,512]{1,0:T(8,128)S(1)}, f32[19,512]{1,0:T(8,128)S(1)}, u32[]{:S(2)}, u32[]{:S(2)}) collective-permute-start(f32[19,512]{1,0:T(8,128)S(1)} %rows_kernel.1.refs_7_.refs_5_.refs_2_), channel_id=1, source_target_pairs={{4,0},{5,1},{6,2},{7,3},{0,4},{1,5},{2,6},{3,7},{12,8},{13,9},{14,... | collective-permute-start | bytes 116744 | tf_op jit(solution)/shard_map/ppermute | solution.py:365
  34.9 4.8 %collective-permute-start.6 = (f32[19,512]{1,0:T(8,128)S(1)}, f32[19,512]{1,0:T(8,128)S(1)}, u32[]{:S(2)}, u32[]{:S(2)}) collective-permute-start(f32[19,512]{1,0:T(8,128)S(1)} %rows_kernel.1.refs_7_.refs_5_.refs_2_), channel_id=1, source_target_pairs={{2,0},{3,1},{0,2},{1,3},{6,4},{7,5},{4,6},{5,7},{10,8},{11,9},{8,1... | collective-permute-start | bytes 116744 | tf_op jit(solution)/shard_map/ppermute | solution.py:365
  36.5 11.8 %collective-permute-start.13 = (bf16[528,512]{1,0:T(8,128)(2,1)S(1)}, bf16[528,512]{1,0:T(8,128)(2,1)S(1)}, u32[]{:S(2)}, u32[]{:S(2)}) collective-permute-start(bf16[528,512]{1,0:T(8,128)(2,1)S(1)} %west_kernel.1.refs_6_), channel_id=1, source_target_pairs={{0,7},{1,0},{2,1},{3,2},{4,3},{5,4},{6,5},{7,6},{8,15},{9,8},{10,9... | collective-permute-start | bytes 1622024 | tf_op jit(solution)/shard_map/ppermute | solution.py:361
  40.0 5.2 %collective-permute-start.9 = (f32[16,512]{1,0:T(8,128)S(1)}, f32[16,512]{1,0:T(8,128)S(1)}, u32[]{:S(2)}, u32[]{:S(2)}) collective-permute-start(f32[16,512]{1,0:T(8,128)S(1)} %get-tuple-element.43), channel_id=1, source_target_pairs={{96,0},{104,8},{112,16},{120,24},{64,32},{72,40},{80,48},{88,56},{... | collective-permute-start | bytes 98312 | tf_op jit(solution)/shard_map/ppermute | solution.py:365
  40.8 5.4 %collective-permute-start.10 = (f32[16,512]{1,0:T(8,128)S(1)}, f32[16,512]{1,0:T(8,128)S(1)}, u32[]{:S(2)}, u32[]{:S(2)}) collective-permute-start(f32[16,512]{1,0:T(8,128)S(1)} %get-tuple-element.44), channel_id=1, source_target_pairs={{64,0},{72,8},{80,16},{88,24},{96,32},{104,40},{112,48},{120,56},{... | collective-permute-start | bytes 98312 | tf_op jit(solution)/shard_map/ppermute | solution.py:365
  41.9 4.4 %collective-permute-start.11 = (f32[16,512]{1,0:T(8,128)S(1)}, f32[16,512]{1,0:T(8,128)S(1)}, u32[]{:S(2)}, u32[]{:S(2)}) collective-permute-start(f32[16,512]{1,0:T(8,128)S(1)} %get-tuple-element.45), channel_id=1, source_target_pairs={{32,0},{40,8},{48,16},{56,24},{0,32},{8,40},{16,48},{24,56},{96,64... | collective-permute-start | bytes 98312 | tf_op jit(solution)/shard_map/ppermute | solution.py:365

commit v5 on v4

--- a/solution.py
+++ b/solution.py
@@ -47,38 +47,23 @@
     return jnp.transpose(jnp.broadcast_to(row, (8, row.shape[1])))[:, :1]
 
 
-def call(kernel, outs, in_specs, out_specs, scratch=(), after=(), into=None, vmem=16, cost=0):
+def call(kernel, outs, in_specs, out_specs, scratch=(), after=(), vmem=16, cost=0):
     n = len(in_specs)
-    several = isinstance(outs, tuple)
-    outs, out_specs = (outs, out_specs) if several else ((outs,), (out_specs,))
-    extra = list(after)
-    aliases = {}
-    if into is not None:
-        aliases = {n + len(extra): len(outs)}
-        extra.append(into)
-        outs = (*outs, jax.ShapeDtypeStruct(into.shape, into.dtype))
-        out_specs = (*out_specs, ANY)
 
     def body(*refs):
-        kernel(*refs[:n], *refs[n + len(extra) :])
+        kernel(*refs[:n], *refs[n + len(after) :])
 
     run = pl.pallas_call(
         body,
         name=kernel.__name__,
         out_shape=outs,
-        in_specs=list(in_specs) + [ANY] * len(extra),
+        in_specs=list(in_specs) + [ANY] * len(after),
         out_specs=out_specs,
         scratch_shapes=list(scratch),
-        input_output_aliases=aliases,
         compiler_params=pltpu.CompilerParams(vmem_limit_bytes=vmem << 20),
         cost_estimate=pl.CostEstimate(flops=1000 + cost * 1_000_000_000, bytes_accessed=1000 + cost * 3_000_000, transcendentals=0),
     )
-
-    def made(*args):
-        result = run(*args, *extra)
-        return result if several or aliases else result[0]
-
-    return made
+    return lambda *args: run(*args, *after)
 
 
 def shape(rows, kind, columns=RHS):
@@ -310,50 +295,38 @@
     return left, right
 
 
-def written(f, n, part, zbuf, z, sem):
-    here = pl.ds(n * 128, 128)
-    zbuf[n * 128 : (n + 1) * 128] = part
-    copy = pltpu.make_async_copy(zbuf.at[here], z.at[f, here], sem.at[n])
-    copy.start()
-    return copy
-
-
-def final_north_kernel(pos, b0, b1, b2, b3, base, got, w, basis, z, cur, cc, slots, zbuf, sem):
+def final_kernel(pos, b0, b1, b2, b3, kept, base, from_east, from_north, w, basis, z, cur, slots, zbuf, sem):
     placed(lax.div(pos[0], 4), (b0, b3, b2, b1), slots)
+    cc = (slots[0] + slots[1]) + (slots[2] + slots[3])
+    wc = column(w[0:1, :])
+    copies = []
+    for f, got in ((1, from_north), (0, from_east)):
+        left, right = correction(f, cc, got, w, basis)
+        for n in range(4):
+            rows = slice(n * 128, (n + 1) * 128)
+            part = base[rows] if f else wc[rows] * kept[rows] + (1.0 - wc[rows]) * got[rows].astype(F32)
+            zbuf[f, rows] = part + mm_tn(left[:, rows], right)
+            here = pl.ds(n * 128, 128)
+            copy = pltpu.make_async_copy(zbuf.at[f, here], z.at[f, here], sem.at[4 * f + n])
+            copy.start()
+            copies.append(copy)
     cur[...] = summed(slots, 12) / FACE
-    cc[...] = (slots[0] + slots[1]) + (slots[2] + slots[3])
-    left, right = correction(1, cc[...], got, w, basis)
-    copies = []
-    for n in range(4):
-        rows = slice(n * 128, (n + 1) * 128)
-        copies.append(written(1, n, base[rows] + mm_tn(left[:, rows], right), zbuf, z, sem))
     for copy in copies:
         copy.wait()
 
 
-def final_east_kernel(cc, kept, got, w, basis, z, zbuf, sem):
-    left, right = correction(0, cc[...], got, w, basis)
-    wc = column(w[0:1, :])
-    copies = []
-    for n in range(4):
-        rows = slice(n * 128, (n + 1) * 128)
-        part = wc[rows] * kept[rows] + (1.0 - wc[rows]) * got[rows].astype(F32)
-        copies.append(written(0, n, part + mm_tn(left[:, rows], right), zbuf, z, sem))
-    for copy in copies:
-        copy.wait()
-
-
 def final(at, blocks, kept, base, from_east, from_north, w, basis):
-    own = [pltpu.VMEM((FACE, RHS), F32), pltpu.SemaphoreType.DMA((4,))]
-    z, currents, cc = call(
-        final_north_kernel,
-        (jax.ShapeDtypeStruct((2, FACE, RHS), F32), shape(NTERM, F32), shape(16, F32)),
-        [SMEM] + [VMEM] * 8,
-        (ANY, VMEM, VMEM),
-        [pltpu.VMEM((4, 16, RHS), F32)] + own,
-    )(at, *blocks, base, from_north, w, basis)
-    (z,) = call(final_east_kernel, (), [VMEM] * 5, (), own, into=z)(cc, kept, from_east, w, basis)
-    return z, currents
+    return call(
+        final_kernel,
+        (jax.ShapeDtypeStruct((2, FACE, RHS), F32), shape(NTERM, F32)),
+        [SMEM] + [VMEM] * 10,
+        (ANY, VMEM),
+        [
+            pltpu.VMEM((4, 16, RHS), F32),
+            pltpu.VMEM((2, FACE, RHS), F32),
+            pltpu.SemaphoreType.DMA((8,)),
+        ],
+    )(at, *blocks, kept, base, from_east, from_north, w, basis)
 
 
 def along(x, axis, d):

time: 49.9 us -> 49 us (0.982)
  Pallas kernels: 22.9 us -> 22 us
    pallas_call x19 -> x18, Pallas kernels: 22.9 us -> 22 us  [call(): return lambda *args: run(*args, *after)]
  transfers between devices with their start and end apart: 14 -> 14, of which waited for: 6 -> 6; matrix products, arithmetic and copies ran while one was open for 0% -> 0% of each run, Pallas kernels for 40% -> 37%
where the time goes in v5:
time: 49 us; the launch traced here: 48.8 us
  Pallas kernels  22 us (45%)
  starting transfers between devices  17.2 us (35%)
  waiting for transfers between devices  6.63 us (14%)
  local copies, waits for them, and re-layouts  2.05 us (4%)
  between operations  1.02 us (2%)
    pallas_call x18, Pallas kernels, call(): return lambda *args: run(*args, *after)  22 us
    ppermute x9, starting transfers between devices, exchanged(): lax.ppermute(x, axis, [(d ^ k * stride, d) for d in range(lax.axis_size(a...  12.7 us
    ppermute x4, starting transfers between devices, along(): return lax.ppermute(x, axis, [(s, (s + d) % n) for s in range(n)])  4.47 us
    ppermute x4, waiting for transfers between devices, along(): return lax.ppermute(x, axis, [(s, (s + d) % n) for s in range(n)])  3.43 us
    ppermute x9, waiting for transfers between devices, exchanged(): lax.ppermute(x, axis, [(d ^ k * stride, d) for d in range(lax.axis_size(a...  2.73 us
    unnamed x22, local copies, waits for them, and re-layouts  2.05 us
  transfers between devices with their start and end apart: 14, of which 6 were waited for; matrix products, arithmetic and copies ran while one was open for 0% of the time, Pallas kernels for 37%

profile of v5, /device:TPU:0, one launch (start us, length us, event | category | flops | bytes accessed | tf_op | source)
XLA Modules:
  0.0 48.8 jit_solution(10706830416409852982)
XLA Ops:
  0.7 1.4 %load_kernel.1.refs_1_ = f32[512,512]{1,0:T(8,128)S(1)} custom-call(f32[2,512,512]{2,1,0:T(8,128)} %bitcast.41), custom_call_target="tpu_custom_call" | custom-call | flops 4000001024 | bytes 12001000 | tf_op jit(solution)/shard_map/load_kernel/pallas_call | solution.py:66
  2.1 0.3 north_kernel.1.refs_3_
  2.3 2.1 %collective-permute-start.1 = (bf16[512,512]{1,0:T(8,128)(2,1)S(1)}, bf16[512,512]{1,0:T(8,128)(2,1)S(1)}, u32[]{:S(2)}, u32[]{:S(2)}) collective-permute-start(bf16[512,512]{1,0:T(8,128)(2,1)S(1)} %north_kernel.1.refs_3_), channel_id=1, source_target_pairs={{0,8},{8,16},{16,24},{24,32},{32,40},{40,48},{48,56},{56,64},{64,7... | collective-permute-start | bytes 1572872 | tf_op jit(solution)/shard_map/ppermute | solution.py:334
  4.4 0.0 copy-start.3
  4.4 0.0 copy-start.7
  4.4 0.0 copy-start.8
  4.4 0.5 east_kernel.1
  4.9 0.0 collective-permute-start
  4.9 0.4 copy-done.2
  5.3 1.3 %table_kernel.1.refs_5_.refs_6_ = f32[64,48]{1,0:T(8,128)S(1)} custom-call(s32[1]{0:T(128)} %bitcast.refs_0_, s32[1]{0:T(128)} %bitcast.5.refs_0_.refs_1_, s32[32,16]{1,0:T(8,128)S(1)} %bitcast.35, s32[32,16]{1,0:T(8,128)S(1)} %bitcast.36, f32[153,153]{1,0:T(8,128)S(1)} %copy-done.2, bf16[1024,512]{1,0:T(8,128)(2,1)S(1)} %get-tuple-element.25.refs_5_.refs_2_), custom_call_target="tpu_custom_call" | custom-call | flops 1000 | bytes 1000 | tf_op jit(solution)/shard_map/table_kernel/pallas_call | solution.py:66
  6.7 0.0 copy-done
  6.7 0.7 %copy-done.7 = f32[1,1,1024,512]{3,2,1,0:T(8,128)S(1)} copy-done((f32[1,1,1024,512]{3,2,1,0:T(8,128)S(1)}, f32[1,1,1024,512]{3,2,1,0:T(8,128)}, u32[]{:S(2)}) %copy-start.7) | copy-done | bytes 2097176
  7.4 2.3 %early_a_kernel.1 = (f32[1024,512]{1,0:T(8,128)S(1)}, f32[8,1024]{1,0:T(8,128)S(1)}, bf16[8,2048]{1,0:T(8,128)(2,1)S(1)}) custom-call(bf16[1024,2048]{1,0:T(8,128)(2,1)S(1)} %bitcast.22, f32[1024,512]{1,0:T(8,128)S(1)} %bitcast.43, bf16[1024,512]{1,0:T(8,128)(2,1)S(1)} %get-tuple-element.25.refs_5_.refs_2_, bf16[4,2048]{1,0:T(4,128)(2,1)S(1)} %bitcast.31, ...), custom_call_target="tpu_custom_call" | custom-call | flops 10000001024 | bytes 30001000 | tf_op jit(solution)/shard_map/early_a_kernel/pallas_call | solution.py:66
  9.7 0.0 slice-start.1
  9.8 1.4 %early_b_kernel.1 = (f32[8,2048]{1,0:T(8,128)S(1)}, f32[8,512]{1,0:T(8,128)S(1)}) custom-call(f32[8,1024]{1,0:T(8,128)S(1)} %get-tuple-element.28.refs_0_, bf16[1024,1024]{1,0:T(8,128)(2,1)S(1)} %bitcast.29, bf16[1024,2048]{1,0:T(8,128)(2,1)S(1)} %bitcast.23, f32[1024,512]{1,0:T(8,128)S(1)} %bitcast.44), custom_call_target="tpu_custom_call" | custom-call | flops 10000001024 | bytes 30001000 | tf_op jit(solution)/shard_map/early_b_kernel/pallas_call | solution.py:66
  11.1 0.9 %slice-done.1 = s8[4194304]{0:T(1024)(128)(4,1)S(1)} async-done(((s8[8388608]{0:T(1024)(128)(4,1)}), s8[4194304]{0:T(1024)(128)(4,1)S(1)}, s32[]{:S(2)}) %slice-start.1) | async-done | bytes 4194328
  12.0 3.6 %early_c_kernel.1 = (f32[2048,512]{1,0:T(8,128)S(1)}, f32[8,512]{1,0:T(8,128)S(1)}, bf16[16,1024]{1,0:T(8,128)(2,1)S(1)}) custom-call(bf16[8,2048]{1,0:T(8,128)(2,1)S(1)} %get-tuple-element.27.refs_0_, bf16[2048,2048]{1,0:T(8,128)(2,1)S(1)} %bitcast.17, bf16[1024,512]{1,0:T(8,128)(2,1)S(1)} %get-tuple-element.25.refs_5_.refs_2_, ...), custom_call_target="tpu_custom_call" | custom-call | flops 10000001024 | bytes 30001000 | tf_op jit(solution)/shard_map/early_c_kernel/pallas_call | solution.py:66
  15.6 0.0 collective-permute-done.refs_6_
  15.6 1.8 %west_terms_kernel.1 = (f32[1024,512]{1,0:T(8,128)S(1)}, f32[2048,512]{1,0:T(8,128)S(1)}, f32[8,512]{1,0:T(8,128)S(1)}) custom-call(bf16[1024,2048]{1,0:T(8,128)(2,1)S(1)} %bitcast.24, bf16[2048,2048]{1,0:T(8,128)(2,1)S(1)} %bitcast.18, f32[1024,512]{1,0:T(8,128)S(1)} %get-tuple-element.26.refs_2_, f32[2048,512]{1,0:T(8,128)S(1)} %get-tuple-element.31.refs_3_, ...), custom_call_target="tpu_custom_call" | custom-call | flops 2000001024 | bytes 6001000 | tf_op jit(solution)/shard_map/west_terms_kernel/pallas_call | solution.py:66
  17.5 3.4 %collective-permute-done.1.refs_2_.refs_6_.refs_5_.refs_4_ = bf16[512,512]{1,0:T(8,128)(2,1)S(1)} collective-permute-done((bf16[512,512]{1,0:T(8,128)(2,1)S(1)}, bf16[512,512]{1,0:T(8,128)(2,1)S(1)}, u32[]{:S(2)}, u32[]{:S(2)}) %collective-permute-start.1) | collective-permute-done | bytes 524320 | tf_op jit(solution)/shard_map/ppermute | solution.py:334
  20.9 0.2 corner_kernel.1.refs_3_.refs_1_
  21.1 0.7 %inner_kernel.1.refs_3_.refs_4_ = bf16[1024,512]{1,0:T(8,128)(2,1)S(1)} custom-call(bf16[1024,2048]{1,0:T(8,128)(2,1)S(1)} %bitcast.25, f32[1024,512]{1,0:T(8,128)S(1)} %get-tuple-element.35.refs_1_, bf16[512,512]{1,0:T(8,128)(2,1)S(1)} %collective-permute-done.1.refs_2_.refs_6_.refs_5_.refs_4_, f32[8,512]{1,0:T(8,128)S(1)} %corner_kernel.1.refs_3_.refs_1_), custom_call_target="tpu_custom_call" | custom-call | flops 1000001024 | bytes 3001000 | tf_op jit(solution)/shard_map/inner_kernel/pallas_call | solution.py:66
  21.8 0.5 collective-permute-done.2.refs_2_
  22.3 0.1 collective-permute-start.5
  22.4 0.8 %collective-permute-start.4 = (f32[10,512]{1,0:T(8,128)S(1)}, f32[10,512]{1,0:T(8,128)S(1)}, u32[]{:S(2)}, u32[]{:S(2)}) collective-permute-start(f32[10,512]{1,0:T(8,128)S(1)} %pair_kernel.1.refs_8_.refs_1_), channel_id=1, source_target_pairs={{16,0},{24,8},{0,16},{8,24},{48,32},{56,40},{32,48},{40,56},{80,64... | collective-permute-start | bytes 61448 | tf_op jit(solution)/shard_map/ppermute | solution.py:338
  23.2 3.3 %collective-permute-start.3 = (f32[10,512]{1,0:T(8,128)S(1)}, f32[10,512]{1,0:T(8,128)S(1)}, u32[]{:S(2)}, u32[]{:S(2)}) collective-permute-start(f32[10,512]{1,0:T(8,128)S(1)} %pair_kernel.1.refs_8_.refs_1_), channel_id=1, source_target_pairs={{8,0},{0,8},{24,16},{16,24},{40,32},{32,40},{56,48},{48,56},{72,64... | collective-permute-start | bytes 61448 | tf_op jit(solution)/shard_map/ppermute | solution.py:338
  26.5 2.8 %solve_kernel.1 = (f32[1024,512]{1,0:T(8,128)}, bf16[528,512]{1,0:T(8,128)(2,1)S(1)}, bf16[1024,512]{1,0:T(8,128)(2,1)S(1)}) custom-call(s32[1]{0:T(128)} %bitcast.refs_0_, bf16[1024,2048]{1,0:T(8,128)(2,1)S(1)} %bitcast.26, bf16[1024,1024]{1,0:T(8,128)(2,1)S(1)} %bitcast.30, bf16[2048,2048]{1,0:T(8,128)(2,1)S(1)} %bitcast.19, ...), custom_call_target="tpu_custom_call" | custom-call | flops 4000001024 | bytes 12001000 | tf_op jit(solution)/shard_map/solve_kernel/pallas_call | solution.py:66
  29.2 1.8 %collective-permute-start.12 = (bf16[528,512]{1,0:T(8,128)(2,1)S(1)}, bf16[528,512]{1,0:T(8,128)(2,1)S(1)}, u32[]{:S(2)}, u32[]{:S(2)}) collective-permute-start(bf16[528,512]{1,0:T(8,128)(2,1)S(1)} %get-tuple-element.39.refs_5_), channel_id=1, source_target_pairs={{0,120},{8,0},{16,8},{24,16},{32,24},{40,32},{48,40},{56,48},{64,5... | collective-permute-start | bytes 1622024 | tf_op jit(solution)/shard_map/ppermute | solution.py:334
  31.0 0.0 collective-permute-done.5.refs_4_
  31.0 0.0 collective-permute-done.4.refs_3_
  31.1 3.0 %collective-permute-start.8 = (f32[19,512]{1,0:T(8,128)S(1)}, f32[19,512]{1,0:T(8,128)S(1)}, u32[]{:S(2)}, u32[]{:S(2)}) collective-permute-start(f32[19,512]{1,0:T(8,128)S(1)} %rows_kernel.1.refs_7_.refs_5_.refs_2_), channel_id=1, source_target_pairs={{6,0},{7,1},{4,2},{5,3},{2,4},{3,5},{0,6},{1,7},{14,8},{15,9},{12,... | collective-permute-start | bytes 116744 | tf_op jit(solution)/shard_map/ppermute | solution.py:338
  34.1 0.8 %collective-permute-start.7 = (f32[19,512]{1,0:T(8,128)S(1)}, f32[19,512]{1,0:T(8,128)S(1)}, u32[]{:S(2)}, u32[]{:S(2)}) collective-permute-start(f32[19,512]{1,0:T(8,128)S(1)} %rows_kernel.1.refs_7_.refs_5_.refs_2_), channel_id=1, source_target_pairs={{4,0},{5,1},{6,2},{7,3},{0,4},{1,5},{2,6},{3,7},{12,8},{13,9},{14,... | collective-permute-start | bytes 116744 | tf_op jit(solution)/shard_map/ppermute | solution.py:338
  34.9 0.5 %collective-permute-start.6 = (f32[19,512]{1,0:T(8,128)S(1)}, f32[19,512]{1,0:T(8,128)S(1)}, u32[]{:S(2)}, u32[]{:S(2)}) collective-permute-start(f32[19,512]{1,0:T(8,128)S(1)} %rows_kernel.1.refs_7_.refs_5_.refs_2_), channel_id=1, source_target_pairs={{2,0},{3,1},{0,2},{1,3},{6,4},{7,5},{4,6},{5,7},{10,8},{11,9},{8,1... | collective-permute-start | bytes 116744 | tf_op jit(solution)/shard_map/ppermute | solution.py:338
  35.5 1.0 %west_kernel.1.refs_6_ = bf16[528,512]{1,0:T(8,128)(2,1)S(1)} custom-call(s32[1]{0:T(128)} %bitcast.5.refs_0_.refs_1_, bf16[1024,2048]{1,0:T(8,128)(2,1)S(1)} %bitcast.27, bf16[2048,2048]{1,0:T(8,128)(2,1)S(1)} %bitcast.20, f32[2048,512]{1,0:T(8,128)S(1)} %get-tuple-element.37.refs_5_.refs_3_.refs_2_, ...), custom_call_target="tpu_custom_call" | custom-call | flops 1000001024 | bytes 3001000 | tf_op jit(solution)/shard_map/west_kernel/pallas_call | solution.py:66
  36.4 0.6 %collective-permute-start.13 = (bf16[528,512]{1,0:T(8,128)(2,1)S(1)}, bf16[528,512]{1,0:T(8,128)(2,1)S(1)}, u32[]{:S(2)}, u32[]{:S(2)}) collective-permute-start(bf16[528,512]{1,0:T(8,128)(2,1)S(1)} %west_kernel.1.refs_6_), channel_id=1, source_target_pairs={{0,7},{1,0},{2,1},{3,2},{4,3},{5,4},{6,5},{7,6},{8,15},{9,8},{10,9... | collective-permute-start | bytes 1622024 | tf_op jit(solution)/shard_map/ppermute | solution.py:334
  37.0 1.8 %kept_kernel.1.refs_7_.refs_0_.refs_5_ = f32[1024,512]{1,0:T(8,128)S(1)} custom-call(bf16[1024,2048]{1,0:T(8,128)(2,1)S(1)} %bitcast.28, bf16[2048,2048]{1,0:T(8,128)(2,1)S(1)} %bitcast.21, f32[2048,512]{1,0:T(8,128)S(1)} %get-tuple-element.37.refs_5_.refs_3_.refs_2_, bf16[1024,512]{1,0:T(8,128)(2,1)S(1)} %get-tuple-element.40.refs_4_.refs_3_, ...), custom_call_target="tpu_custom_call" | custom-call | flops 30000001024 | bytes 90001000 | tf_op jit(solution)/shard_map/kept_kernel/pallas_call | solution.py:66
  38.8 0.9 %collective-permute-done.7.refs_4_ = f32[19,512]{1,0:T(8,128)S(1)} collective-permute-done((f32[19,512]{1,0:T(8,128)S(1)}, f32[19,512]{1,0:T(8,128)S(1)}, u32[]{:S(2)}, u32[]{:S(2)}) %collective-permute-start.7) | collective-permute-done | bytes 38944 | tf_op jit(solution)/shard_map/ppermute | solution.py:338
  39.7 0.0 collective-permute-done.6.refs_3_
  39.7 0.2 columns_kernel.1
  40.0 0.8 %collective-permute-start.9 = (f32[16,512]{1,0:T(8,128)S(1)}, f32[16,512]{1,0:T(8,128)S(1)}, u32[]{:S(2)}, u32[]{:S(2)}) collective-permute-start(f32[16,512]{1,0:T(8,128)S(1)} %get-tuple-element.42), channel_id=1, source_target_pairs={{96,0},{104,8},{112,16},{120,24},{64,32},{72,40},{80,48},{88,56},{... | collective-permute-start | bytes 98312 | tf_op jit(solution)/shard_map/ppermute | solution.py:338
  40.8 1.1 %collective-permute-start.10 = (f32[16,512]{1,0:T(8,128)S(1)}, f32[16,512]{1,0:T(8,128)S(1)}, u32[]{:S(2)}, u32[]{:S(2)}) collective-permute-start(f32[16,512]{1,0:T(8,128)S(1)} %get-tuple-element.43), channel_id=1, source_target_pairs={{64,0},{72,8},{80,16},{88,24},{96,32},{104,40},{112,48},{120,56},{... | collective-permute-start | bytes 98312 | tf_op jit(solution)/shard_map/ppermute | solution.py:338
  41.9 2.2 %collective-permute-start.11 = (f32[16,512]{1,0:T(8,128)S(1)}, f32[16,512]{1,0:T(8,128)S(1)}, u32[]{:S(2)}, u32[]{:S(2)}) collective-permute-start(f32[16,512]{1,0:T(8,128)S(1)} %get-tuple-element.44), channel_id=1, source_target_pairs={{32,0},{40,8},{48,16},{56,24},{0,32},{8,40},{16,48},{24,56},{96,64... | collective-permute-start | bytes 98312 | tf_op jit(solution)/shard_map/ppermute | solution.py:338
  44.1 0.0 collective-permute-done.12.refs_1_.refs_8_
  44.1 0.4 base_kernel.1.refs_6_
  44.6 0.6 %collective-permute-done.9.refs_2_ = f32[16,512]{1,0:T(8,128)S(1)} collective-permute-done((f32[16,512]{1,0:T(8,128)S(1)}, f32[16,512]{1,0:T(8,128)S(1)}, u32[]{:S(2)}, u32[]{:S(2)}) %collective-permute-start.9) | collective-permute-done | bytes 32800 | tf_op jit(solution)/shard_map/ppermute | solution.py:338
  45.2 1.0 %collective-permute-done.10.refs_3_ = f32[16,512]{1,0:T(8,128)S(1)} collective-permute-done((f32[16,512]{1,0:T(8,128)S(1)}, f32[16,512]{1,0:T(8,128)S(1)}, u32[]{:S(2)}, u32[]{:S(2)}) %collective-permute-start.10) | collective-permute-done | bytes 32800 | tf_op jit(solution)/shard_map/ppermute | solution.py:338
  46.2 0.2 collective-permute-done.11.refs_4_
  46.4 2.3 %final_kernel.1 = (f32[2,512,512]{2,1,0:T(8,128)}, f32[4,512]{1,0:T(4,128)}) custom-call(s32[1]{0:T(128)} %bitcast.refs_0_, f32[16,512]{1,0:T(8,128)S(1)} %get-tuple-element.41.refs_3_.refs_1_, f32[16,512]{1,0:T(8,128)S(1)} %collective-permute-done.9.refs_2_, f32[16,512]{1,0:T(8,128)S(1)} %collective-permute-done.10.refs_3_, ...), custom_call_target="tpu_custom_call" | custom-call | flops 1000 | bytes 1000 | tf_op jit(solution)/shard_map/final_kernel/pallas_call | solution.py:66
  (21 shorter events, 0.1 us)
Async XLA Ops:
  0.6 1.4 %copy-start.5 = (f32[1,1,2,512]{3,2,1,0:T(2,128)S(1)}, f32[1,1,2,512]{3,2,1,0:T(2,128)}, u32[]{:S(2)}) copy-start(f32[1,1,2,512]{3,2,1,0:T(2,128)} %param.12) | copy-start | bytes 12292
  0.6 3.8 %copy-start.6 = (f32[1,1,2,512,512]{4,3,2,1,0:T(8,128)S(1)}, f32[1,1,2,512,512]{4,3,2,1,0:T(8,128)}, u32[]{:S(2)}) copy-start(f32[1,1,2,512,512]{4,3,2,1,0:T(8,128)} %param.11) | copy-start | bytes 6291460
  2.3 18.6 %collective-permute-start.1 = (bf16[512,512]{1,0:T(8,128)(2,1)S(1)}, bf16[512,512]{1,0:T(8,128)(2,1)S(1)}, u32[]{:S(2)}, u32[]{:S(2)}) collective-permute-start(bf16[512,512]{1,0:T(8,128)(2,1)S(1)} %north_kernel.1.refs_3_), channel_id=1, source_target_pairs={{0,8},{8,16},{16,24},{24,32},{32,40},{40,48},{48,56},{56,64},{64,7... | collective-permute-start | bytes 1572872 | tf_op jit(solution)/shard_map/ppermute | solution.py:334
  4.4 0.9 %copy-start.2 = (f32[153,153]{1,0:T(8,128)S(1)}, f32[153,153]{1,0:T(8,128)}, u32[]{:S(2)}) copy-start(f32[153,153]{1,0:T(8,128)} %refs_4_.1) | copy-start | bytes 280912
  4.4 0.9 %copy-start.4 = (s32[16,8,4]{0,2,1:T(4,128)S(1)}, s32[16,8,4]{0,2,1:T(4,128)}, u32[]{:S(2)}) copy-start(s32[16,8,4]{0,2,1:T(4,128)} %param.18) | copy-start | bytes 6148
  4.4 2.3 %copy-start = (bf16[1,1,1024,2048]{3,2,1,0:T(8,128)(2,1)S(1)}, bf16[1,1,1024,2048]{3,2,1,0:T(8,128)(2,1)}, u32[]{:S(2)}) copy-start(bf16[1,1,1024,2048]{3,2,1,0:T(8,128)(2,1)} %param.14) | copy-start | bytes 12582916
  4.4 2.3 %copy-start.3 = (bf16[1,1,4,2048]{3,2,1,0:T(4,128)(2,1)S(1)}, bf16[1,1,4,2048]{3,2,1,0:T(4,128)(2,1)}, u32[]{:S(2)}) copy-start(bf16[1,1,4,2048]{3,2,1,0:T(4,128)(2,1)} %param.16) | copy-start | bytes 49156
  4.4 3.0 %copy-start.7 = (f32[1,1,1024,512]{3,2,1,0:T(8,128)S(1)}, f32[1,1,1024,512]{3,2,1,0:T(8,128)}, u32[]{:S(2)}) copy-start(f32[1,1,1024,512]{3,2,1,0:T(8,128)} %param.10) | copy-start | bytes 6291460
  4.4 3.0 %copy-start.8 = (s32[1,1,4,512]{3,2,1,0:T(4,128)S(1)}, s32[1,1,4,512]{3,2,1,0:T(4,128)}, u32[]{:S(2)}) copy-start(s32[1,1,4,512]{3,2,1,0:T(4,128)} %param.19) | copy-start | bytes 24580
  4.9 10.7 %collective-permute-start = (bf16[512,512]{1,0:T(8,128)(2,1)S(1)}, bf16[512,512]{1,0:T(8,128)(2,1)S(1)}, u32[]{:S(2)}, u32[]{:S(2)}) collective-permute-start(bf16[512,512]{1,0:T(8,128)(2,1)S(1)} %get-tuple-element.34), channel_id=1, source_target_pairs={{0,1},{1,2},{2,3},{3,4},{4,5},{5,6},{6,7},{7,0},{8,9},{9,10},{10,1... | collective-permute-start | bytes 1572872 | tf_op jit(solution)/shard_map/ppermute | solution.py:334
  7.4 2.3 %copy-start.1 = (bf16[1,1,1024,1024]{3,2,1,0:T(8,128)(2,1)S(1)}, bf16[1,1,1024,1024]{3,2,1,0:T(8,128)(2,1)}, u32[]{:S(2)}) copy-start(bf16[1,1,1024,1024]{3,2,1,0:T(8,128)(2,1)} %param.13) | copy-start | bytes 6291460
  7.4 3.7 %slice-start = ((s8[8388608]{0:T(1024)(128)(4,1)}), s8[4194304]{0:T(1024)(128)(4,1)S(1)}, s32[]{:S(2)}) async-start(s8[8388608]{0:T(1024)(128)(4,1)} %bitcast.15), calls=%async_computation | async-start | bytes 8388608
  9.7 2.3 %slice-start.1 = ((s8[8388608]{0:T(1024)(128)(4,1)}), s8[4194304]{0:T(1024)(128)(4,1)S(1)}, s32[]{:S(2)}) async-start(s8[8388608]{0:T(1024)(128)(4,1)} %bitcast.15), calls=%async_computation.1 | async-start | bytes 8388608
  21.1 1.2 %collective-permute-start.2 = (f32[8,512]{1,0:T(8,128)S(1)}, f32[8,512]{1,0:T(8,128)S(1)}, u32[]{:S(2)}, u32[]{:S(2)}) collective-permute-start(f32[8,512]{1,0:T(8,128)S(1)} %corner_kernel.1.refs_3_.refs_1_), channel_id=1, source_target_pairs={{0,1},{1,0},{2,3},{3,2},{4,5},{5,4},{6,7},{7,6},{8,9},{9,8},{10,11... | collective-permute-start | bytes 49160 | tf_op jit(solution)/shard_map/ppermute | solution.py:397
  22.3 8.8 %collective-permute-start.5 = (f32[10,512]{1,0:T(8,128)S(1)}, f32[10,512]{1,0:T(8,128)S(1)}, u32[]{:S(2)}, u32[]{:S(2)}) collective-permute-start(f32[10,512]{1,0:T(8,128)S(1)} %pair_kernel.1.refs_8_.refs_1_), channel_id=1, source_target_pairs={{24,0},{16,8},{8,16},{0,24},{56,32},{48,40},{40,48},{32,56},{88,64... | collective-permute-start | bytes 61448 | tf_op jit(solution)/shard_map/ppermute | solution.py:338
  22.4 8.7 %collective-permute-start.4 = (f32[10,512]{1,0:T(8,128)S(1)}, f32[10,512]{1,0:T(8,128)S(1)}, u32[]{:S(2)}, u32[]{:S(2)}) collective-permute-start(f32[10,512]{1,0:T(8,128)S(1)} %pair_kernel.1.refs_8_.refs_1_), channel_id=1, source_target_pairs={{16,0},{24,8},{0,16},{8,24},{48,32},{56,40},{32,48},{40,56},{80,64... | collective-permute-start | bytes 61448 | tf_op jit(solution)/shard_map/ppermute | solution.py:338
  23.2 7.9 %collective-permute-start.3 = (f32[10,512]{1,0:T(8,128)S(1)}, f32[10,512]{1,0:T(8,128)S(1)}, u32[]{:S(2)}, u32[]{:S(2)}) collective-permute-start(f32[10,512]{1,0:T(8,128)S(1)} %pair_kernel.1.refs_8_.refs_1_), channel_id=1, source_target_pairs={{8,0},{0,8},{24,16},{16,24},{40,32},{32,40},{56,48},{48,56},{72,64... | collective-permute-start | bytes 61448 | tf_op jit(solution)/shard_map/ppermute | solution.py:338
  29.2 14.9 %collective-permute-start.12 = (bf16[528,512]{1,0:T(8,128)(2,1)S(1)}, bf16[528,512]{1,0:T(8,128)(2,1)S(1)}, u32[]{:S(2)}, u32[]{:S(2)}) collective-permute-start(bf16[528,512]{1,0:T(8,128)(2,1)S(1)} %get-tuple-element.39.refs_5_), channel_id=1, source_target_pairs={{0,120},{8,0},{16,8},{24,16},{32,24},{40,32},{48,40},{56,48},{64,5... | collective-permute-start | bytes 1622024 | tf_op jit(solution)/shard_map/ppermute | solution.py:334
  31.1 7.7 %collective-permute-start.8 = (f32[19,512]{1,0:T(8,128)S(1)}, f32[19,512]{1,0:T(8,128)S(1)}, u32[]{:S(2)}, u32[]{:S(2)}) collective-permute-start(f32[19,512]{1,0:T(8,128)S(1)} %rows_kernel.1.refs_7_.refs_5_.refs_2_), channel_id=1, source_target_pairs={{6,0},{7,1},{4,2},{5,3},{2,4},{3,5},{0,6},{1,7},{14,8},{15,9},{12,... | collective-permute-start | bytes 116744 | tf_op jit(solution)/shard_map/ppermute | solution.py:338
  34.1 5.6 %collective-permute-start.7 = (f32[19,512]{1,0:T(8,128)S(1)}, f32[19,512]{1,0:T(8,128)S(1)}, u32[]{:S(2)}, u32[]{:S(2)}) collective-permute-start(f32[19,512]{1,0:T(8,128)S(1)} %rows_kernel.1.refs_7_.refs_5_.refs_2_), channel_id=1, source_target_pairs={{4,0},{5,1},{6,2},{7,3},{0,4},{1,5},{2,6},{3,7},{12,8},{13,9},{14,... | collective-permute-start | bytes 116744 | tf_op jit(solution)/shard_map/ppermute | solution.py:338
  34.9 4.8 %collective-permute-start.6 = (f32[19,512]{1,0:T(8,128)S(1)}, f32[19,512]{1,0:T(8,128)S(1)}, u32[]{:S(2)}, u32[]{:S(2)}) collective-permute-start(f32[19,512]{1,0:T(8,128)S(1)} %rows_kernel.1.refs_7_.refs_5_.refs_2_), channel_id=1, source_target_pairs={{2,0},{3,1},{0,2},{1,3},{6,4},{7,5},{4,6},{5,7},{10,8},{11,9},{8,1... | collective-permute-start | bytes 116744 | tf_op jit(solution)/shard_map/ppermute | solution.py:338
  36.4 9.9 %collective-permute-start.13 = (bf16[528,512]{1,0:T(8,128)(2,1)S(1)}, bf16[528,512]{1,0:T(8,128)(2,1)S(1)}, u32[]{:S(2)}, u32[]{:S(2)}) collective-permute-start(bf16[528,512]{1,0:T(8,128)(2,1)S(1)} %west_kernel.1.refs_6_), channel_id=1, source_target_pairs={{0,7},{1,0},{2,1},{3,2},{4,3},{5,4},{6,5},{7,6},{8,15},{9,8},{10,9... | collective-permute-start | bytes 1622024 | tf_op jit(solution)/shard_map/ppermute | solution.py:334
  40.0 5.2 %collective-permute-start.9 = (f32[16,512]{1,0:T(8,128)S(1)}, f32[16,512]{1,0:T(8,128)S(1)}, u32[]{:S(2)}, u32[]{:S(2)}) collective-permute-start(f32[16,512]{1,0:T(8,128)S(1)} %get-tuple-element.42), channel_id=1, source_target_pairs={{96,0},{104,8},{112,16},{120,24},{64,32},{72,40},{80,48},{88,56},{... | collective-permute-start | bytes 98312 | tf_op jit(solution)/shard_map/ppermute | solution.py:338
  40.8 5.4 %collective-permute-start.10 = (f32[16,512]{1,0:T(8,128)S(1)}, f32[16,512]{1,0:T(8,128)S(1)}, u32[]{:S(2)}, u32[]{:S(2)}) collective-permute-start(f32[16,512]{1,0:T(8,128)S(1)} %get-tuple-element.43), channel_id=1, source_target_pairs={{64,0},{72,8},{80,16},{88,24},{96,32},{104,40},{112,48},{120,56},{... | collective-permute-start | bytes 98312 | tf_op jit(solution)/shard_map/ppermute | solution.py:338
  41.9 4.4 %collective-permute-start.11 = (f32[16,512]{1,0:T(8,128)S(1)}, f32[16,512]{1,0:T(8,128)S(1)}, u32[]{:S(2)}, u32[]{:S(2)}) collective-permute-start(f32[16,512]{1,0:T(8,128)S(1)} %get-tuple-element.44), channel_id=1, source_target_pairs={{32,0},{40,8},{48,16},{56,24},{0,32},{8,40},{16,48},{24,56},{96,64... | collective-permute-start | bytes 98312 | tf_op jit(solution)/shard_map/ppermute | solution.py:338

commit v6 on v5

--- a/solution.py
+++ b/solution.py
@@ -83,19 +83,38 @@
 
 def north_face(i, faces, w):
     face = call(load_kernel, shape(FACE, F32), [ANY], VMEM, [pltpu.SemaphoreType.DMA(())], vmem=52, cost=4)(faces)
-    return call(north_kernel, shape(FACE, BF16), [SMEM, VMEM, VMEM], VMEM)(i, face, w)
-
-
-def east_kernel(pos, faces, w, out, own):
+    return call(north_kernel, shape(FACE, BF16), [SMEM, VMEM, VMEM], VMEM)(i, face, w), face
+
+
+def east_kernel(pos, faces, north, w, out, own, face, sem):
+    rows = FACE // 2
+    copies = [
+        pltpu.make_async_copy(faces.at[0, pl.ds(c * rows, rows)], face.at[pl.ds(c * rows, rows)], sem.at[c])
+        for c in range(2)
+    ]
+    for copy in copies:
+        copy.start()
+    own[FACE:] = (column(w[1:2, :]) * north[...]).astype(BF16)
     keep = (pos[0] < COLS - 1).astype(F32)
-    c = column(w[0:1, :])
-    out[...] = ((1.0 - c) * keep * faces[0]).astype(BF16)
-    own[:FACE] = (c * faces[0]).astype(BF16)
-    own[FACE:] = (column(w[1:2, :]) * faces[1]).astype(BF16)
-
-
-def east_face(j, faces, w, after):
-    return call(east_kernel, (shape(FACE, BF16), shape(2 * FACE, BF16)), [SMEM, VMEM, VMEM], (VMEM, VMEM), after=after, cost=4)(j, faces, w)
+    wc = column(w[0:1, :])
+    for c, copy in enumerate(copies):
+        copy.wait()
+        at = slice(c * rows, (c + 1) * rows)
+        out[at] = ((1.0 - wc[at]) * keep * face[at]).astype(BF16)
+        own[at] = (wc[at] * face[at]).astype(BF16)
+
+
+def east_face(j, faces, north, w, after):
+    return call(
+        east_kernel,
+        (shape(FACE, BF16), shape(2 * FACE, BF16)),
+        [SMEM, ANY, VMEM, VMEM],
+        (VMEM, VMEM),
+        [pltpu.VMEM((FACE, RHS), F32), pltpu.SemaphoreType.DMA((2,))],
+        after=after,
+        vmem=50,
+        cost=4,
+    )(j, faces, north, w)
 
 
 def table_kernel(i, j, cm, cmv, cinv, out, rows, lat):
@@ -363,9 +382,9 @@
     inv, coup, block = interior_inverse_block[0, 0], coupling[0, 0], interface_block[0, 0]
     basis = corner_trace_basis[0, 0]
 
-    to_north = north_face(i, faces_in, w)
+    to_north, north = north_face(i, faces_in, w)
     south = along(to_north, "row", 1)
-    to_east, own = east_face(j, faces_in, w, (to_north,))
+    to_east, own = east_face(j, faces_in, north, w, (to_north,))
     west = along(to_east, "col", 1)
     e = table(i, j, corner_map, coarse_inv, (own,))
     p, g, bt = call(

time: 49 us -> 51.3 us (1.047); the launches traced: 48.8 us -> 50.5 us
  waiting for transfers between devices: 6.63 us -> 4.64 us
  starting transfers between devices: 17.2 us -> 19.1 us
  Pallas kernels: 22 us -> 22.9 us
  local copies, waits for them, and re-layouts: 2.05 us -> 2.81 us
    ppermute x4, starting transfers between devices: 4.47 us -> 6.41 us  [along(): return lax.ppermute(x, axis, [(s, (s + d) % n) for s in range(n)])]
    ppermute x4, waiting for transfers between devices: 3.43 us -> 1.63 us  [along(): return lax.ppermute(x, axis, [(s, (s + d) % n) for s in range(n)])]
    pallas_call x18, Pallas kernels: 22 us -> 22.9 us  [call(): return lambda *args: run(*args, *after)]
    unnamed x22, local copies, waits for them, and re-layouts: 2.05 us -> 2.81 us
  transfers between devices with their start and end apart: 14 -> 14, of which waited for: 6 -> 7; matrix products, arithmetic and copies ran while one was open for 0% -> 0% of each run, Pallas kernels for 37% -> 37%
where the time goes in v6:
time: 51.3 us; the launch traced here: 50.5 us
  Pallas kernels  22.9 us (45%)
  starting transfers between devices  19.1 us (37%)
  waiting for transfers between devices  4.64 us (9%)
  local copies, waits for them, and re-layouts  2.81 us (5%)
  between operations  1.05 us (2%)
    pallas_call x18, Pallas kernels, call(): return lambda *args: run(*args, *after)  22.9 us
    ppermute x9, starting transfers between devices, exchanged(): lax.ppermute(x, axis, [(d ^ k * stride, d) for d in range(lax.axis_size(a...  12.7 us
    ppermute x4, starting transfers between devices, along(): return lax.ppermute(x, axis, [(s, (s + d) % n) for s in range(n)])  6.41 us
    unnamed x22, local copies, waits for them, and re-layouts  2.81 us
    ppermute x9, waiting for transfers between devices, exchanged(): lax.ppermute(x, axis, [(d ^ k * stride, d) for d in range(lax.axis_size(a...  2.55 us
    ppermute x4, waiting for transfers between devices, along(): return lax.ppermute(x, axis, [(s, (s + d) % n) for s in range(n)])  1.63 us
  transfers between devices with their start and end apart: 14, of which 7 were waited for; matrix products, arithmetic and copies ran while one was open for 0% of the time, Pallas kernels for 37%

profile of v6, /device:TPU:0, one launch (start us, length us, event | category | flops | bytes accessed | tf_op | source)
XLA Modules:
  0.0 50.5 jit_solution(3275444637995717233)
XLA Ops:
  0.6 1.2 %load_kernel.1.refs_1_.refs_2_ = f32[512,512]{1,0:T(8,128)S(1)} custom-call(f32[2,512,512]{2,1,0:T(8,128)} %bitcast.44), custom_call_target="tpu_custom_call" | custom-call | flops 4000001024 | bytes 12001000 | tf_op jit(solution)/shard_map/load_kernel/pallas_call | solution.py:66
  1.9 0.3 north_kernel.1.refs_4_
  2.2 2.1 %collective-permute-start.1 = (bf16[512,512]{1,0:T(8,128)(2,1)S(1)}, bf16[512,512]{1,0:T(8,128)(2,1)S(1)}, u32[]{:S(2)}, u32[]{:S(2)}) collective-permute-start(bf16[512,512]{1,0:T(8,128)(2,1)S(1)} %north_kernel.1.refs_4_), channel_id=1, source_target_pairs={{0,8},{8,16},{16,24},{24,32},{32,40},{40,48},{48,56},{56,64},{64,7... | collective-permute-start | bytes 1572872 | tf_op jit(solution)/shard_map/ppermute | solution.py:353
  4.3 0.0 copy-start.8
  4.3 1.5 %east_kernel.1 = (bf16[512,512]{1,0:T(8,128)(2,1)S(1)}, bf16[1024,512]{1,0:T(8,128)(2,1)S(1)}) custom-call(s32[1]{0:T(128)} %bitcast.5.refs_0_.refs_1_, f32[2,512,512]{2,1,0:T(8,128)} %bitcast.45, f32[512,512]{1,0:T(8,128)S(1)} %load_kernel.1.refs_1_.refs_2_, f32[2,512]{1,0:T(2,128)S(1)} %bitcast.38, bf16[512,512]{1,0:T(8,128)(2,1)S(1)} %north_kernel.1.refs_4_), custom_call_target="tpu_custom_call" | custom-call | flops 4000001024 | bytes 12001000 | tf_op jit(solution)/shard_map/east_kernel/pallas_call | solution.py:66
  5.8 0.0 collective-permute-start
  5.8 1.3 %table_kernel.1.refs_5_.refs_6_ = f32[64,48]{1,0:T(8,128)S(1)} custom-call(s32[1]{0:T(128)} %bitcast.refs_0_, s32[1]{0:T(128)} %bitcast.5.refs_0_.refs_1_, s32[32,16]{1,0:T(8,128)S(1)} %bitcast.35, s32[32,16]{1,0:T(8,128)S(1)} %bitcast.36, f32[153,153]{1,0:T(8,128)S(1)} %copy-done.2, bf16[1024,512]{1,0:T(8,128)(2,1)S(1)} %get-tuple-element.25.refs_5_.refs_2_), custom_call_target="tpu_custom_call" | custom-call | flops 1000 | bytes 1000 | tf_op jit(solution)/shard_map/table_kernel/pallas_call | solution.py:66
  7.2 0.0 copy-start.6
  7.2 1.6 %copy-done.6 = f32[1,1,1024,512]{3,2,1,0:T(8,128)S(1)} copy-done((f32[1,1,1024,512]{3,2,1,0:T(8,128)S(1)}, f32[1,1,1024,512]{3,2,1,0:T(8,128)}, u32[]{:S(2)}) %copy-start.6) | copy-done | bytes 2097176
  8.8 2.3 %early_a_kernel.1 = (f32[1024,512]{1,0:T(8,128)S(1)}, f32[8,1024]{1,0:T(8,128)S(1)}, bf16[8,2048]{1,0:T(8,128)(2,1)S(1)}) custom-call(bf16[1024,2048]{1,0:T(8,128)(2,1)S(1)} %bitcast.22, f32[1024,512]{1,0:T(8,128)S(1)} %bitcast.41, bf16[1024,512]{1,0:T(8,128)(2,1)S(1)} %get-tuple-element.25.refs_5_.refs_2_, bf16[4,2048]{1,0:T(4,128)(2,1)S(1)} %bitcast.31, ...), custom_call_target="tpu_custom_call" | custom-call | flops 10000001024 | bytes 30001000 | tf_op jit(solution)/shard_map/early_a_kernel/pallas_call | solution.py:66
  11.2 0.0 slice-start.1
  11.2 1.3 %early_b_kernel.1 = (f32[8,2048]{1,0:T(8,128)S(1)}, f32[8,512]{1,0:T(8,128)S(1)}) custom-call(f32[8,1024]{1,0:T(8,128)S(1)} %get-tuple-element.28.refs_0_, bf16[1024,1024]{1,0:T(8,128)(2,1)S(1)} %bitcast.29, bf16[1024,2048]{1,0:T(8,128)(2,1)S(1)} %bitcast.23, f32[1024,512]{1,0:T(8,128)S(1)} %bitcast.42), custom_call_target="tpu_custom_call" | custom-call | flops 10000001024 | bytes 30001000 | tf_op jit(solution)/shard_map/early_b_kernel/pallas_call | solution.py:66
  12.5 1.2 %slice-done.1 = s8[4194304]{0:T(1024)(128)(4,1)S(1)} async-done(((s8[8388608]{0:T(1024)(128)(4,1)}), s8[4194304]{0:T(1024)(128)(4,1)S(1)}, s32[]{:S(2)}) %slice-start.1) | async-done | bytes 4194328
  13.7 3.6 %early_c_kernel.1 = (f32[2048,512]{1,0:T(8,128)S(1)}, f32[8,512]{1,0:T(8,128)S(1)}, bf16[16,1024]{1,0:T(8,128)(2,1)S(1)}) custom-call(bf16[8,2048]{1,0:T(8,128)(2,1)S(1)} %get-tuple-element.27.refs_0_, bf16[2048,2048]{1,0:T(8,128)(2,1)S(1)} %bitcast.17, bf16[1024,512]{1,0:T(8,128)(2,1)S(1)} %get-tuple-element.25.refs_5_.refs_2_, ...), custom_call_target="tpu_custom_call" | custom-call | flops 10000001024 | bytes 30001000 | tf_op jit(solution)/shard_map/early_c_kernel/pallas_call | solution.py:66
  17.3 0.0 collective-permute-done.refs_6_
  17.3 1.8 %west_terms_kernel.1 = (f32[1024,512]{1,0:T(8,128)S(1)}, f32[2048,512]{1,0:T(8,128)S(1)}, f32[8,512]{1,0:T(8,128)S(1)}) custom-call(bf16[1024,2048]{1,0:T(8,128)(2,1)S(1)} %bitcast.24, bf16[2048,2048]{1,0:T(8,128)(2,1)S(1)} %bitcast.18, f32[1024,512]{1,0:T(8,128)S(1)} %get-tuple-element.26.refs_2_, f32[2048,512]{1,0:T(8,128)S(1)} %get-tuple-element.31.refs_3_, ...), custom_call_target="tpu_custom_call" | custom-call | flops 2000001024 | bytes 6001000 | tf_op jit(solution)/shard_map/west_terms_kernel/pallas_call | solution.py:66
  19.1 1.6 %collective-permute-done.1.refs_2_.refs_6_.refs_5_.refs_4_ = bf16[512,512]{1,0:T(8,128)(2,1)S(1)} collective-permute-done((bf16[512,512]{1,0:T(8,128)(2,1)S(1)}, bf16[512,512]{1,0:T(8,128)(2,1)S(1)}, u32[]{:S(2)}, u32[]{:S(2)}) %collective-permute-start.1) | collective-permute-done | bytes 524320 | tf_op jit(solution)/shard_map/ppermute | solution.py:353
  20.7 0.2 corner_kernel.1.refs_3_.refs_1_
  20.9 0.0 collective-permute-start.2
  20.9 0.7 %inner_kernel.1.refs_3_.refs_4_ = bf16[1024,512]{1,0:T(8,128)(2,1)S(1)} custom-call(bf16[1024,2048]{1,0:T(8,128)(2,1)S(1)} %bitcast.25, f32[1024,512]{1,0:T(8,128)S(1)} %get-tuple-element.35.refs_1_, bf16[512,512]{1,0:T(8,128)(2,1)S(1)} %collective-permute-done.1.refs_2_.refs_6_.refs_5_.refs_4_, f32[8,512]{1,0:T(8,128)S(1)} %corner_kernel.1.refs_3_.refs_1_), custom_call_target="tpu_custom_call" | custom-call | flops 1000001024 | bytes 3001000 | tf_op jit(solution)/shard_map/inner_kernel/pallas_call | solution.py:66
  21.6 0.5 collective-permute-done.2.refs_2_
  22.1 2.0 %collective-permute-start.5 = (f32[10,512]{1,0:T(8,128)S(1)}, f32[10,512]{1,0:T(8,128)S(1)}, u32[]{:S(2)}, u32[]{:S(2)}) collective-permute-start(f32[10,512]{1,0:T(8,128)S(1)} %pair_kernel.1.refs_8_.refs_1_), channel_id=1, source_target_pairs={{24,0},{16,8},{8,16},{0,24},{56,32},{48,40},{40,48},{32,56},{88,64... | collective-permute-start | bytes 61448 | tf_op jit(solution)/shard_map/ppermute | solution.py:357
  24.2 1.6 %collective-permute-start.4 = (f32[10,512]{1,0:T(8,128)S(1)}, f32[10,512]{1,0:T(8,128)S(1)}, u32[]{:S(2)}, u32[]{:S(2)}) collective-permute-start(f32[10,512]{1,0:T(8,128)S(1)} %pair_kernel.1.refs_8_.refs_1_), channel_id=1, source_target_pairs={{16,0},{24,8},{0,16},{8,24},{48,32},{56,40},{32,48},{40,56},{80,64... | collective-permute-start | bytes 61448 | tf_op jit(solution)/shard_map/ppermute | solution.py:357
  25.8 0.5 collective-permute-start.3
  26.3 2.8 %solve_kernel.1 = (f32[1024,512]{1,0:T(8,128)}, bf16[528,512]{1,0:T(8,128)(2,1)S(1)}, bf16[1024,512]{1,0:T(8,128)(2,1)S(1)}) custom-call(s32[1]{0:T(128)} %bitcast.refs_0_, bf16[1024,2048]{1,0:T(8,128)(2,1)S(1)} %bitcast.26, bf16[1024,1024]{1,0:T(8,128)(2,1)S(1)} %bitcast.30, bf16[2048,2048]{1,0:T(8,128)(2,1)S(1)} %bitcast.19, ...), custom_call_target="tpu_custom_call" | custom-call | flops 4000001024 | bytes 12001000 | tf_op jit(solution)/shard_map/solve_kernel/pallas_call | solution.py:66
  29.1 4.3 %collective-permute-start.12 = (bf16[528,512]{1,0:T(8,128)(2,1)S(1)}, bf16[528,512]{1,0:T(8,128)(2,1)S(1)}, u32[]{:S(2)}, u32[]{:S(2)}) collective-permute-start(bf16[528,512]{1,0:T(8,128)(2,1)S(1)} %get-tuple-element.39.refs_5_), channel_id=1, source_target_pairs={{0,120},{8,0},{16,8},{24,16},{32,24},{40,32},{48,40},{56,48},{64,5... | collective-permute-start | bytes 1622024 | tf_op jit(solution)/shard_map/ppermute | solution.py:353
  33.4 0.0 collective-permute-done.5.refs_4_
  33.4 0.0 collective-permute-done.4.refs_3_
  33.4 0.0 collective-permute-done.3.refs_2_
  33.5 2.0 %collective-permute-start.8 = (f32[19,512]{1,0:T(8,128)S(1)}, f32[19,512]{1,0:T(8,128)S(1)}, u32[]{:S(2)}, u32[]{:S(2)}) collective-permute-start(f32[19,512]{1,0:T(8,128)S(1)} %rows_kernel.1.refs_7_.refs_5_.refs_2_), channel_id=1, source_target_pairs={{6,0},{7,1},{4,2},{5,3},{2,4},{3,5},{0,6},{1,7},{14,8},{15,9},{12,... | collective-permute-start | bytes 116744 | tf_op jit(solution)/shard_map/ppermute | solution.py:357
  35.5 1.8 %collective-permute-start.7 = (f32[19,512]{1,0:T(8,128)S(1)}, f32[19,512]{1,0:T(8,128)S(1)}, u32[]{:S(2)}, u32[]{:S(2)}) collective-permute-start(f32[19,512]{1,0:T(8,128)S(1)} %rows_kernel.1.refs_7_.refs_5_.refs_2_), channel_id=1, source_target_pairs={{4,0},{5,1},{6,2},{7,3},{0,4},{1,5},{2,6},{3,7},{12,8},{13,9},{14,... | collective-permute-start | bytes 116744 | tf_op jit(solution)/shard_map/ppermute | solution.py:357
  37.3 0.5 %collective-permute-start.6 = (f32[19,512]{1,0:T(8,128)S(1)}, f32[19,512]{1,0:T(8,128)S(1)}, u32[]{:S(2)}, u32[]{:S(2)}) collective-permute-start(f32[19,512]{1,0:T(8,128)S(1)} %rows_kernel.1.refs_7_.refs_5_.refs_2_), channel_id=1, source_target_pairs={{2,0},{3,1},{0,2},{1,3},{6,4},{7,5},{4,6},{5,7},{10,8},{11,9},{8,1... | collective-permute-start | bytes 116744 | tf_op jit(solution)/shard_map/ppermute | solution.py:357
  37.8 1.0 %west_kernel.1.refs_6_ = bf16[528,512]{1,0:T(8,128)(2,1)S(1)} custom-call(s32[1]{0:T(128)} %bitcast.5.refs_0_.refs_1_, bf16[1024,2048]{1,0:T(8,128)(2,1)S(1)} %bitcast.27, bf16[2048,2048]{1,0:T(8,128)(2,1)S(1)} %bitcast.20, f32[2048,512]{1,0:T(8,128)S(1)} %get-tuple-element.37.refs_5_.refs_3_.refs_2_, ...), custom_call_target="tpu_custom_call" | custom-call | flops 1000001024 | bytes 3001000 | tf_op jit(solution)/shard_map/west_kernel/pallas_call | solution.py:66
  38.8 0.0 collective-permute-start.13
  38.8 1.8 %kept_kernel.1.refs_7_.refs_0_.refs_5_ = f32[1024,512]{1,0:T(8,128)S(1)} custom-call(bf16[1024,2048]{1,0:T(8,128)(2,1)S(1)} %bitcast.28, bf16[2048,2048]{1,0:T(8,128)(2,1)S(1)} %bitcast.21, f32[2048,512]{1,0:T(8,128)S(1)} %get-tuple-element.37.refs_5_.refs_3_.refs_2_, bf16[1024,512]{1,0:T(8,128)(2,1)S(1)} %get-tuple-element.40.refs_4_.refs_3_, ...), custom_call_target="tpu_custom_call" | custom-call | flops 30000001024 | bytes 90001000 | tf_op jit(solution)/shard_map/kept_kernel/pallas_call | solution.py:66
  40.6 0.4 collective-permute-done.7.refs_4_
  41.0 0.3 collective-permute-done.6.refs_3_
  41.4 0.2 columns_kernel.1
  41.6 0.8 %collective-permute-start.9 = (f32[16,512]{1,0:T(8,128)S(1)}, f32[16,512]{1,0:T(8,128)S(1)}, u32[]{:S(2)}, u32[]{:S(2)}) collective-permute-start(f32[16,512]{1,0:T(8,128)S(1)} %get-tuple-element.42), channel_id=1, source_target_pairs={{96,0},{104,8},{112,16},{120,24},{64,32},{72,40},{80,48},{88,56},{... | collective-permute-start | bytes 98312 | tf_op jit(solution)/shard_map/ppermute | solution.py:357
  42.4 0.5 collective-permute-start.10
  42.9 2.8 %collective-permute-start.11 = (f32[16,512]{1,0:T(8,128)S(1)}, f32[16,512]{1,0:T(8,128)S(1)}, u32[]{:S(2)}, u32[]{:S(2)}) collective-permute-start(f32[16,512]{1,0:T(8,128)S(1)} %get-tuple-element.44), channel_id=1, source_target_pairs={{32,0},{40,8},{48,16},{56,24},{0,32},{8,40},{16,48},{24,56},{96,64... | collective-permute-start | bytes 98312 | tf_op jit(solution)/shard_map/ppermute | solution.py:357
  45.8 0.0 collective-permute-done.12.refs_1_.refs_8_
  45.8 0.4 base_kernel.1.refs_6_
  46.2 0.6 %collective-permute-done.9.refs_2_ = f32[16,512]{1,0:T(8,128)S(1)} collective-permute-done((f32[16,512]{1,0:T(8,128)S(1)}, f32[16,512]{1,0:T(8,128)S(1)}, u32[]{:S(2)}, u32[]{:S(2)}) %collective-permute-start.9) | collective-permute-done | bytes 32800 | tf_op jit(solution)/shard_map/ppermute | solution.py:357
  46.8 1.0 %collective-permute-done.10.refs_3_ = f32[16,512]{1,0:T(8,128)S(1)} collective-permute-done((f32[16,512]{1,0:T(8,128)S(1)}, f32[16,512]{1,0:T(8,128)S(1)}, u32[]{:S(2)}, u32[]{:S(2)}) %collective-permute-start.10) | collective-permute-done | bytes 32800 | tf_op jit(solution)/shard_map/ppermute | solution.py:357
  47.9 0.2 collective-permute-done.11.refs_4_
  48.0 0.0 collective-permute-done.13.refs_7_
  48.0 2.3 %final_kernel.1 = (f32[2,512,512]{2,1,0:T(8,128)}, f32[4,512]{1,0:T(4,128)}) custom-call(s32[1]{0:T(128)} %bitcast.refs_0_, f32[16,512]{1,0:T(8,128)S(1)} %get-tuple-element.41.refs_3_.refs_1_, f32[16,512]{1,0:T(8,128)S(1)} %collective-permute-done.9.refs_2_, f32[16,512]{1,0:T(8,128)S(1)} %collective-permute-done.10.refs_3_, ...), custom_call_target="tpu_custom_call" | custom-call | flops 1000 | bytes 1000 | tf_op jit(solution)/shard_map/final_kernel/pallas_call | solution.py:66
  (21 shorter events, 0.1 us)
Async XLA Ops:
  0.6 1.3 %copy-start.5 = (f32[1,1,2,512]{3,2,1,0:T(2,128)S(1)}, f32[1,1,2,512]{3,2,1,0:T(2,128)}, u32[]{:S(2)}) copy-start(f32[1,1,2,512]{3,2,1,0:T(2,128)} %param.12) | copy-start | bytes 12292
  2.2 18.6 %collective-permute-start.1 = (bf16[512,512]{1,0:T(8,128)(2,1)S(1)}, bf16[512,512]{1,0:T(8,128)(2,1)S(1)}, u32[]{:S(2)}, u32[]{:S(2)}) collective-permute-start(bf16[512,512]{1,0:T(8,128)(2,1)S(1)} %north_kernel.1.refs_4_), channel_id=1, source_target_pairs={{0,8},{8,16},{16,24},{24,32},{32,40},{40,48},{48,56},{56,64},{64,7... | collective-permute-start | bytes 1572872 | tf_op jit(solution)/shard_map/ppermute | solution.py:353
  4.2 1.6 %copy-start.2 = (f32[153,153]{1,0:T(8,128)S(1)}, f32[153,153]{1,0:T(8,128)}, u32[]{:S(2)}) copy-start(f32[153,153]{1,0:T(8,128)} %refs_4_.1) | copy-start | bytes 280912
  4.2 1.6 %copy-start.4 = (s32[16,8,4]{0,2,1:T(4,128)S(1)}, s32[16,8,4]{0,2,1:T(4,128)}, u32[]{:S(2)}) copy-start(s32[16,8,4]{0,2,1:T(4,128)} %param.18) | copy-start | bytes 6148
  4.2 2.9 %copy-start = (bf16[1,1,1024,2048]{3,2,1,0:T(8,128)(2,1)S(1)}, bf16[1,1,1024,2048]{3,2,1,0:T(8,128)(2,1)}, u32[]{:S(2)}) copy-start(bf16[1,1,1024,2048]{3,2,1,0:T(8,128)(2,1)} %param.14) | copy-start | bytes 12582916
  4.2 2.9 %copy-start.3 = (bf16[1,1,4,2048]{3,2,1,0:T(4,128)(2,1)S(1)}, bf16[1,1,4,2048]{3,2,1,0:T(4,128)(2,1)}, u32[]{:S(2)}) copy-start(bf16[1,1,4,2048]{3,2,1,0:T(4,128)(2,1)} %param.16) | copy-start | bytes 49156
  4.3 2.9 %copy-start.8 = (s32[1,1,4,512]{3,2,1,0:T(4,128)S(1)}, s32[1,1,4,512]{3,2,1,0:T(4,128)}, u32[]{:S(2)}) copy-start(s32[1,1,4,512]{3,2,1,0:T(4,128)} %param.19) | copy-start | bytes 24580
  5.8 11.5 %collective-permute-start = (bf16[512,512]{1,0:T(8,128)(2,1)S(1)}, bf16[512,512]{1,0:T(8,128)(2,1)S(1)}, u32[]{:S(2)}, u32[]{:S(2)}) collective-permute-start(bf16[512,512]{1,0:T(8,128)(2,1)S(1)} %get-tuple-element.34), channel_id=1, source_target_pairs={{0,1},{1,2},{2,3},{3,4},{4,5},{5,6},{6,7},{7,0},{8,9},{9,10},{10,1... | collective-permute-start | bytes 1572872 | tf_op jit(solution)/shard_map/ppermute | solution.py:353
  7.2 1.6 %copy-start.6 = (f32[1,1,1024,512]{3,2,1,0:T(8,128)S(1)}, f32[1,1,1024,512]{3,2,1,0:T(8,128)}, u32[]{:S(2)}) copy-start(f32[1,1,1024,512]{3,2,1,0:T(8,128)} %param.10) | copy-start | bytes 6291460
  8.8 2.3 %copy-start.1 = (bf16[1,1,1024,1024]{3,2,1,0:T(8,128)(2,1)S(1)}, bf16[1,1,1024,1024]{3,2,1,0:T(8,128)(2,1)}, u32[]{:S(2)}) copy-start(bf16[1,1,1024,1024]{3,2,1,0:T(8,128)(2,1)} %param.13) | copy-start | bytes 6291460
  8.8 2.4 %copy-start.7 = (f32[1,1,1024,512]{3,2,1,0:T(8,128)S(1)}, f32[1,1,1024,512]{3,2,1,0:T(8,128)}, u32[]{:S(2)}) copy-start(f32[1,1,1024,512]{3,2,1,0:T(8,128)} %param.10) | copy-start | bytes 6291460
  8.8 3.7 %slice-start = ((s8[8388608]{0:T(1024)(128)(4,1)}), s8[4194304]{0:T(1024)(128)(4,1)S(1)}, s32[]{:S(2)}) async-start(s8[8388608]{0:T(1024)(128)(4,1)} %bitcast.15), calls=%async_computation | async-start | bytes 8388608
  11.2 2.5 %slice-start.1 = ((s8[8388608]{0:T(1024)(128)(4,1)}), s8[4194304]{0:T(1024)(128)(4,1)S(1)}, s32[]{:S(2)}) async-start(s8[8388608]{0:T(1024)(128)(4,1)} %bitcast.15), calls=%async_computation.1 | async-start | bytes 8388608
  20.9 1.2 %collective-permute-start.2 = (f32[8,512]{1,0:T(8,128)S(1)}, f32[8,512]{1,0:T(8,128)S(1)}, u32[]{:S(2)}, u32[]{:S(2)}) collective-permute-start(f32[8,512]{1,0:T(8,128)S(1)} %corner_kernel.1.refs_3_.refs_1_), channel_id=1, source_target_pairs={{0,1},{1,0},{2,3},{3,2},{4,5},{5,4},{6,7},{7,6},{8,9},{9,8},{10,11... | collective-permute-start | bytes 49160 | tf_op jit(solution)/shard_map/ppermute | solution.py:416
  22.1 11.3 %collective-permute-start.5 = (f32[10,512]{1,0:T(8,128)S(1)}, f32[10,512]{1,0:T(8,128)S(1)}, u32[]{:S(2)}, u32[]{:S(2)}) collective-permute-start(f32[10,512]{1,0:T(8,128)S(1)} %pair_kernel.1.refs_8_.refs_1_), channel_id=1, source_target_pairs={{24,0},{16,8},{8,16},{0,24},{56,32},{48,40},{40,48},{32,56},{88,64... | collective-permute-start | bytes 61448 | tf_op jit(solution)/shard_map/ppermute | solution.py:357
  24.2 9.2 %collective-permute-start.4 = (f32[10,512]{1,0:T(8,128)S(1)}, f32[10,512]{1,0:T(8,128)S(1)}, u32[]{:S(2)}, u32[]{:S(2)}) collective-permute-start(f32[10,512]{1,0:T(8,128)S(1)} %pair_kernel.1.refs_8_.refs_1_), channel_id=1, source_target_pairs={{16,0},{24,8},{0,16},{8,24},{48,32},{56,40},{32,48},{40,56},{80,64... | collective-permute-start | bytes 61448 | tf_op jit(solution)/shard_map/ppermute | solution.py:357
  25.8 7.6 %collective-permute-start.3 = (f32[10,512]{1,0:T(8,128)S(1)}, f32[10,512]{1,0:T(8,128)S(1)}, u32[]{:S(2)}, u32[]{:S(2)}) collective-permute-start(f32[10,512]{1,0:T(8,128)S(1)} %pair_kernel.1.refs_8_.refs_1_), channel_id=1, source_target_pairs={{8,0},{0,8},{24,16},{16,24},{40,32},{32,40},{56,48},{48,56},{72,64... | collective-permute-start | bytes 61448 | tf_op jit(solution)/shard_map/ppermute | solution.py:357
  29.1 16.7 %collective-permute-start.12 = (bf16[528,512]{1,0:T(8,128)(2,1)S(1)}, bf16[528,512]{1,0:T(8,128)(2,1)S(1)}, u32[]{:S(2)}, u32[]{:S(2)}) collective-permute-start(bf16[528,512]{1,0:T(8,128)(2,1)S(1)} %get-tuple-element.39.refs_5_), channel_id=1, source_target_pairs={{0,120},{8,0},{16,8},{24,16},{32,24},{40,32},{48,40},{56,48},{64,5... | collective-permute-start | bytes 1622024 | tf_op jit(solution)/shard_map/ppermute | solution.py:353
  33.5 7.2 %collective-permute-start.8 = (f32[19,512]{1,0:T(8,128)S(1)}, f32[19,512]{1,0:T(8,128)S(1)}, u32[]{:S(2)}, u32[]{:S(2)}) collective-permute-start(f32[19,512]{1,0:T(8,128)S(1)} %rows_kernel.1.refs_7_.refs_5_.refs_2_), channel_id=1, source_target_pairs={{6,0},{7,1},{4,2},{5,3},{2,4},{3,5},{0,6},{1,7},{14,8},{15,9},{12,... | collective-permute-start | bytes 116744 | tf_op jit(solution)/shard_map/ppermute | solution.py:357
  35.5 5.6 %collective-permute-start.7 = (f32[19,512]{1,0:T(8,128)S(1)}, f32[19,512]{1,0:T(8,128)S(1)}, u32[]{:S(2)}, u32[]{:S(2)}) collective-permute-start(f32[19,512]{1,0:T(8,128)S(1)} %rows_kernel.1.refs_7_.refs_5_.refs_2_), channel_id=1, source_target_pairs={{4,0},{5,1},{6,2},{7,3},{0,4},{1,5},{2,6},{3,7},{12,8},{13,9},{14,... | collective-permute-start | bytes 116744 | tf_op jit(solution)/shard_map/ppermute | solution.py:357
  37.3 4.1 %collective-permute-start.6 = (f32[19,512]{1,0:T(8,128)S(1)}, f32[19,512]{1,0:T(8,128)S(1)}, u32[]{:S(2)}, u32[]{:S(2)}) collective-permute-start(f32[19,512]{1,0:T(8,128)S(1)} %rows_kernel.1.refs_7_.refs_5_.refs_2_), channel_id=1, source_target_pairs={{2,0},{3,1},{0,2},{1,3},{6,4},{7,5},{4,6},{5,7},{10,8},{11,9},{8,1... | collective-permute-start | bytes 116744 | tf_op jit(solution)/shard_map/ppermute | solution.py:357
  38.8 9.2 %collective-permute-start.13 = (bf16[528,512]{1,0:T(8,128)(2,1)S(1)}, bf16[528,512]{1,0:T(8,128)(2,1)S(1)}, u32[]{:S(2)}, u32[]{:S(2)}) collective-permute-start(bf16[528,512]{1,0:T(8,128)(2,1)S(1)} %west_kernel.1.refs_6_), channel_id=1, source_target_pairs={{0,7},{1,0},{2,1},{3,2},{4,3},{5,4},{6,5},{7,6},{8,15},{9,8},{10,9... | collective-permute-start | bytes 1622024 | tf_op jit(solution)/shard_map/ppermute | solution.py:353
  41.6 5.2 %collective-permute-start.9 = (f32[16,512]{1,0:T(8,128)S(1)}, f32[16,512]{1,0:T(8,128)S(1)}, u32[]{:S(2)}, u32[]{:S(2)}) collective-permute-start(f32[16,512]{1,0:T(8,128)S(1)} %get-tuple-element.42), channel_id=1, source_target_pairs={{96,0},{104,8},{112,16},{120,24},{64,32},{72,40},{80,48},{88,56},{... | collective-permute-start | bytes 98312 | tf_op jit(solution)/shard_map/ppermute | solution.py:357
  42.4 5.4 %collective-permute-start.10 = (f32[16,512]{1,0:T(8,128)S(1)}, f32[16,512]{1,0:T(8,128)S(1)}, u32[]{:S(2)}, u32[]{:S(2)}) collective-permute-start(f32[16,512]{1,0:T(8,128)S(1)} %get-tuple-element.43), channel_id=1, source_target_pairs={{64,0},{72,8},{80,16},{88,24},{96,32},{104,40},{112,48},{120,56},{... | collective-permute-start | bytes 98312 | tf_op jit(solution)/shard_map/ppermute | solution.py:357
  42.9 5.1 %collective-permute-start.11 = (f32[16,512]{1,0:T(8,128)S(1)}, f32[16,512]{1,0:T(8,128)S(1)}, u32[]{:S(2)}, u32[]{:S(2)}) collective-permute-start(f32[16,512]{1,0:T(8,128)S(1)} %get-tuple-element.44), channel_id=1, source_target_pairs={{32,0},{40,8},{48,16},{56,24},{0,32},{8,40},{16,48},{24,56},{96,64... | collective-permute-start | bytes 98312 | tf_op jit(solution)/shard_map/ppermute | solution.py:357

commit v7 on v5

--- a/solution.py
+++ b/solution.py
@@ -220,9 +220,9 @@
     sent[FACE:] = tail(basis, 2, keep)
 
 
-def kept_kernel(coup, block, h, ub, south, kept):
+def kept_kernel(coup, block, h, ub, south, w, kept):
     for f in range(2):
-        kept[f * FACE : (f + 1) * FACE] = result(f, coup, block, h, ub, south)
+        kept[f * FACE : (f + 1) * FACE] = column(w[f : f + 1, :]) * result(f, coup, block, h, ub, south)
 
 
 def pair_kernel(pos, mine, theirs, out):
@@ -279,7 +279,7 @@
 
 def base_kernel(kept, got, w, out):
     wc = column(w[1:2, :])
-    out[...] = wc * kept[FACE:] + (1.0 - wc) * got[:FACE].astype(F32)
+    out[...] = kept[FACE:] + (1.0 - wc) * got[:FACE].astype(F32)
 
 
 def correction(f, cc, got, w, basis):
@@ -304,7 +304,7 @@
         left, right = correction(f, cc, got, w, basis)
         for n in range(4):
             rows = slice(n * 128, (n + 1) * 128)
-            part = base[rows] if f else wc[rows] * kept[rows] + (1.0 - wc[rows]) * got[rows].astype(F32)
+            part = base[rows] if f else kept[rows] + (1.0 - wc[rows]) * got[rows].astype(F32)
             zbuf[f, rows] = part + mm_tn(left[:, rows], right)
             here = pl.ds(n * 128, 128)
             copy = pltpu.make_async_copy(zbuf.at[f, here], z.at[f, here], sem.at[4 * f + n])
@@ -416,8 +416,8 @@
         j, coup, block, h, ub, south, basis
     )
     from_east = along(to_west, "col", -1)
-    kept = call(kept_kernel, shape(2 * FACE, F32), [VMEM] * 5, VMEM, after=(sums, to_west), cost=30)(
-        coup, block, h, ub, south
+    kept = call(kept_kernel, shape(2 * FACE, F32), [VMEM] * 6, VMEM, after=(sums, to_west), cost=30)(
+        coup, block, h, ub, south, w
     )
     shares = call(
         columns_kernel,

time: 49 us -> 49 us (level)
  no operation moved by 1% of the time
where the time goes in v7:
time: 49 us; the launch traced here: 48.8 us
  Pallas kernels  21.9 us (45%)
  starting transfers between devices  17.2 us (35%)
  waiting for transfers between devices  6.66 us (14%)
  local copies, waits for them, and re-layouts  2.05 us (4%)
  between operations  1.02 us (2%)
    pallas_call x18, Pallas kernels, call(): return lambda *args: run(*args, *after)  21.9 us
    ppermute x9, starting transfers between devices, exchanged(): lax.ppermute(x, axis, [(d ^ k * stride, d) for d in range(lax.axis_size(a...  12.7 us
    ppermute x4, starting transfers between devices, along(): return lax.ppermute(x, axis, [(s, (s + d) % n) for s in range(n)])  4.47 us
    ppermute x4, waiting for transfers between devices, along(): return lax.ppermute(x, axis, [(s, (s + d) % n) for s in range(n)])  3.43 us
    ppermute x9, waiting for transfers between devices, exchanged(): lax.ppermute(x, axis, [(d ^ k * stride, d) for d in range(lax.axis_size(a...  2.77 us
    unnamed x22, local copies, waits for them, and re-layouts  2.05 us
  transfers between devices with their start and end apart: 14, of which 6 were waited for; matrix products, arithmetic and copies ran while one was open for 0% of the time, Pallas kernels for 37%

profile of v7, /device:TPU:0, one launch (start us, length us, event | category | flops | bytes accessed | tf_op | source)
XLA Modules:
  0.0 48.8 jit_solution(7180553654751908939)
XLA Ops:
  0.7 1.4 %load_kernel.1.refs_1_ = f32[512,512]{1,0:T(8,128)S(1)} custom-call(f32[2,512,512]{2,1,0:T(8,128)} %bitcast.42), custom_call_target="tpu_custom_call" | custom-call | flops 4000001024 | bytes 12001000 | tf_op jit(solution)/shard_map/load_kernel/pallas_call | solution.py:66
  2.1 0.3 north_kernel.1.refs_3_
  2.3 2.1 %collective-permute-start.1 = (bf16[512,512]{1,0:T(8,128)(2,1)S(1)}, bf16[512,512]{1,0:T(8,128)(2,1)S(1)}, u32[]{:S(2)}, u32[]{:S(2)}) collective-permute-start(bf16[512,512]{1,0:T(8,128)(2,1)S(1)} %north_kernel.1.refs_3_), channel_id=1, source_target_pairs={{0,8},{8,16},{16,24},{24,32},{32,40},{40,48},{48,56},{56,64},{64,7... | collective-permute-start | bytes 1572872 | tf_op jit(solution)/shard_map/ppermute | solution.py:334
  4.4 0.0 copy-start.3
  4.4 0.0 copy-start.7
  4.4 0.0 copy-start.8
  4.4 0.5 east_kernel.1
  4.9 0.0 collective-permute-start
  4.9 0.4 copy-done.2
  5.3 1.3 %table_kernel.1.refs_5_.refs_6_ = f32[64,48]{1,0:T(8,128)S(1)} custom-call(s32[1]{0:T(128)} %bitcast.refs_0_, s32[1]{0:T(128)} %bitcast.5.refs_0_.refs_1_, s32[32,16]{1,0:T(8,128)S(1)} %bitcast.35, s32[32,16]{1,0:T(8,128)S(1)} %bitcast.36, f32[153,153]{1,0:T(8,128)S(1)} %copy-done.2, bf16[1024,512]{1,0:T(8,128)(2,1)S(1)} %get-tuple-element.25.refs_5_.refs_2_), custom_call_target="tpu_custom_call" | custom-call | flops 1000 | bytes 1000 | tf_op jit(solution)/shard_map/table_kernel/pallas_call | solution.py:66
  6.7 0.0 copy-done
  6.7 0.7 %copy-done.7 = f32[1,1,1024,512]{3,2,1,0:T(8,128)S(1)} copy-done((f32[1,1,1024,512]{3,2,1,0:T(8,128)S(1)}, f32[1,1,1024,512]{3,2,1,0:T(8,128)}, u32[]{:S(2)}) %copy-start.7) | copy-done | bytes 2097176
  7.4 2.3 %early_a_kernel.1 = (f32[1024,512]{1,0:T(8,128)S(1)}, f32[8,1024]{1,0:T(8,128)S(1)}, bf16[8,2048]{1,0:T(8,128)(2,1)S(1)}) custom-call(bf16[1024,2048]{1,0:T(8,128)(2,1)S(1)} %bitcast.22, f32[1024,512]{1,0:T(8,128)S(1)} %bitcast.44, bf16[1024,512]{1,0:T(8,128)(2,1)S(1)} %get-tuple-element.25.refs_5_.refs_2_, bf16[4,2048]{1,0:T(4,128)(2,1)S(1)} %bitcast.31, ...), custom_call_target="tpu_custom_call" | custom-call | flops 10000001024 | bytes 30001000 | tf_op jit(solution)/shard_map/early_a_kernel/pallas_call | solution.py:66
  9.7 0.0 slice-start.1
  9.8 1.4 %early_b_kernel.1 = (f32[8,2048]{1,0:T(8,128)S(1)}, f32[8,512]{1,0:T(8,128)S(1)}) custom-call(f32[8,1024]{1,0:T(8,128)S(1)} %get-tuple-element.28.refs_0_, bf16[1024,1024]{1,0:T(8,128)(2,1)S(1)} %bitcast.29, bf16[1024,2048]{1,0:T(8,128)(2,1)S(1)} %bitcast.23, f32[1024,512]{1,0:T(8,128)S(1)} %bitcast.45), custom_call_target="tpu_custom_call" | custom-call | flops 10000001024 | bytes 30001000 | tf_op jit(solution)/shard_map/early_b_kernel/pallas_call | solution.py:66
  11.1 0.9 %slice-done.1 = s8[4194304]{0:T(1024)(128)(4,1)S(1)} async-done(((s8[8388608]{0:T(1024)(128)(4,1)}), s8[4194304]{0:T(1024)(128)(4,1)S(1)}, s32[]{:S(2)}) %slice-start.1) | async-done | bytes 4194328
  12.0 3.6 %early_c_kernel.1 = (f32[2048,512]{1,0:T(8,128)S(1)}, f32[8,512]{1,0:T(8,128)S(1)}, bf16[16,1024]{1,0:T(8,128)(2,1)S(1)}) custom-call(bf16[8,2048]{1,0:T(8,128)(2,1)S(1)} %get-tuple-element.27.refs_0_, bf16[2048,2048]{1,0:T(8,128)(2,1)S(1)} %bitcast.17, bf16[1024,512]{1,0:T(8,128)(2,1)S(1)} %get-tuple-element.25.refs_5_.refs_2_, ...), custom_call_target="tpu_custom_call" | custom-call | flops 10000001024 | bytes 30001000 | tf_op jit(solution)/shard_map/early_c_kernel/pallas_call | solution.py:66
  15.6 0.0 collective-permute-done.refs_6_
  15.6 1.8 %west_terms_kernel.1 = (f32[1024,512]{1,0:T(8,128)S(1)}, f32[2048,512]{1,0:T(8,128)S(1)}, f32[8,512]{1,0:T(8,128)S(1)}) custom-call(bf16[1024,2048]{1,0:T(8,128)(2,1)S(1)} %bitcast.24, bf16[2048,2048]{1,0:T(8,128)(2,1)S(1)} %bitcast.18, f32[1024,512]{1,0:T(8,128)S(1)} %get-tuple-element.26.refs_2_, f32[2048,512]{1,0:T(8,128)S(1)} %get-tuple-element.31.refs_3_, ...), custom_call_target="tpu_custom_call" | custom-call | flops 2000001024 | bytes 6001000 | tf_op jit(solution)/shard_map/west_terms_kernel/pallas_call | solution.py:66
  17.5 3.4 %collective-permute-done.1.refs_2_.refs_6_.refs_5_.refs_4_ = bf16[512,512]{1,0:T(8,128)(2,1)S(1)} collective-permute-done((bf16[512,512]{1,0:T(8,128)(2,1)S(1)}, bf16[512,512]{1,0:T(8,128)(2,1)S(1)}, u32[]{:S(2)}, u32[]{:S(2)}) %collective-permute-start.1) | collective-permute-done | bytes 524320 | tf_op jit(solution)/shard_map/ppermute | solution.py:334
  20.9 0.2 corner_kernel.1.refs_3_.refs_1_
  21.1 0.7 %inner_kernel.1.refs_3_.refs_4_ = bf16[1024,512]{1,0:T(8,128)(2,1)S(1)} custom-call(bf16[1024,2048]{1,0:T(8,128)(2,1)S(1)} %bitcast.25, f32[1024,512]{1,0:T(8,128)S(1)} %get-tuple-element.35.refs_1_, bf16[512,512]{1,0:T(8,128)(2,1)S(1)} %collective-permute-done.1.refs_2_.refs_6_.refs_5_.refs_4_, f32[8,512]{1,0:T(8,128)S(1)} %corner_kernel.1.refs_3_.refs_1_), custom_call_target="tpu_custom_call" | custom-call | flops 1000001024 | bytes 3001000 | tf_op jit(solution)/shard_map/inner_kernel/pallas_call | solution.py:66
  21.8 0.5 collective-permute-done.2.refs_2_
  22.3 0.1 collective-permute-start.5
  22.4 0.8 %collective-permute-start.4 = (f32[10,512]{1,0:T(8,128)S(1)}, f32[10,512]{1,0:T(8,128)S(1)}, u32[]{:S(2)}, u32[]{:S(2)}) collective-permute-start(f32[10,512]{1,0:T(8,128)S(1)} %pair_kernel.1.refs_8_.refs_1_), channel_id=1, source_target_pairs={{16,0},{24,8},{0,16},{8,24},{48,32},{56,40},{32,48},{40,56},{80,64... | collective-permute-start | bytes 61448 | tf_op jit(solution)/shard_map/ppermute | solution.py:338
  23.2 3.3 %collective-permute-start.3 = (f32[10,512]{1,0:T(8,128)S(1)}, f32[10,512]{1,0:T(8,128)S(1)}, u32[]{:S(2)}, u32[]{:S(2)}) collective-permute-start(f32[10,512]{1,0:T(8,128)S(1)} %pair_kernel.1.refs_8_.refs_1_), channel_id=1, source_target_pairs={{8,0},{0,8},{24,16},{16,24},{40,32},{32,40},{56,48},{48,56},{72,64... | collective-permute-start | bytes 61448 | tf_op jit(solution)/shard_map/ppermute | solution.py:338
  26.5 2.8 %solve_kernel.1 = (f32[1024,512]{1,0:T(8,128)}, bf16[528,512]{1,0:T(8,128)(2,1)S(1)}, bf16[1024,512]{1,0:T(8,128)(2,1)S(1)}) custom-call(s32[1]{0:T(128)} %bitcast.refs_0_, bf16[1024,2048]{1,0:T(8,128)(2,1)S(1)} %bitcast.26, bf16[1024,1024]{1,0:T(8,128)(2,1)S(1)} %bitcast.30, bf16[2048,2048]{1,0:T(8,128)(2,1)S(1)} %bitcast.19, ...), custom_call_target="tpu_custom_call" | custom-call | flops 4000001024 | bytes 12001000 | tf_op jit(solution)/shard_map/solve_kernel/pallas_call | solution.py:66
  29.2 1.8 %collective-permute-start.12 = (bf16[528,512]{1,0:T(8,128)(2,1)S(1)}, bf16[528,512]{1,0:T(8,128)(2,1)S(1)}, u32[]{:S(2)}, u32[]{:S(2)}) collective-permute-start(bf16[528,512]{1,0:T(8,128)(2,1)S(1)} %get-tuple-element.39.refs_5_), channel_id=1, source_target_pairs={{0,120},{8,0},{16,8},{24,16},{32,24},{40,32},{48,40},{56,48},{64,5... | collective-permute-start | bytes 1622024 | tf_op jit(solution)/shard_map/ppermute | solution.py:334
  31.0 0.0 collective-permute-done.5.refs_4_
  31.0 0.0 collective-permute-done.4.refs_3_
  31.1 3.0 %collective-permute-start.8 = (f32[19,512]{1,0:T(8,128)S(1)}, f32[19,512]{1,0:T(8,128)S(1)}, u32[]{:S(2)}, u32[]{:S(2)}) collective-permute-start(f32[19,512]{1,0:T(8,128)S(1)} %rows_kernel.1.refs_7_.refs_6_.refs_2_), channel_id=1, source_target_pairs={{6,0},{7,1},{4,2},{5,3},{2,4},{3,5},{0,6},{1,7},{14,8},{15,9},{12,... | collective-permute-start | bytes 116744 | tf_op jit(solution)/shard_map/ppermute | solution.py:338
  34.1 0.8 %collective-permute-start.7 = (f32[19,512]{1,0:T(8,128)S(1)}, f32[19,512]{1,0:T(8,128)S(1)}, u32[]{:S(2)}, u32[]{:S(2)}) collective-permute-start(f32[19,512]{1,0:T(8,128)S(1)} %rows_kernel.1.refs_7_.refs_6_.refs_2_), channel_id=1, source_target_pairs={{4,0},{5,1},{6,2},{7,3},{0,4},{1,5},{2,6},{3,7},{12,8},{13,9},{14,... | collective-permute-start | bytes 116744 | tf_op jit(solution)/shard_map/ppermute | solution.py:338
  34.9 0.5 %collective-permute-start.6 = (f32[19,512]{1,0:T(8,128)S(1)}, f32[19,512]{1,0:T(8,128)S(1)}, u32[]{:S(2)}, u32[]{:S(2)}) collective-permute-start(f32[19,512]{1,0:T(8,128)S(1)} %rows_kernel.1.refs_7_.refs_6_.refs_2_), channel_id=1, source_target_pairs={{2,0},{3,1},{0,2},{1,3},{6,4},{7,5},{4,6},{5,7},{10,8},{11,9},{8,1... | collective-permute-start | bytes 116744 | tf_op jit(solution)/shard_map/ppermute | solution.py:338
  35.5 1.0 %west_kernel.1.refs_7_ = bf16[528,512]{1,0:T(8,128)(2,1)S(1)} custom-call(s32[1]{0:T(128)} %bitcast.5.refs_0_.refs_1_, bf16[1024,2048]{1,0:T(8,128)(2,1)S(1)} %bitcast.27, bf16[2048,2048]{1,0:T(8,128)(2,1)S(1)} %bitcast.20, f32[2048,512]{1,0:T(8,128)S(1)} %get-tuple-element.37.refs_5_.refs_3_.refs_2_, ...), custom_call_target="tpu_custom_call" | custom-call | flops 1000001024 | bytes 3001000 | tf_op jit(solution)/shard_map/west_kernel/pallas_call | solution.py:66
  36.4 0.6 %collective-permute-start.13 = (bf16[528,512]{1,0:T(8,128)(2,1)S(1)}, bf16[528,512]{1,0:T(8,128)(2,1)S(1)}, u32[]{:S(2)}, u32[]{:S(2)}) collective-permute-start(bf16[528,512]{1,0:T(8,128)(2,1)S(1)} %west_kernel.1.refs_7_), channel_id=1, source_target_pairs={{0,7},{1,0},{2,1},{3,2},{4,3},{5,4},{6,5},{7,6},{8,15},{9,8},{10,9... | collective-permute-start | bytes 1622024 | tf_op jit(solution)/shard_map/ppermute | solution.py:334
  37.0 1.9 %kept_kernel.1.refs_7_.refs_0_.refs_5_ = f32[1024,512]{1,0:T(8,128)S(1)} custom-call(bf16[1024,2048]{1,0:T(8,128)(2,1)S(1)} %bitcast.28, bf16[2048,2048]{1,0:T(8,128)(2,1)S(1)} %bitcast.21, f32[2048,512]{1,0:T(8,128)S(1)} %get-tuple-element.37.refs_5_.refs_3_.refs_2_, bf16[1024,512]{1,0:T(8,128)(2,1)S(1)} %get-tuple-element.40.refs_4_.refs_3_, ...), custom_call_target="tpu_custom_call" | custom-call | flops 30000001024 | bytes 90001000 | tf_op jit(solution)/shard_map/kept_kernel/pallas_call | solution.py:66
  38.9 0.0 collective-permute-done.8.refs_5_
  38.9 0.8 %collective-permute-done.7.refs_4_ = f32[19,512]{1,0:T(8,128)S(1)} collective-permute-done((f32[19,512]{1,0:T(8,128)S(1)}, f32[19,512]{1,0:T(8,128)S(1)}, u32[]{:S(2)}, u32[]{:S(2)}) %collective-permute-start.7) | collective-permute-done | bytes 38944 | tf_op jit(solution)/shard_map/ppermute | solution.py:338
  39.7 0.0 collective-permute-done.6.refs_3_
  39.7 0.2 columns_kernel.1
  40.0 0.8 %collective-permute-start.9 = (f32[16,512]{1,0:T(8,128)S(1)}, f32[16,512]{1,0:T(8,128)S(1)}, u32[]{:S(2)}, u32[]{:S(2)}) collective-permute-start(f32[16,512]{1,0:T(8,128)S(1)} %get-tuple-element.42), channel_id=1, source_target_pairs={{96,0},{104,8},{112,16},{120,24},{64,32},{72,40},{80,48},{88,56},{... | collective-permute-start | bytes 98312 | tf_op jit(solution)/shard_map/ppermute | solution.py:338
  40.8 1.1 %collective-permute-start.10 = (f32[16,512]{1,0:T(8,128)S(1)}, f32[16,512]{1,0:T(8,128)S(1)}, u32[]{:S(2)}, u32[]{:S(2)}) collective-permute-start(f32[16,512]{1,0:T(8,128)S(1)} %get-tuple-element.43), channel_id=1, source_target_pairs={{64,0},{72,8},{80,16},{88,24},{96,32},{104,40},{112,48},{120,56},{... | collective-permute-start | bytes 98312 | tf_op jit(solution)/shard_map/ppermute | solution.py:338
  41.9 2.2 %collective-permute-start.11 = (f32[16,512]{1,0:T(8,128)S(1)}, f32[16,512]{1,0:T(8,128)S(1)}, u32[]{:S(2)}, u32[]{:S(2)}) collective-permute-start(f32[16,512]{1,0:T(8,128)S(1)} %get-tuple-element.44), channel_id=1, source_target_pairs={{32,0},{40,8},{48,16},{56,24},{0,32},{8,40},{16,48},{24,56},{96,64... | collective-permute-start | bytes 98312 | tf_op jit(solution)/shard_map/ppermute | solution.py:338
  44.1 0.3 base_kernel.1.refs_6_
  44.5 0.7 %collective-permute-done.9.refs_2_ = f32[16,512]{1,0:T(8,128)S(1)} collective-permute-done((f32[16,512]{1,0:T(8,128)S(1)}, f32[16,512]{1,0:T(8,128)S(1)}, u32[]{:S(2)}, u32[]{:S(2)}) %collective-permute-start.9) | collective-permute-done | bytes 32800 | tf_op jit(solution)/shard_map/ppermute | solution.py:338
  45.2 1.0 %collective-permute-done.10.refs_3_ = f32[16,512]{1,0:T(8,128)S(1)} collective-permute-done((f32[16,512]{1,0:T(8,128)S(1)}, f32[16,512]{1,0:T(8,128)S(1)}, u32[]{:S(2)}, u32[]{:S(2)}) %collective-permute-start.10) | collective-permute-done | bytes 32800 | tf_op jit(solution)/shard_map/ppermute | solution.py:338
  46.2 0.2 collective-permute-done.11.refs_4_
  46.4 2.3 %final_kernel.1 = (f32[2,512,512]{2,1,0:T(8,128)}, f32[4,512]{1,0:T(4,128)}) custom-call(s32[1]{0:T(128)} %bitcast.refs_0_, f32[16,512]{1,0:T(8,128)S(1)} %get-tuple-element.41.refs_3_.refs_1_, f32[16,512]{1,0:T(8,128)S(1)} %collective-permute-done.9.refs_2_, f32[16,512]{1,0:T(8,128)S(1)} %collective-permute-done.10.refs_3_, ...), custom_call_target="tpu_custom_call" | custom-call | flops 1000 | bytes 1000 | tf_op jit(solution)/shard_map/final_kernel/pallas_call | solution.py:66
  (21 shorter events, 0.1 us)
Async XLA Ops:
  0.6 1.4 %copy-start.5 = (f32[1,1,2,512]{3,2,1,0:T(2,128)S(1)}, f32[1,1,2,512]{3,2,1,0:T(2,128)}, u32[]{:S(2)}) copy-start(f32[1,1,2,512]{3,2,1,0:T(2,128)} %param.12) | copy-start | bytes 12292
  0.6 3.8 %copy-start.6 = (f32[1,1,2,512,512]{4,3,2,1,0:T(8,128)S(1)}, f32[1,1,2,512,512]{4,3,2,1,0:T(8,128)}, u32[]{:S(2)}) copy-start(f32[1,1,2,512,512]{4,3,2,1,0:T(8,128)} %param.11) | copy-start | bytes 6291460
  2.3 18.6 %collective-permute-start.1 = (bf16[512,512]{1,0:T(8,128)(2,1)S(1)}, bf16[512,512]{1,0:T(8,128)(2,1)S(1)}, u32[]{:S(2)}, u32[]{:S(2)}) collective-permute-start(bf16[512,512]{1,0:T(8,128)(2,1)S(1)} %north_kernel.1.refs_3_), channel_id=1, source_target_pairs={{0,8},{8,16},{16,24},{24,32},{32,40},{40,48},{48,56},{56,64},{64,7... | collective-permute-start | bytes 1572872 | tf_op jit(solution)/shard_map/ppermute | solution.py:334
  4.4 0.9 %copy-start.2 = (f32[153,153]{1,0:T(8,128)S(1)}, f32[153,153]{1,0:T(8,128)}, u32[]{:S(2)}) copy-start(f32[153,153]{1,0:T(8,128)} %refs_4_.1) | copy-start | bytes 280912
  4.4 0.9 %copy-start.4 = (s32[16,8,4]{0,2,1:T(4,128)S(1)}, s32[16,8,4]{0,2,1:T(4,128)}, u32[]{:S(2)}) copy-start(s32[16,8,4]{0,2,1:T(4,128)} %param.18) | copy-start | bytes 6148
  4.4 2.3 %copy-start = (bf16[1,1,1024,2048]{3,2,1,0:T(8,128)(2,1)S(1)}, bf16[1,1,1024,2048]{3,2,1,0:T(8,128)(2,1)}, u32[]{:S(2)}) copy-start(bf16[1,1,1024,2048]{3,2,1,0:T(8,128)(2,1)} %param.14) | copy-start | bytes 12582916
  4.4 2.3 %copy-start.3 = (bf16[1,1,4,2048]{3,2,1,0:T(4,128)(2,1)S(1)}, bf16[1,1,4,2048]{3,2,1,0:T(4,128)(2,1)}, u32[]{:S(2)}) copy-start(bf16[1,1,4,2048]{3,2,1,0:T(4,128)(2,1)} %param.16) | copy-start | bytes 49156
  4.4 3.0 %copy-start.7 = (f32[1,1,1024,512]{3,2,1,0:T(8,128)S(1)}, f32[1,1,1024,512]{3,2,1,0:T(8,128)}, u32[]{:S(2)}) copy-start(f32[1,1,1024,512]{3,2,1,0:T(8,128)} %param.10) | copy-start | bytes 6291460
  4.4 3.0 %copy-start.8 = (s32[1,1,4,512]{3,2,1,0:T(4,128)S(1)}, s32[1,1,4,512]{3,2,1,0:T(4,128)}, u32[]{:S(2)}) copy-start(s32[1,1,4,512]{3,2,1,0:T(4,128)} %param.19) | copy-start | bytes 24580
  4.9 10.7 %collective-permute-start = (bf16[512,512]{1,0:T(8,128)(2,1)S(1)}, bf16[512,512]{1,0:T(8,128)(2,1)S(1)}, u32[]{:S(2)}, u32[]{:S(2)}) collective-permute-start(bf16[512,512]{1,0:T(8,128)(2,1)S(1)} %get-tuple-element.34), channel_id=1, source_target_pairs={{0,1},{1,2},{2,3},{3,4},{4,5},{5,6},{6,7},{7,0},{8,9},{9,10},{10,1... | collective-permute-start | bytes 1572872 | tf_op jit(solution)/shard_map/ppermute | solution.py:334
  7.4 2.3 %copy-start.1 = (bf16[1,1,1024,1024]{3,2,1,0:T(8,128)(2,1)S(1)}, bf16[1,1,1024,1024]{3,2,1,0:T(8,128)(2,1)}, u32[]{:S(2)}) copy-start(bf16[1,1,1024,1024]{3,2,1,0:T(8,128)(2,1)} %param.13) | copy-start | bytes 6291460
  7.4 3.7 %slice-start = ((s8[8388608]{0:T(1024)(128)(4,1)}), s8[4194304]{0:T(1024)(128)(4,1)S(1)}, s32[]{:S(2)}) async-start(s8[8388608]{0:T(1024)(128)(4,1)} %bitcast.15), calls=%async_computation | async-start | bytes 8388608
  9.7 2.3 %slice-start.1 = ((s8[8388608]{0:T(1024)(128)(4,1)}), s8[4194304]{0:T(1024)(128)(4,1)S(1)}, s32[]{:S(2)}) async-start(s8[8388608]{0:T(1024)(128)(4,1)} %bitcast.15), calls=%async_computation.1 | async-start | bytes 8388608
  21.1 1.2 %collective-permute-start.2 = (f32[8,512]{1,0:T(8,128)S(1)}, f32[8,512]{1,0:T(8,128)S(1)}, u32[]{:S(2)}, u32[]{:S(2)}) collective-permute-start(f32[8,512]{1,0:T(8,128)S(1)} %corner_kernel.1.refs_3_.refs_1_), channel_id=1, source_target_pairs={{0,1},{1,0},{2,3},{3,2},{4,5},{5,4},{6,7},{7,6},{8,9},{9,8},{10,11... | collective-permute-start | bytes 49160 | tf_op jit(solution)/shard_map/ppermute | solution.py:397
  22.3 8.8 %collective-permute-start.5 = (f32[10,512]{1,0:T(8,128)S(1)}, f32[10,512]{1,0:T(8,128)S(1)}, u32[]{:S(2)}, u32[]{:S(2)}) collective-permute-start(f32[10,512]{1,0:T(8,128)S(1)} %pair_kernel.1.refs_8_.refs_1_), channel_id=1, source_target_pairs={{24,0},{16,8},{8,16},{0,24},{56,32},{48,40},{40,48},{32,56},{88,64... | collective-permute-start | bytes 61448 | tf_op jit(solution)/shard_map/ppermute | solution.py:338
  22.4 8.7 %collective-permute-start.4 = (f32[10,512]{1,0:T(8,128)S(1)}, f32[10,512]{1,0:T(8,128)S(1)}, u32[]{:S(2)}, u32[]{:S(2)}) collective-permute-start(f32[10,512]{1,0:T(8,128)S(1)} %pair_kernel.1.refs_8_.refs_1_), channel_id=1, source_target_pairs={{16,0},{24,8},{0,16},{8,24},{48,32},{56,40},{32,48},{40,56},{80,64... | collective-permute-start | bytes 61448 | tf_op jit(solution)/shard_map/ppermute | solution.py:338
  23.2 7.9 %collective-permute-start.3 = (f32[10,512]{1,0:T(8,128)S(1)}, f32[10,512]{1,0:T(8,128)S(1)}, u32[]{:S(2)}, u32[]{:S(2)}) collective-permute-start(f32[10,512]{1,0:T(8,128)S(1)} %pair_kernel.1.refs_8_.refs_1_), channel_id=1, source_target_pairs={{8,0},{0,8},{24,16},{16,24},{40,32},{32,40},{56,48},{48,56},{72,64... | collective-permute-start | bytes 61448 | tf_op jit(solution)/shard_map/ppermute | solution.py:338
  29.2 14.9 %collective-permute-start.12 = (bf16[528,512]{1,0:T(8,128)(2,1)S(1)}, bf16[528,512]{1,0:T(8,128)(2,1)S(1)}, u32[]{:S(2)}, u32[]{:S(2)}) collective-permute-start(bf16[528,512]{1,0:T(8,128)(2,1)S(1)} %get-tuple-element.39.refs_5_), channel_id=1, source_target_pairs={{0,120},{8,0},{16,8},{24,16},{32,24},{40,32},{48,40},{56,48},{64,5... | collective-permute-start | bytes 1622024 | tf_op jit(solution)/shard_map/ppermute | solution.py:334
  31.1 7.8 %collective-permute-start.8 = (f32[19,512]{1,0:T(8,128)S(1)}, f32[19,512]{1,0:T(8,128)S(1)}, u32[]{:S(2)}, u32[]{:S(2)}) collective-permute-start(f32[19,512]{1,0:T(8,128)S(1)} %rows_kernel.1.refs_7_.refs_6_.refs_2_), channel_id=1, source_target_pairs={{6,0},{7,1},{4,2},{5,3},{2,4},{3,5},{0,6},{1,7},{14,8},{15,9},{12,... | collective-permute-start | bytes 116744 | tf_op jit(solution)/shard_map/ppermute | solution.py:338
  34.1 5.6 %collective-permute-start.7 = (f32[19,512]{1,0:T(8,128)S(1)}, f32[19,512]{1,0:T(8,128)S(1)}, u32[]{:S(2)}, u32[]{:S(2)}) collective-permute-start(f32[19,512]{1,0:T(8,128)S(1)} %rows_kernel.1.refs_7_.refs_6_.refs_2_), channel_id=1, source_target_pairs={{4,0},{5,1},{6,2},{7,3},{0,4},{1,5},{2,6},{3,7},{12,8},{13,9},{14,... | collective-permute-start | bytes 116744 | tf_op jit(solution)/shard_map/ppermute | solution.py:338
  34.9 4.8 %collective-permute-start.6 = (f32[19,512]{1,0:T(8,128)S(1)}, f32[19,512]{1,0:T(8,128)S(1)}, u32[]{:S(2)}, u32[]{:S(2)}) collective-permute-start(f32[19,512]{1,0:T(8,128)S(1)} %rows_kernel.1.refs_7_.refs_6_.refs_2_), channel_id=1, source_target_pairs={{2,0},{3,1},{0,2},{1,3},{6,4},{7,5},{4,6},{5,7},{10,8},{11,9},{8,1... | collective-permute-start | bytes 116744 | tf_op jit(solution)/shard_map/ppermute | solution.py:338
  36.4 9.9 %collective-permute-start.13 = (bf16[528,512]{1,0:T(8,128)(2,1)S(1)}, bf16[528,512]{1,0:T(8,128)(2,1)S(1)}, u32[]{:S(2)}, u32[]{:S(2)}) collective-permute-start(bf16[528,512]{1,0:T(8,128)(2,1)S(1)} %west_kernel.1.refs_7_), channel_id=1, source_target_pairs={{0,7},{1,0},{2,1},{3,2},{4,3},{5,4},{6,5},{7,6},{8,15},{9,8},{10,9... | collective-permute-start | bytes 1622024 | tf_op jit(solution)/shard_map/ppermute | solution.py:334
  40.0 5.2 %collective-permute-start.9 = (f32[16,512]{1,0:T(8,128)S(1)}, f32[16,512]{1,0:T(8,128)S(1)}, u32[]{:S(2)}, u32[]{:S(2)}) collective-permute-start(f32[16,512]{1,0:T(8,128)S(1)} %get-tuple-element.42), channel_id=1, source_target_pairs={{96,0},{104,8},{112,16},{120,24},{64,32},{72,40},{80,48},{88,56},{... | collective-permute-start | bytes 98312 | tf_op jit(solution)/shard_map/ppermute | solution.py:338
  40.8 5.4 %collective-permute-start.10 = (f32[16,512]{1,0:T(8,128)S(1)}, f32[16,512]{1,0:T(8,128)S(1)}, u32[]{:S(2)}, u32[]{:S(2)}) collective-permute-start(f32[16,512]{1,0:T(8,128)S(1)} %get-tuple-element.43), channel_id=1, source_target_pairs={{64,0},{72,8},{80,16},{88,24},{96,32},{104,40},{112,48},{120,56},{... | collective-permute-start | bytes 98312 | tf_op jit(solution)/shard_map/ppermute | solution.py:338
  41.9 4.4 %collective-permute-start.11 = (f32[16,512]{1,0:T(8,128)S(1)}, f32[16,512]{1,0:T(8,128)S(1)}, u32[]{:S(2)}, u32[]{:S(2)}) collective-permute-start(f32[16,512]{1,0:T(8,128)S(1)} %get-tuple-element.44), channel_id=1, source_target_pairs={{32,0},{40,8},{48,16},{56,24},{0,32},{8,40},{16,48},{24,56},{96,64... | collective-permute-start | bytes 98312 | tf_op jit(solution)/shard_map/ppermute | solution.py:338
